TPU v7x, 128 devices: a whole 4x4x4 slice. The times are simulated.
128 devices in a mesh: cell: 32 (over x, y, core), gene: 4 (over z).
Axes of the slice: x: 4, y: 4, z: 4, core: 2. Of those that a mesh axis runs over, the one named last changes fastest.
Arguments:
- counts: float32 [65536, 8192], P('cell', 'gene'), may hold values from 0 to 9, as said below
- donors: int32 [65536], P('cell'), may hold values from 0 to 127
- offset_table: int32 [128], replicated, may hold values from -8 to 8
- factors: float32 [64, 65536], P(None, 'cell'), may hold values from -2.4 to 2.4
- factor_mean: float32 [64, 65536], P(None, 'cell'), may hold values from -1.2 to 1.2
- factor_var: float32 [64, 65536], P(None, 'cell'), may hold values from 0.006 to 4, as said below
- loadings: float32 [64, 8192], P(None, 'gene'), may hold values from -1.5 to 1.5
- loading_mean: float32 [64, 8192], P(None, 'gene'), may hold values from -1.2 to 1.2
- loading_var: float32 [64, 8192], P(None, 'gene'), may hold values from 0.006 to 4, as said below
Outputs:
- new_factors: float32 [64, 65536], P(None, 'cell')
- new_factor_mean: float32 [64, 65536], P(None, 'cell')
- new_factor_var: float32 [64, 65536], P(None, 'cell')
- new_loadings: float32 [64, 8192], P(None, 'gene')
- new_loading_mean: float32 [64, 8192], P(None, 'gene')
- new_loading_var: float32 [64, 8192], P(None, 'gene')
Inputs may be any that keep to these rules, and one draw needn't show every extreme that they name: `counts`: whole numbers, products of two whole numbers from 0 to 3. `factor_var`: positive. `loading_var`: positive.
All inputs are finite; a program needn't handle non-finite values.
Results may differ from a plain program's by a relative error of at most 0.0003.
Values sent between devices are 32-bit elements; how exact they have to be, the bound alone decides.
No kernel may reach another device: no remote copies, remote signals or barrier semaphores. Data moves between devices by JAX's collectives and lax.ppermute only.
A program may use at most 128 MiB of HBM per device.

v0:
```python
import jax
import jax.numpy as jnp
from jax import lax
from jax.sharding import PartitionSpec as P

ROUNDS = 2


decay_first = 0.9
decay_second = 0.999
epsilon = 1e-06
rate_factors = 0.2
rate_loadings = 0.2
offset_unit = 0.125


def inverse_root(variance):
    return 1.0 / (jnp.sqrt(variance) + epsilon)


def moment_step(values, mean_old, var_old, gradient, scale, total, entries, rate):
    mean_new = decay_first * mean_old + (1.0 - decay_first) * gradient
    factor = rate / jnp.sqrt(total / entries)
    values_new = values - factor * mean_new * scale
    var_new = decay_second * var_old + (1.0 - decay_second) * gradient * gradient
    return (values_new, mean_new, var_new)


def on_device(
    counts,
    donors,
    offset_table,
    factors,
    factor_mean,
    factor_var,
    loadings,
    loading_mean,
    loading_var,
):
    highest = lax.Precision.HIGHEST
    cell_local = factors.shape[1]
    gene_local = loadings.shape[1]
    factor_width = factors.shape[0]
    cells_total = cell_local * lax.axis_size("cell")
    genes_total = gene_local * lax.axis_size("gene")
    donor_count = offset_table.shape[0]
    onehot = (donors[:, None] == jnp.arange(donor_count, dtype=jnp.int32)[None, :]).astype(
        jnp.float32
    )
    offsets = offset_unit * jnp.dot(onehot, offset_table.astype(jnp.float32), precision=highest)

    def residual_of(current, load):
        linear = (
            lax.dot_general(current, load, (((0,), (0,)), ((), ())), precision=highest)
            + offsets[:, None]
        )
        return jnp.exp(linear) - counts

    for repeat in range(ROUNDS):
        residual_tile = residual_of(factors, loadings)
        partial_grad = lax.dot_general(
            loadings, residual_tile, (((1,), (1,)), ((), ())), precision=highest
        ) / jnp.sqrt(float(genes_total))
        load_scale = inverse_root(loading_var)
        grad_factors, load_total = lax.psum(
            (partial_grad, jnp.sum(load_scale * load_scale)), "gene"
        )
        fac_scale = inverse_root(factor_var)
        fac_total = lax.psum(jnp.sum(fac_scale * fac_scale), "cell")
        factors, factor_mean, factor_var = moment_step(
            factors,
            factor_mean,
            factor_var,
            grad_factors,
            fac_scale,
            fac_total,
            float(cells_total * factor_width),
            rate_factors,
        )
        residual_tile = residual_of(factors, loadings)
        partial_load = lax.dot_general(
            factors, residual_tile, (((1,), (0,)), ((), ())), precision=highest
        ) / jnp.sqrt(float(cells_total))
        grad_loadings = lax.psum(partial_load, "cell")
        loadings, loading_mean, loading_var = moment_step(
            loadings,
            loading_mean,
            loading_var,
            grad_loadings,
            load_scale,
            load_total,
            float(genes_total * factor_width),
            rate_loadings,
        )
    return (factors, factor_mean, factor_var, loadings, loading_mean, loading_var)


def solution(mesh):
    return jax.shard_map(
        on_device,
        mesh=mesh,
        in_specs=(
            P("cell", "gene"),
            P("cell"),
            P(),
            P(None, "cell"),
            P(None, "cell"),
            P(None, "cell"),
            P(None, "gene"),
            P(None, "gene"),
            P(None, "gene"),
        ),
        out_specs=(
            P(None, "cell"),
            P(None, "cell"),
            P(None, "cell"),
            P(None, "gene"),
            P(None, "gene"),
            P(None, "gene"),
        ),
        check_vma=False,
    )
```

profile of v0, /device:TPU:1, one launch (start us, length us, event | category | flops | bytes accessed | tf_op | source)
XLA Modules:
  0.0 548.4 jit_solution(7903893763101162196)
XLA Ops:
  7.2 1.5 fusion.35
  8.7 17.0 %fusion.43 = f32[2048,2048]{1,0:T(8,128)} fusion(f32[64,2048]{1,0:T(8,128)} %param.12, f32[64,2048]{1,0:T(8,128)} %param.15), kind=kOutput, calls=%fused_computation.55 | convolution fusion | flops 3221225472 | bytes 17825792 | tf_op jit(solution)/shard_map/dot_general | solution.py:54
  25.7 25.2 %fusion.23 = f32[64,2048]{1,0:T(8,128)} fusion(f32[64,2048]{1,0:T(8,128)S(1)} %copy-done, f32[2048,2048]{1,0:T(8,128)} %param.9, f32[2048,2048]{1,0:T(8,128)} %fusion.43, f32[2048]{0:T(1024)S(1)} %broadcast_multiply_fusion), kind=kOutput, calls=%fused_computation.21 | convolution fusion | flops 3229745152 | bytes 34611200 | tf_op jit(solution)/shard_map/dot_general | solution.py:61
  51.0 0.0 all-reduce.9.cloned.1.call-start
  51.1 44.4 %all-reduce.7.cloned.1.call-done = f32[64,2048]{1,0:T(8,128)} async-done(((f32[64,2048]{1,0:T(8,128)}), f32[64,2048]{1,0:T(8,128)}) %all-reduce.7.cloned.1.call-update) | async-done | bytes 524304 | tf_op jit(solution)/shard_map/psum | solution.py:65
  95.5 2.1 multiply_reduce_fusion.2
  97.6 65.9 %all-reduce = (f32[]{:T(128)}, f32[]{:T(128)}) all-reduce(f32[]{:T(128)} %get-tuple-element.9, f32[]{:T(128)} %get-tuple-element.8), channel_id=1, replica_groups=mesh['cell'=32,'gene'=4] {'cell'}, use_global_device_ids=true, to_apply=%region_1.0 | all-reduce | flops 2 | bytes 16 | tf_op jit(solution)/shard_map/psum | solution.py:69
  164.2 1.3 multiply_subtract_fusion.3
  165.5 15.9 %fusion.44 = f32[2048,2048]{1,0:T(8,128)} fusion(f32[64,2048]{1,0:T(8,128)S(1)} %multiply_subtract_fusion.3, f32[64,2048]{1,0:T(8,128)S(1)} %copy-done), kind=kOutput, calls=%fused_computation.56 | convolution fusion | flops 3221225472 | bytes 17825792 | tf_op jit(solution)/shard_map/dot_general | solution.py:54
  181.4 19.2 %fusion.26 = f32[64,2048]{1,0:T(8,128)} fusion(f32[64,2048]{1,0:T(8,128)S(1)} %multiply_subtract_fusion.3, f32[2048,2048]{1,0:T(8,128)} %param.9, f32[2048,2048]{1,0:T(8,128)} %fusion.44, f32[2048]{0:T(1024)S(1)} %broadcast_multiply_fusion), kind=kOutput, calls=%fused_computation.22 | convolution fusion | flops 3229745152 | bytes 34611200 | tf_op jit(solution)/shard_map/dot_general | solution.py:81
  200.7 0.0 all-reduce.11.cloned.1.call-start
  200.7 101.1 %all-reduce.9.cloned.1.call-done = f32[64,2048]{1,0:T(8,128)} async-done(((f32[64,2048]{1,0:T(8,128)}), f32[64,2048]{1,0:T(8,128)}) %all-reduce.9.cloned.1.call-update) | async-done | bytes 524304 | tf_op jit(solution)/shard_map/psum | solution.py:84
  301.8 2.1 multiply_reduce_fusion
  303.9 9.4 %all-reduce.1 = (f32[]{:T(128)}, f32[]{:T(128)}) all-reduce(f32[]{:T(128)} %get-tuple-element.7, f32[]{:T(128)} %get-tuple-element.6), channel_id=1, replica_groups=mesh['cell'=32,'gene'=4] {'gene'}, use_global_device_ids=true, to_apply=%region_6.0 | all-reduce | flops 2 | bytes 16 | tf_op jit(solution)/shard_map/psum | solution.py:65
  314.1 1.3 multiply_subtract_fusion.2
  315.4 15.9 %fusion.45 = f32[2048,2048]{1,0:T(8,128)} fusion(f32[64,2048]{1,0:T(8,128)S(1)} %multiply_subtract_fusion.3, f32[64,2048]{1,0:T(8,128)S(1)} %multiply_subtract_fusion.2), kind=kOutput, calls=%fused_computation.57 | convolution fusion | flops 3221225472 | bytes 17825792 | tf_op jit(solution)/shard_map/dot_general | solution.py:54
  331.3 23.7 %fusion.29 = f32[64,2048]{1,0:T(8,128)} fusion(f32[64,2048]{1,0:T(8,128)S(1)} %multiply_subtract_fusion.2, f32[2048,2048]{1,0:T(8,128)} %param.9, f32[2048,2048]{1,0:T(8,128)} %fusion.45, f32[2048]{0:T(1024)S(1)} %broadcast_multiply_fusion), kind=kOutput, calls=%fused_computation.23 | convolution fusion | flops 3229745152 | bytes 34611200 | tf_op jit(solution)/shard_map/dot_general | solution.py:61
  355.0 0.3 all-reduce.13.cloned.1.call-start
  356.0 39.4 %all-reduce.11.cloned.1.call-done = f32[64,2048]{1,0:T(8,128)} async-done(((f32[64,2048]{1,0:T(8,128)}), f32[64,2048]{1,0:T(8,128)}) %all-reduce.11.cloned.1.call-update) | async-done | bytes 524304 | tf_op jit(solution)/shard_map/psum | solution.py:65
  395.4 2.6 multiply_subtract_fusion.1
  398.0 15.9 %fusion.46 = f32[2048,2048]{1,0:T(8,128)} fusion(f32[64,2048]{1,0:T(8,128)S(1)} %get-tuple-element.16, f32[64,2048]{1,0:T(8,128)S(1)} %multiply_subtract_fusion.2), kind=kOutput, calls=%fused_computation.58 | convolution fusion | flops 3221225472 | bytes 17825792 | tf_op jit(solution)/shard_map/dot_general | solution.py:54
  413.9 19.2 %fusion.32 = f32[64,2048]{1,0:T(8,128)} fusion(f32[64,2048]{1,0:T(8,128)S(1)} %get-tuple-element.16, f32[2048,2048]{1,0:T(8,128)} %param.9, f32[2048,2048]{1,0:T(8,128)} %fusion.46, f32[2048]{0:T(1024)S(1)} %broadcast_multiply_fusion), kind=kOutput, calls=%fused_computation.24 | convolution fusion | flops 3229745152 | bytes 34611200 | tf_op jit(solution)/shard_map/dot_general | solution.py:81
  433.8 105.3 %all-reduce.13.cloned.1.call-done = f32[64,2048]{1,0:T(8,128)} async-done(((f32[64,2048]{1,0:T(8,128)}), f32[64,2048]{1,0:T(8,128)}) %all-reduce.13.cloned.1.call-update) | async-done | bytes 524304 | tf_op jit(solution)/shard_map/psum | solution.py:84
  539.1 2.6 multiply_subtract_fusion
  (26 shorter events, 0.2 us)
Async XLA Ops:
  7.2 18.5 %copy-start = (f32[64,2048]{1,0:T(8,128)S(1)}, f32[64,2048]{1,0:T(8,128)}, u32[]{:S(2)}) copy-start(f32[64,2048]{1,0:T(8,128)} %param.15) | copy-start | bytes 1572868
  7.2 88.3 %all-reduce.7.cloned.1.call-start = ((), (), s32[]{:S(2)}) async-start(), calls=%async_computation | async-start | bytes 1048576 | tf_op jit(solution)/shard_map/psum | solution.py:65
  25.7 69.8 %copy-start.2 = (f32[64,2048]{1,0:T(8,128)S(1)}, f32[64,2048]{1,0:T(8,128)}, u32[]{:S(2)}) copy-start(f32[64,2048]{1,0:T(8,128)} %param.14) | copy-start | bytes 1572868
  25.7 138.5 %copy-start.6 = (f32[64,2048]{1,0:T(8,128)S(1)}, f32[64,2048]{1,0:T(8,128)}, u32[]{:S(2)}) copy-start(f32[64,2048]{1,0:T(8,128)} %param.12) | copy-start | bytes 1572868
  25.7 138.5 %copy-start.7 = (f32[64,2048]{1,0:T(8,128)S(1)}, f32[64,2048]{1,0:T(8,128)}, u32[]{:S(2)}) copy-start(f32[64,2048]{1,0:T(8,128)} %param.13) | copy-start | bytes 1572868
  51.0 250.8 %all-reduce.9.cloned.1.call-start = ((), (), s32[]{:S(2)}) async-start(), calls=%async_computation.1 | async-start | bytes 1048576 | tf_op jit(solution)/shard_map/psum | solution.py:84
  181.4 120.4 %copy-start.3 = (f32[64,2048]{1,0:T(8,128)S(1)}, f32[64,2048]{1,0:T(8,128)}, u32[]{:S(2)}) copy-start(f32[64,2048]{1,0:T(8,128)} %param.17) | copy-start | bytes 1572868
  181.4 132.7 %copy-start.8 = (f32[64,2048]{1,0:T(8,128)S(1)}, f32[64,2048]{1,0:T(8,128)}, u32[]{:S(2)}) copy-start(f32[64,2048]{1,0:T(8,128)} %param.16) | copy-start | bytes 1572868
  200.7 194.8 %all-reduce.11.cloned.1.call-start = ((), (), s32[]{:S(2)}) async-start(), calls=%async_computation.2 | async-start | bytes 1048576 | tf_op jit(solution)/shard_map/psum | solution.py:65
  331.3 64.1 %copy-start.4 = (f32[64,2048]{1,0:T(8,128)S(1)}, f32[64,2048]{1,0:T(8,128)}, u32[]{:S(2)}) copy-start(f32[64,2048]{1,0:T(8,128)} %all-reduce.7.cloned.1.call-done) | copy-start | bytes 1572868
  355.0 184.0 %all-reduce.13.cloned.1.call-start = ((), (), s32[]{:S(2)}) async-start(), calls=%async_computation.3 | async-start | bytes 1048576 | tf_op jit(solution)/shard_map/psum | solution.py:84
  398.0 35.1 %copy-start.1 = (f32[64,2048]{1,0:T(8,128)}, f32[64,2048]{1,0:T(8,128)S(1)}, u32[]{:S(2)}) copy-start(f32[64,2048]{1,0:T(8,128)S(1)} %get-tuple-element.16) | copy-start | bytes 1572868
  413.9 125.2 %copy-start.5 = (f32[64,2048]{1,0:T(8,128)S(1)}, f32[64,2048]{1,0:T(8,128)}, u32[]{:S(2)}) copy-start(f32[64,2048]{1,0:T(8,128)} %all-reduce.9.cloned.1.call-done) | copy-start | bytes 1572868
  413.9 125.2 %copy-start.9 = (f32[64,2048]{1,0:T(8,128)S(1)}, f32[64,2048]{1,0:T(8,128)}, u32[]{:S(2)}) copy-start(f32[64,2048]{1,0:T(8,128)} %param.16) | copy-start | bytes 1572868
Sparse Core Ops, SparseCore 0:
  51.1 44.2 all-reduce.6
  200.8 101.0 all-reduce.8
  355.1 40.2 all-reduce.10
  433.3 105.7 all-reduce.12
where the time goes:
time: 557 us; the launch traced here: 548 us
  waiting for transfers between devices  290 us (52%)
  matrix products  154 us (28%)
  blocking collectives  75.4 us (14%)
  between operations  16.7 us (3%)
  other arithmetic  12 us (2%)
    psum x2, waiting for transfers between devices, on_device(): grad_loadings = lax.psum(partial_load, 'cell')  206 us
    psum x2, waiting for transfers between devices, on_device(): lax.psum((partial_grad, jnp.sum(load_scale * load_scale)), 'gene')  83.9 us
    psum x1, blocking collectives, on_device(): fac_total = lax.psum(jnp.sum(fac_scale * fac_scale), 'cell')  65.9 us
    dot_general x4, matrix products, residual_of(): lax.dot_general(current, load, (((0,), (0,)), ((), ())), precision=highest)  64.7 us
    dot_general x2, matrix products, on_device(): lax.dot_general(loadings, residual_tile, (((1,), (1,)), ((), ())), precis...  49 us
    dot_general x2, matrix products, on_device(): lax.dot_general(factors, residual_tile, (((1,), (0,)), ((), ())), precisi...  38.5 us
  transfers between devices with their start and end apart: 4, of which 4 were waited for; matrix products, arithmetic and copies ran while one was open for 0% of the time, Pallas kernels for 0%

commit v1 on v0

v1 whole, which is shorter than its diff:
```python
import functools
import math

import jax
import jax.numpy as jnp
from jax import lax
from jax.experimental import pallas as pl
from jax.experimental.pallas import tpu as pltpu
from jax.sharding import PartitionSpec as P

decay_first = 0.9
decay_second = 0.999
epsilon = 1e-06
rate_factors = 0.2
rate_loadings = 0.2
offset_unit = 0.125
LOG2E = math.log2(math.e)
LANES = 128
SUB = 8
DEPTH = 256
f32 = jnp.float32
bf16 = jnp.bfloat16
VMEM_LIMIT = 20 << 20
CELL_BLOCK = 512
GENE_BLOCK = 256
CHUNK = 256


def split(x):
    high = x.astype(bf16)
    return high, (x - high.astype(f32)).astype(bf16)


def inverse_root(variance):
    return 1.0 / (jnp.sqrt(variance) + epsilon)


def square_tile(scale):
    square = scale * scale
    total = None
    for r in range(0, scale.shape[0], SUB):
        for c in range(0, scale.shape[1], LANES):
            part = square[r : r + SUB, c : c + LANES]
            total = part if total is None else total + part
    return total


def cell_operand(f, off):
    high, low = split(f)
    first = off.astype(bf16).astype(f32)
    rest = off - first
    second = rest.astype(bf16).astype(f32)
    third = rest - second
    row = lax.broadcasted_iota(jnp.int32, f.shape, 0)
    extra = jnp.where(row == 0, first, jnp.where(row == 1, second, jnp.where(row == 2, third, 0.0)))
    return high, low, jnp.concatenate([high, high, low, extra.astype(bf16)], 0)


def gene_operand(l):
    high, low = split(l * LOG2E)
    row = lax.broadcasted_iota(jnp.int32, l.shape, 0)
    ones = jnp.where(row < 3, 1.0, 0.0).astype(bf16)
    return jnp.concatenate([high, low, high, ones], 0)


def offsets_of(donors, table):
    which = lax.broadcasted_iota(jnp.int32, (table.shape[0], donors.shape[1]), 0)
    picked = jnp.where(which == donors, table.astype(f32), 0.0)
    return jnp.sum(picked, axis=0, keepdims=True) * (offset_unit * LOG2E)


def set_loads(l, load_cat, load_hl):
    load_cat[...] = gene_operand(l)
    high, low = split(l)
    load_hl[...] = jnp.concatenate([high, low], 0).T


def cell_pass(f_ref, off_ref, load_cat, load_hl, counts, g_ref, genes_total, ready=None):
    width, cells = f_ref.shape

    def block(b, _):
        if ready is not None:
            ready(b)
        at = pl.ds(pl.multiple_of(b * CELL_BLOCK, CELL_BLOCK), CELL_BLOCK)
        _, _, cat = cell_operand(f_ref[:, at], off_ref[:, at])
        lhs = cat.T
        total = None
        for g in range(0, load_cat.shape[1], CHUNK):
            of = slice(g, g + CHUNK)
            lin = jnp.dot(lhs, load_cat[:, of], preferred_element_type=f32)
            high, low = split(jnp.exp2(lin) - counts[at, of])
            part = jnp.dot(high, load_hl[of, :], preferred_element_type=f32)
            part += jnp.dot(low, load_hl[of, :], preferred_element_type=f32)
            total = part if total is None else total + part
        total = total.T
        grad = (total[:width] + total[width:]) * (1.0 / math.sqrt(genes_total))
        rows = CELL_BLOCK // LANES * width
        grad = jnp.concatenate([grad[:, c : c + LANES] for c in range(0, CELL_BLOCK, LANES)], 0)
        g_ref[pl.ds(pl.multiple_of(b * rows, rows), rows), :] = grad
        return 0

    lax.fori_loop(0, cells // CELL_BLOCK, block, 0)


def gene_pass(l_ref, cell_cat, cell_hl, counts, g_ref, cells_total):
    width, genes = l_ref.shape
    cells = cell_cat.shape[0]
    half = genes // GENE_BLOCK // 2
    rows = GENE_BLOCK // LANES * width

    def block(b, _):
        at = pl.ds(pl.multiple_of(b * GENE_BLOCK, GENE_BLOCK), GENE_BLOCK)
        load = gene_operand(l_ref[:, at])
        total = None
        for c in range(0, cells, CHUNK):
            of = slice(c, c + CHUNK)
            lin = jnp.dot(cell_cat[of, :], load, preferred_element_type=f32)
            resid = (jnp.exp2(lin) - counts[of, at]).astype(bf16)
            part = jnp.dot(cell_hl[:, of], resid, preferred_element_type=f32)
            total = part if total is None else total + part
        grad = (total[:width] + total[width:]) * (1.0 / math.sqrt(cells_total))
        grad = jnp.concatenate([grad[:, c : c + LANES] for c in range(0, GENE_BLOCK, LANES)], 0)
        g_ref[b // half, pl.ds(pl.multiple_of(b % half * rows, rows), rows), :] = grad
        return 0

    lax.fori_loop(0, 2 * half, block, 0)


def move(refs, grad_row, total, entries, rate, outs):
    values_ref, mean_ref, var_ref = refs
    width, length = values_ref.shape
    factor = rate / jnp.sqrt(total / entries)
    tile = None
    for c in range(0, length, LANES):
        at = slice(c, c + LANES)
        gradient = grad_row(c // LANES)
        var_old = var_ref[:, at]
        mean = decay_first * mean_ref[:, at] + (1.0 - decay_first) * gradient
        var = decay_second * var_old + (1.0 - decay_second) * gradient * gradient
        outs[0][:, at] = values_ref[:, at] - factor * mean * inverse_root(var_old)
        outs[1][:, at] = mean
        outs[2][:, at] = var
        part = square_tile(inverse_root(var))
        tile = part if tile is None else tile + part
    return tile


def total_kernel(var_ref, tile_ref):
    tile_ref[...] = square_tile(inverse_root(var_ref[...]))


def first_kernel(
    donors_ref, table_ref, f_ref, l_ref, lv_ref, counts_hbm, g_ref, off_ref, counts_ref, load_cat, load_hl, sems, *, genes_total
):
    cells = f_ref.shape[1]
    copies = []
    for b in range(cells // CELL_BLOCK):
        at = pl.ds(b * CELL_BLOCK, CELL_BLOCK)
        copies.append(pltpu.make_async_copy(counts_hbm.at[at], counts_ref.at[at], sems.at[b]))
        copies[-1].start()
    off_ref[...] = offsets_of(donors_ref[...], table_ref[...])
    set_loads(l_ref[...], load_cat, load_hl)
    rows = f_ref.shape[0] * cells // LANES
    g_ref[rows : rows + SUB, :] = square_tile(inverse_root(lv_ref[...]))

    def ready(b):
        at = pl.ds(pl.multiple_of(b * CELL_BLOCK, CELL_BLOCK), CELL_BLOCK)
        pltpu.make_async_copy(counts_hbm.at[at], counts_ref.at[at], sems.at[b]).wait()

    cell_pass(f_ref, off_ref, load_cat, load_hl, counts_ref, g_ref, genes_total, ready)


def gene_kernel(
    tile_ref, f_ref, fm_ref, fv_ref, grad_ref, off_ref, l_ref, counts_ref,
    g_ref, nf_ref, nm_ref, nv_ref, cell_cat, cell_hl, *, cells_total
):
    width, cells = f_ref.shape
    tile = move(
        (f_ref, fm_ref, fv_ref), lambda c: grad_ref[c * width : (c + 1) * width, :], jnp.sum(tile_ref[...]),
        cells_total * width, rate_factors, (nf_ref, nm_ref, nv_ref),
    )
    rows = g_ref.shape[1]
    for h in range(2):
        g_ref[h, rows - SUB : rows, :] = tile
    high, low, cat = cell_operand(nf_ref[...], off_ref[...])
    cell_cat[...] = cat.T
    cell_hl[...] = jnp.concatenate([high, low], 0)
    gene_pass(l_ref, cell_cat, cell_hl, counts_ref, g_ref, cells_total)


def grad_of_halves(grad_ref, width):
    per = (grad_ref.shape[1] - SUB) // width
    return lambda c: grad_ref[c // per, c % per * width : (c % per + 1) * width, :]


def cell_kernel(
    tile_ref, l_ref, lm_ref, lv_ref, grad_ref, f_ref, off_ref, counts_ref,
    g_ref, nl_ref, nm_ref, nv_ref, load_cat, load_hl, *, genes_total
):
    width, genes = l_ref.shape
    tile = move(
        (l_ref, lm_ref, lv_ref), grad_of_halves(grad_ref, width), jnp.sum(tile_ref[...]),
        genes_total * width, rate_loadings, (nl_ref, nm_ref, nv_ref),
    )
    rows = g_ref.shape[0]
    g_ref[rows - SUB : rows, :] = tile
    set_loads(nl_ref[...], load_cat, load_hl)
    cell_pass(f_ref, off_ref, load_cat, load_hl, counts_ref, g_ref, genes_total)


def last_kernel(tile_ref, l_ref, lm_ref, lv_ref, grad_ref, nl_ref, nm_ref, nv_ref, *, genes_total):
    width, genes = l_ref.shape
    move(
        (l_ref, lm_ref, lv_ref), grad_of_halves(grad_ref, width), jnp.sum(tile_ref[...]),
        genes_total * width, rate_loadings, (nl_ref, nm_ref, nv_ref),
    )


def exchange(value, partner):
    pairs = []
    for cell in range(32):
        for z in range(4):
            x, y, core, depth = partner(cell // 8, cell // 2 % 4, cell % 2, z)
            pairs.append((cell * 4 + z, ((x * 4 + y) * 2 + core) * 4 + depth))
    return lax.ppermute(value, ("cell", "gene"), pairs)


def near(i):
    return i ^ 1


def far(i):
    return 3 - i


def other_core(value):
    return exchange(value, lambda x, y, core, z: (x, y, 1 - core, z))


def along_cells(step):
    turn = near if step % 2 == 0 else far

    def partner(x, y, core, z):
        if (step // 2 + core) % 2 == 0:
            return turn(x), y, core, z
        return x, turn(y), core, z

    return partner


def along_genes(step):
    def partner(x, y, core, z):
        return x, y, core, (near if (step + core) % 2 == 0 else far)(z)

    return partner


def sum_over_genes(value):
    for step in range(2):
        value = value + exchange(value, along_genes(step))
    return value


def sum_over_chips(value):
    for step in range(4):
        value = value + exchange(value, along_cells(step))
    return value


def sum_over_cells(halves):
    core = lax.axis_index("cell") % 2
    mine = lax.dynamic_index_in_dim(halves, core, 0, keepdims=False)
    theirs = lax.dynamic_index_in_dim(halves, 1 - core, 0, keepdims=False)
    mine = sum_over_chips(mine + other_core(theirs))
    theirs = other_core(mine)
    return jnp.stack([jnp.where(core == 0, mine, theirs), jnp.where(core == 0, theirs, mine)])


def on_device(counts, donors, offset_table, factors, factor_mean, factor_var, loadings, loading_mean, loading_var):
    width, cells = factors.shape
    genes = loadings.shape[1]
    cells_total = float(cells * lax.axis_size("cell"))
    genes_total = float(genes * lax.axis_size("gene"))
    vmem = pl.BlockSpec(memory_space=pltpu.VMEM)
    like = lambda *shape: jax.ShapeDtypeStruct(shape, f32)
    cell_rows = width * cells // LANES + SUB
    gene_rows = width * genes // LANES // 2 + SUB
    cell_scratch = [pltpu.VMEM((DEPTH, genes), bf16), pltpu.VMEM((genes, 2 * width), bf16)]
    gene_scratch = [pltpu.VMEM((cells, DEPTH), bf16), pltpu.VMEM((2 * width, cells), bf16)]
    flops = 2 * (2 * DEPTH) * cells * genes

    def call(kernel, name, ins, outs, scratch=(), in_specs=None, work=1):
        return pl.pallas_call(
            kernel,
            name=name,
            in_specs=in_specs or [vmem] * len(ins),
            out_specs=[vmem] * len(outs),
            out_shape=outs,
            scratch_shapes=list(scratch),
            compiler_params=pltpu.CompilerParams(vmem_limit_bytes=VMEM_LIMIT),
            cost_estimate=pl.CostEstimate(
                flops=flops * work, bytes_accessed=4 * width * cells, transcendentals=cells * genes * work
            ),
        )(*ins)

    (fac_tile,) = call(total_kernel, "factor_scale_total", [factor_var], [like(SUB, LANES)], work=0)
    fac_tile = fac_tile + other_core(fac_tile)
    fac_tile = sum_over_chips(fac_tile)
    grad, off, held = call(
        functools.partial(first_kernel, genes_total=genes_total),
        "cell_pass_first",
        [donors.reshape(1, cells), offset_table.reshape(-1, 1), factors, loadings, loading_var, counts],
        [like(cell_rows, LANES), like(1, cells), pltpu.VMEM((cells, genes), f32)],
        cell_scratch + [pltpu.SemaphoreType.DMA((cells // CELL_BLOCK,))],
        [vmem] * 5 + [pl.BlockSpec(memory_space=pl.ANY)],
    )
    grad = sum_over_genes(grad)
    load_tile = grad[-SUB:]

    def loading_gradient(fac_tile, f, fm, fv, grad, l):
        return call(
            functools.partial(gene_kernel, cells_total=cells_total),
            "gene_pass",
            [fac_tile, f, fm, fv, grad, off, l, held],
            [like(2, gene_rows, LANES)] + [like(width, cells)] * 3,
            gene_scratch,
        )

    grad_l, f, fm, fv = loading_gradient(fac_tile, factors, factor_mean, factor_var, grad, loadings)
    grad_l = sum_over_cells(grad_l)
    fac_tile = grad_l[0, -SUB:]
    grad, l, lm, lv = call(
        functools.partial(cell_kernel, genes_total=genes_total),
        "cell_pass",
        [load_tile, loadings, loading_mean, loading_var, grad_l, f, off, held],
        [like(cell_rows, LANES)] + [like(width, genes)] * 3,
        cell_scratch,
    )
    grad = sum_over_genes(grad)
    load_tile = grad[-SUB:]
    grad_l, f, fm, fv = loading_gradient(fac_tile, f, fm, fv, grad, l)
    grad_l = sum_over_cells(grad_l)
    l, lm, lv = call(
        functools.partial(last_kernel, genes_total=genes_total),
        "loading_move",
        [load_tile, l, lm, lv, grad_l],
        [like(width, genes)] * 3,
        work=0,
    )
    return f, fm, fv, l, lm, lv


def solution(mesh):
    by_cell, by_gene = P(None, "cell"), P(None, "gene")
    return jax.shard_map(
        on_device,
        mesh=mesh,
        in_specs=(P("cell", "gene"), P("cell"), P(), by_cell, by_cell, by_cell, by_gene, by_gene, by_gene),
        out_specs=(by_cell, by_cell, by_cell, by_gene, by_gene, by_gene),
        check_vma=False,
    )
```

time: 557 us -> 191 us (0.34); the launches traced: 548 us -> 190 us
  waiting for transfers between devices: 290 us -> 73.3 us
  matrix products: 154 us -> 0 us
  blocking collectives: 75.4 us -> 0 us
  Pallas kernels: 0 us -> 43.5 us
  starting transfers between devices: 0.38 us -> 42.7 us
  local copies, waits for them, and re-layouts: 0.04 us -> 25.7 us
  between operations: 16.7 us -> 0.9 us
  other arithmetic: 12 us -> 4.01 us
    psum x4 -> x0, waiting for transfers between devices: 290 us -> none  [the longest x2 206 us: on_device(): grad_loadings = lax.psum(partial_load, 'cell')]
    dot_general x9 -> x0, matrix products: 154 us -> none  [the longest x4 64.7 us: residual_of(): lax.dot_general(current, load, (((0,), (0,)), ((), ())), precision=highest)]
    psum x2 -> x0, blocking collectives: 75.4 us -> none  [the longest x1 65.9 us: on_device(): fac_total = lax.psum(jnp.sum(fac_scale * fac_scale), 'cell')]
    ppermute x0 -> x21, waiting for transfers between devices: none -> 73.3 us  [exchange(): return lax.ppermute(value, ('cell', 'gene'), pairs)]
    pallas_call x0 -> x6, Pallas kernels: none -> 43.5 us  [call(): pl.pallas_call(kernel, name=name, in_specs=in_specs or [vmem] * len(ins),...]
    ppermute x0 -> x21, starting transfers between devices: none -> 42.7 us  [exchange(): return lax.ppermute(value, ('cell', 'gene'), pairs)]
    unnamed x20 -> x40, local copies, waits for them, and re-layouts: 0.04 us -> 24.9 us
    sub x4 -> x0, other arithmetic: 7.77 us -> none  [moment_step(): values_new = values - factor * mean_new * scale]
  transfers between devices with their start and end apart: 4 -> 21, of which waited for: 4 -> 20; matrix products, arithmetic and copies ran while one was open for 0% -> 0% of each run, Pallas kernels for 0% -> 0%
where the time goes in v1:
time: 191 us; the launch traced here: 190 us
  waiting for transfers between devices  73.3 us (38%)
  Pallas kernels  43.5 us (23%)
  starting transfers between devices  42.7 us (22%)
  local copies, waits for them, and re-layouts  25.7 us (13%)
  other arithmetic  4.01 us (2%)
    ppermute x21, waiting for transfers between devices, exchange(): return lax.ppermute(value, ('cell', 'gene'), pairs)  73.3 us
    pallas_call x6, Pallas kernels, call(): pl.pallas_call(kernel, name=name, in_specs=in_specs or [vmem] * len(ins),...  43.5 us
    ppermute x21, starting transfers between devices, exchange(): return lax.ppermute(value, ('cell', 'gene'), pairs)  42.7 us
    unnamed x40, local copies, waits for them, and re-layouts  24.9 us
  transfers between devices with their start and end apart: 21, of which 20 were waited for; matrix products, arithmetic and copies ran while one was open for 0% of the time, Pallas kernels for 0%

profile of v1, /device:TPU:1, one launch (start us, length us, event | category | flops | bytes accessed | tf_op | source)
XLA Modules:
  0.0 190.1 jit_solution(10692648503908058696)
XLA Ops:
  5.2 13.7 %cell_pass_first.1 = (f32[1032,128]{1,0:T(8,128)S(1)}, f32[1,2048]{1,0:T(1,128)S(1)}, f32[2048,2048]{1,0:T(8,128)S(1)}) custom-call(s32[1,2048]{1,0:T(1,128)S(1)} %bitcast.20, s32[128,1]{1,0:T(8,128)S(1)} %copy.15.table_ref, f32[64,2048]{1,0:T(8,128)S(1)} %copy-done.6, f32[64,2048]{1,0:T(8,128)S(1)} %copy-done.4, f32[64,2048]{1,0:T(8,128)S(1)} %copy-done.8, ...), custom_call_target="tpu_custom_call" | custom-call | flops 4294967296 | bytes 524288 | tf_op jit(solution)/shard_map/cell_pass_first/pallas_call | solution.py:293
  18.9 5.8 %copy-done = f32[2048,2048]{1,0:T(8,128)} copy-done((f32[2048,2048]{1,0:T(8,128)}, f32[2048,2048]{1,0:T(8,128)S(1)}, u32[]{:S(2)}) %copy-start) | copy-done | bytes 16777240
  24.7 4.6 %collective-permute-start.5 = (f32[1032,128]{1,0:T(8,128)S(1)}, f32[1032,128]{1,0:T(8,128)S(1)}, u32[]{:S(2)}, u32[]{:S(2)}) collective-permute-start(f32[1032,128]{1,0:T(8,128)S(1)} %get-tuple-element.24), channel_id=1, source_target_pairs={{0,1},{1,0},{2,3},{3,2},{4,7},{5,6},{6,5},{7,4},{8,9},{9,8},{10,11... | collective-permute-start | bytes 1585160 | tf_op jit(solution)/shard_map/ppermute | solution.py:225
  29.3 6.6 %collective-permute-done.5 = f32[1032,128]{1,0:T(8,128)S(1)} collective-permute-done((f32[1032,128]{1,0:T(8,128)S(1)}, f32[1032,128]{1,0:T(8,128)S(1)}, u32[]{:S(2)}, u32[]{:S(2)}) %collective-permute-start.5) | collective-permute-done | bytes 528416 | tf_op jit(solution)/shard_map/ppermute | solution.py:225
  36.3 3.6 %collective-permute-start = (f32[8,128]{1,0:T(8,128)S(1)}, f32[8,128]{1,0:T(8,128)S(1)}, u32[]{:S(2)}, u32[]{:S(2)}) collective-permute-start(f32[8,128]{1,0:T(8,128)S(1)} %factor_scale_total.1), channel_id=1, source_target_pairs={{0,4},{1,5},{2,6},{3,7},{4,0},{5,1},{6,2},{7,3},{8,12},{9,13},{10,... | collective-permute-start | bytes 12296 | tf_op jit(solution)/shard_map/ppermute | solution.py:225
  54.8 5.8 %copy-done.1 = f32[2048,2048]{1,0:T(8,128)S(1)} copy-done((f32[2048,2048]{1,0:T(8,128)S(1)}, f32[2048,2048]{1,0:T(8,128)}, u32[]{:S(2)}) %copy-start.1) | copy-done | bytes 16777240
  61.6 7.8 %gene_pass.2 = (f32[2,520,128]{2,1,0:T(8,128)S(1)}, f32[64,2048]{1,0:T(8,128)S(1)}, f32[64,2048]{1,0:T(8,128)S(1)}, f32[64,2048]{1,0:T(8,128)S(1)}) custom-call(f32[8,128]{1,0:T(8,128)S(1)} %add.77.tile_ref, f32[64,2048]{1,0:T(8,128)S(1)} %copy-done.7, f32[64,2048]{1,0:T(8,128)S(1)} %copy-done.12, f32[64,2048]{1,0:T(8,128)S(1)} %copy-done.10, ...), custom_call_target="tpu_custom_call" | custom-call | flops 4294967296 | bytes 524288 | tf_op jit(solution)/shard_map/gene_pass/pallas_call | solution.py:293
  71.1 4.5 %collective-permute-start.7 = (f32[520,128]{1,0:T(8,128)S(1)}, f32[520,128]{1,0:T(8,128)}, u32[]{:S(2)}, u32[]{:S(2)}) collective-permute-start(f32[520,128]{1,0:T(8,128)S(1)} %dynamic-slice_bitcast_fusion.1), channel_id=1, source_target_pairs={{0,4},{1,5},{2,6},{3,7},{4,0},{5,1},{6,2},{7,3},{8,12},{9,13},{10,... | collective-permute-start | bytes 798728 | tf_op jit(solution)/shard_map/ppermute | solution.py:225
  78.1 5.5 %collective-permute-done.8 = f32[520,128]{1,0:T(8,128)S(1)} collective-permute-done((f32[520,128]{1,0:T(8,128)S(1)}, f32[520,128]{1,0:T(8,128)S(1)}, u32[]{:S(2)}, u32[]{:S(2)}) %collective-permute-start.8) | collective-permute-done | bytes 266272 | tf_op jit(solution)/shard_map/ppermute | solution.py:225
  86.4 4.1 %collective-permute-done.9 = f32[520,128]{1,0:T(8,128)S(1)} collective-permute-done((f32[520,128]{1,0:T(8,128)S(1)}, f32[520,128]{1,0:T(8,128)S(1)}, u32[]{:S(2)}, u32[]{:S(2)}) %collective-permute-start.9) | collective-permute-done | bytes 266272 | tf_op jit(solution)/shard_map/ppermute | solution.py:225
  90.7 5.5 %collective-permute-done.10 = f32[520,128]{1,0:T(8,128)S(1)} collective-permute-done((f32[520,128]{1,0:T(8,128)S(1)}, f32[520,128]{1,0:T(8,128)S(1)}, u32[]{:S(2)}, u32[]{:S(2)}) %collective-permute-start.10) | collective-permute-done | bytes 266272 | tf_op jit(solution)/shard_map/ppermute | solution.py:225
  98.8 4.0 %collective-permute-done.11 = f32[520,128]{1,0:T(8,128)S(1)} collective-permute-done((f32[520,128]{1,0:T(8,128)S(1)}, f32[520,128]{1,0:T(8,128)S(1)}, u32[]{:S(2)}, u32[]{:S(2)}) %collective-permute-start.11) | collective-permute-done | bytes 266272 | tf_op jit(solution)/shard_map/ppermute | solution.py:225
  102.9 4.1 %collective-permute-start.12 = (f32[520,128]{1,0:T(8,128)S(1)}, f32[520,128]{1,0:T(8,128)}, u32[]{:S(2)}, u32[]{:S(2)}) collective-permute-start(f32[520,128]{1,0:T(8,128)S(1)} %add.86), channel_id=1, source_target_pairs={{0,4},{1,5},{2,6},{3,7},{4,0},{5,1},{6,2},{7,3},{8,12},{9,13},{10,... | collective-permute-start | bytes 798728 | tf_op jit(solution)/shard_map/ppermute | solution.py:225
  109.3 5.8 %copy-done.2 = f32[2048,2048]{1,0:T(8,128)S(1)} copy-done((f32[2048,2048]{1,0:T(8,128)S(1)}, f32[2048,2048]{1,0:T(8,128)}, u32[]{:S(2)}) %copy-start.2) | copy-done | bytes 16777240
  116.1 12.3 %cell_pass.1 = (f32[1032,128]{1,0:T(8,128)S(1)}, f32[64,2048]{1,0:T(8,128)S(1)}, f32[64,2048]{1,0:T(8,128)S(1)}, f32[64,2048]{1,0:T(8,128)S(1)}) custom-call(f32[8,128]{1,0:T(8,128)S(1)} %slice.13.tile_ref, f32[64,2048]{1,0:T(8,128)S(1)} %copy-done.5, f32[64,2048]{1,0:T(8,128)S(1)} %copy-done.13, f32[64,2048]{1,0:T(8,128)S(1)} %copy-done.9, ...), custom_call_target="tpu_custom_call" | custom-call | flops 4294967296 | bytes 524288 | tf_op jit(solution)/shard_map/cell_pass/pallas_call | solution.py:293
  128.6 9.3 %collective-permute-done.13 = f32[1032,128]{1,0:T(8,128)S(1)} collective-permute-done((f32[1032,128]{1,0:T(8,128)S(1)}, f32[1032,128]{1,0:T(8,128)S(1)}, u32[]{:S(2)}, u32[]{:S(2)}) %collective-permute-start.13) | collective-permute-done | bytes 528416 | tf_op jit(solution)/shard_map/ppermute | solution.py:225
  138.2 8.3 %collective-permute-done.14 = f32[1032,128]{1,0:T(8,128)S(1)} collective-permute-done((f32[1032,128]{1,0:T(8,128)S(1)}, f32[1032,128]{1,0:T(8,128)S(1)}, u32[]{:S(2)}, u32[]{:S(2)}) %collective-permute-start.14) | collective-permute-done | bytes 528416 | tf_op jit(solution)/shard_map/ppermute | solution.py:225
  146.6 8.0 %gene_pass.3 = (f32[2,520,128]{2,1,0:T(8,128)S(1)}, f32[64,2048]{1,0:T(8,128)}, f32[64,2048]{1,0:T(8,128)}, f32[64,2048]{1,0:T(8,128)}) custom-call(f32[8,128]{1,0:T(8,128)S(1)} %slice_bitcast_fusion.tile_ref, f32[64,2048]{1,0:T(8,128)S(1)} %get-tuple-element.28.f_ref, f32[64,2048]{1,0:T(8,128)S(1)} %copy-done.15, f32[64,2048]{1,0:T(8,128)S(1)} %copy-done.17, ...), custom_call_target="tpu_custom_call" | custom-call | flops 4294967296 | bytes 524288 | tf_op jit(solution)/shard_map/gene_pass/pallas_call | solution.py:293
  158.5 5.5 %collective-permute-done.16 = f32[520,128]{1,0:T(8,128)S(1)} collective-permute-done((f32[520,128]{1,0:T(8,128)S(1)}, f32[520,128]{1,0:T(8,128)S(1)}, u32[]{:S(2)}, u32[]{:S(2)}) %collective-permute-start.16) | collective-permute-done | bytes 266272 | tf_op jit(solution)/shard_map/ppermute | solution.py:225
  164.0 2.8 %collective-permute-start.17 = (f32[520,128]{1,0:T(8,128)S(1)}, f32[520,128]{1,0:T(8,128)S(1)}, u32[]{:S(2)}, u32[]{:S(2)}) collective-permute-start(f32[520,128]{1,0:T(8,128)S(1)} %add.90), channel_id=1, source_target_pairs={{0,96},{1,97},{2,98},{3,99},{4,28},{5,29},{6,30},{7,31},{8,104},{9... | collective-permute-start | bytes 798728 | tf_op jit(solution)/shard_map/ppermute | solution.py:225
  166.8 4.1 %collective-permute-done.17 = f32[520,128]{1,0:T(8,128)S(1)} collective-permute-done((f32[520,128]{1,0:T(8,128)S(1)}, f32[520,128]{1,0:T(8,128)S(1)}, u32[]{:S(2)}, u32[]{:S(2)}) %collective-permute-start.17) | collective-permute-done | bytes 266272 | tf_op jit(solution)/shard_map/ppermute | solution.py:225
  171.1 5.5 %collective-permute-done.18 = f32[520,128]{1,0:T(8,128)S(1)} collective-permute-done((f32[520,128]{1,0:T(8,128)S(1)}, f32[520,128]{1,0:T(8,128)S(1)}, u32[]{:S(2)}, u32[]{:S(2)}) %collective-permute-start.18) | collective-permute-done | bytes 266272 | tf_op jit(solution)/shard_map/ppermute | solution.py:225
  179.2 4.0 %collective-permute-done.19 = f32[520,128]{1,0:T(8,128)S(1)} collective-permute-done((f32[520,128]{1,0:T(8,128)S(1)}, f32[520,128]{1,0:T(8,128)S(1)}, u32[]{:S(2)}, u32[]{:S(2)}) %collective-permute-start.19) | collective-permute-done | bytes 266272 | tf_op jit(solution)/shard_map/ppermute | solution.py:225
  183.3 4.1 %collective-permute-start.20 = (f32[520,128]{1,0:T(8,128)S(1)}, f32[520,128]{1,0:T(8,128)S(1)}, u32[]{:S(2)}, u32[]{:S(2)}) collective-permute-start(f32[520,128]{1,0:T(8,128)S(1)} %add.93), channel_id=1, source_target_pairs={{0,4},{1,5},{2,6},{3,7},{4,0},{5,1},{6,2},{7,3},{8,12},{9,13},{10,... | collective-permute-start | bytes 798728 | tf_op jit(solution)/shard_map/ppermute | solution.py:225
  (93 shorter events, 43.8 us)
Async XLA Ops:
  24.7 84.6 %copy-start.9 = (f32[64,2048]{1,0:T(8,128)S(1)}, f32[64,2048]{1,0:T(8,128)}, u32[]{:S(2)}) copy-start(f32[64,2048]{1,0:T(8,128)} %lv_ref.3) | copy-start | bytes 1572868
  24.7 11.2 %collective-permute-start.5 = (f32[1032,128]{1,0:T(8,128)S(1)}, f32[1032,128]{1,0:T(8,128)S(1)}, u32[]{:S(2)}, u32[]{:S(2)}) collective-permute-start(f32[1032,128]{1,0:T(8,128)S(1)} %get-tuple-element.24), channel_id=1, source_target_pairs={{0,1},{1,0},{2,3},{3,2},{4,7},{5,6},{6,5},{7,4},{8,9},{9,8},{10,11... | collective-permute-start | bytes 1585160 | tf_op jit(solution)/shard_map/ppermute | solution.py:225
  36.0 17.5 %collective-permute-start.6 = (f32[1032,128]{1,0:T(8,128)S(1)}, f32[1032,128]{1,0:T(8,128)}, u32[]{:S(2)}, u32[]{:S(2)}) collective-permute-start(f32[1032,128]{1,0:T(8,128)S(1)} %add.78), channel_id=1, source_target_pairs={{0,3},{1,2},{2,1},{3,0},{4,5},{5,4},{6,7},{7,6},{8,11},{9,10},{10,... | collective-permute-start | bytes 1585160 | tf_op jit(solution)/shard_map/ppermute | solution.py:225
  36.3 4.4 %collective-permute-start = (f32[8,128]{1,0:T(8,128)S(1)}, f32[8,128]{1,0:T(8,128)S(1)}, u32[]{:S(2)}, u32[]{:S(2)}) collective-permute-start(f32[8,128]{1,0:T(8,128)S(1)} %factor_scale_total.1), channel_id=1, source_target_pairs={{0,4},{1,5},{2,6},{3,7},{4,0},{5,1},{6,2},{7,3},{8,12},{9,13},{10,... | collective-permute-start | bytes 12296 | tf_op jit(solution)/shard_map/ppermute | solution.py:225
  40.7 2.9 %collective-permute-start.1 = (f32[8,128]{1,0:T(8,128)S(1)}, f32[8,128]{1,0:T(8,128)S(1)}, u32[]{:S(2)}, u32[]{:S(2)}) collective-permute-start(f32[8,128]{1,0:T(8,128)S(1)} %add.73), channel_id=1, source_target_pairs={{0,32},{1,33},{2,34},{3,35},{4,12},{5,13},{6,14},{7,15},{8,40},{9,... | collective-permute-start | bytes 12296 | tf_op jit(solution)/shard_map/ppermute | solution.py:225
  43.6 3.7 %collective-permute-start.2 = (f32[8,128]{1,0:T(8,128)S(1)}, f32[8,128]{1,0:T(8,128)S(1)}, u32[]{:S(2)}, u32[]{:S(2)}) collective-permute-start(f32[8,128]{1,0:T(8,128)S(1)} %add.74), channel_id=1, source_target_pairs={{0,96},{1,97},{2,98},{3,99},{4,28},{5,29},{6,30},{7,31},{8,104},{9... | collective-permute-start | bytes 12296 | tf_op jit(solution)/shard_map/ppermute | solution.py:225
  47.3 2.5 %collective-permute-start.3 = (f32[8,128]{1,0:T(8,128)S(1)}, f32[8,128]{1,0:T(8,128)S(1)}, u32[]{:S(2)}, u32[]{:S(2)}) collective-permute-start(f32[8,128]{1,0:T(8,128)S(1)} %add.75), channel_id=1, source_target_pairs={{0,8},{1,9},{2,10},{3,11},{4,36},{5,37},{6,38},{7,39},{8,0},{9,1},... | collective-permute-start | bytes 12296 | tf_op jit(solution)/shard_map/ppermute | solution.py:225
  49.8 3.7 %collective-permute-start.4 = (f32[8,128]{1,0:T(8,128)S(1)}, f32[8,128]{1,0:T(8,128)S(1)}, u32[]{:S(2)}, u32[]{:S(2)}) collective-permute-start(f32[8,128]{1,0:T(8,128)S(1)} %add.76), channel_id=1, source_target_pairs={{0,24},{1,25},{2,26},{3,27},{4,100},{5,101},{6,102},{7,103},{8,16}... | collective-permute-start | bytes 12296 | tf_op jit(solution)/shard_map/ppermute | solution.py:225
  70.9 75.7 %copy-start.17 = (f32[64,2048]{1,0:T(8,128)S(1)}, f32[64,2048]{1,0:T(8,128)}, u32[]{:S(2)}) copy-start(f32[64,2048]{1,0:T(8,128)} %copy-done.16) | copy-start | bytes 1572868
  71.1 5.8 %collective-permute-start.7 = (f32[520,128]{1,0:T(8,128)S(1)}, f32[520,128]{1,0:T(8,128)}, u32[]{:S(2)}, u32[]{:S(2)}) collective-permute-start(f32[520,128]{1,0:T(8,128)S(1)} %dynamic-slice_bitcast_fusion.1), channel_id=1, source_target_pairs={{0,4},{1,5},{2,6},{3,7},{4,0},{5,1},{6,2},{7,3},{8,12},{9,13},{10,... | collective-permute-start | bytes 798728 | tf_op jit(solution)/shard_map/ppermute | solution.py:225
  75.6 71.0 %copy-start.15 = (f32[64,2048]{1,0:T(8,128)S(1)}, f32[64,2048]{1,0:T(8,128)}, u32[]{:S(2)}) copy-start(f32[64,2048]{1,0:T(8,128)} %copy-done.14) | copy-start | bytes 1572868
  77.9 5.6 %collective-permute-start.8 = (f32[520,128]{1,0:T(8,128)S(1)}, f32[520,128]{1,0:T(8,128)S(1)}, u32[]{:S(2)}, u32[]{:S(2)}) collective-permute-start(f32[520,128]{1,0:T(8,128)S(1)} %bitcast_add_fusion.1), channel_id=1, source_target_pairs={{0,32},{1,33},{2,34},{3,35},{4,12},{5,13},{6,14},{7,15},{8,40},{9,... | collective-permute-start | bytes 798728 | tf_op jit(solution)/shard_map/ppermute | solution.py:225
  83.6 6.9 %collective-permute-start.9 = (f32[520,128]{1,0:T(8,128)S(1)}, f32[520,128]{1,0:T(8,128)S(1)}, u32[]{:S(2)}, u32[]{:S(2)}) collective-permute-start(f32[520,128]{1,0:T(8,128)S(1)} %add.83), channel_id=1, source_target_pairs={{0,96},{1,97},{2,98},{3,99},{4,28},{5,29},{6,30},{7,31},{8,104},{9... | collective-permute-start | bytes 798728 | tf_op jit(solution)/shard_map/ppermute | solution.py:225
  90.6 5.6 %collective-permute-start.10 = (f32[520,128]{1,0:T(8,128)S(1)}, f32[520,128]{1,0:T(8,128)S(1)}, u32[]{:S(2)}, u32[]{:S(2)}) collective-permute-start(f32[520,128]{1,0:T(8,128)S(1)} %add.84), channel_id=1, source_target_pairs={{0,8},{1,9},{2,10},{3,11},{4,36},{5,37},{6,38},{7,39},{8,0},{9,1},... | collective-permute-start | bytes 798728 | tf_op jit(solution)/shard_map/ppermute | solution.py:225
  96.3 6.6 %collective-permute-start.11 = (f32[520,128]{1,0:T(8,128)S(1)}, f32[520,128]{1,0:T(8,128)S(1)}, u32[]{:S(2)}, u32[]{:S(2)}) collective-permute-start(f32[520,128]{1,0:T(8,128)S(1)} %add.85), channel_id=1, source_target_pairs={{0,24},{1,25},{2,26},{3,27},{4,100},{5,101},{6,102},{7,103},{8,16}... | collective-permute-start | bytes 798728 | tf_op jit(solution)/shard_map/ppermute | solution.py:225
  102.9 5.4 %collective-permute-start.12 = (f32[520,128]{1,0:T(8,128)S(1)}, f32[520,128]{1,0:T(8,128)}, u32[]{:S(2)}, u32[]{:S(2)}) collective-permute-start(f32[520,128]{1,0:T(8,128)S(1)} %add.86), channel_id=1, source_target_pairs={{0,4},{1,5},{2,6},{3,7},{4,0},{5,1},{6,2},{7,3},{8,12},{9,13},{10,... | collective-permute-start | bytes 798728 | tf_op jit(solution)/shard_map/ppermute | solution.py:225
  128.5 9.4 %collective-permute-start.13 = (f32[1032,128]{1,0:T(8,128)S(1)}, f32[1032,128]{1,0:T(8,128)S(1)}, u32[]{:S(2)}, u32[]{:S(2)}) collective-permute-start(f32[1032,128]{1,0:T(8,128)S(1)} %get-tuple-element.31), channel_id=1, source_target_pairs={{0,1},{1,0},{2,3},{3,2},{4,7},{5,6},{6,5},{7,4},{8,9},{9,8},{10,11... | collective-permute-start | bytes 1585160 | tf_op jit(solution)/shard_map/ppermute | solution.py:225
  137.9 8.6 %collective-permute-start.14 = (f32[1032,128]{1,0:T(8,128)S(1)}, f32[1032,128]{1,0:T(8,128)S(1)}, u32[]{:S(2)}, u32[]{:S(2)}) collective-permute-start(f32[1032,128]{1,0:T(8,128)S(1)} %add.87), channel_id=1, source_target_pairs={{0,3},{1,2},{2,1},{3,0},{4,5},{5,4},{6,7},{7,6},{8,11},{9,10},{10,... | collective-permute-start | bytes 1585160 | tf_op jit(solution)/shard_map/ppermute | solution.py:225
  154.7 3.6 %collective-permute-start.15 = (f32[520,128]{1,0:T(8,128)S(1)}, f32[520,128]{1,0:T(8,128)S(1)}, u32[]{:S(2)}, u32[]{:S(2)}) collective-permute-start(f32[520,128]{1,0:T(8,128)S(1)} %dynamic-slice_bitcast_fusion), channel_id=1, source_target_pairs={{0,4},{1,5},{2,6},{3,7},{4,0},{5,1},{6,2},{7,3},{8,12},{9,13},{10,... | collective-permute-start | bytes 798728 | tf_op jit(solution)/shard_map/ppermute | solution.py:225
  158.4 5.6 %collective-permute-start.16 = (f32[520,128]{1,0:T(8,128)S(1)}, f32[520,128]{1,0:T(8,128)S(1)}, u32[]{:S(2)}, u32[]{:S(2)}) collective-permute-start(f32[520,128]{1,0:T(8,128)S(1)} %bitcast_add_fusion), channel_id=1, source_target_pairs={{0,32},{1,33},{2,34},{3,35},{4,12},{5,13},{6,14},{7,15},{8,40},{9,... | collective-permute-start | bytes 798728 | tf_op jit(solution)/shard_map/ppermute | solution.py:225
  164.0 6.9 %collective-permute-start.17 = (f32[520,128]{1,0:T(8,128)S(1)}, f32[520,128]{1,0:T(8,128)S(1)}, u32[]{:S(2)}, u32[]{:S(2)}) collective-permute-start(f32[520,128]{1,0:T(8,128)S(1)} %add.90), channel_id=1, source_target_pairs={{0,96},{1,97},{2,98},{3,99},{4,28},{5,29},{6,30},{7,31},{8,104},{9... | collective-permute-start | bytes 798728 | tf_op jit(solution)/shard_map/ppermute | solution.py:225
  171.0 5.6 %collective-permute-start.18 = (f32[520,128]{1,0:T(8,128)S(1)}, f32[520,128]{1,0:T(8,128)S(1)}, u32[]{:S(2)}, u32[]{:S(2)}) collective-permute-start(f32[520,128]{1,0:T(8,128)S(1)} %add.91), channel_id=1, source_target_pairs={{0,8},{1,9},{2,10},{3,11},{4,36},{5,37},{6,38},{7,39},{8,0},{9,1},... | collective-permute-start | bytes 798728 | tf_op jit(solution)/shard_map/ppermute | solution.py:225
  176.7 6.6 %collective-permute-start.19 = (f32[520,128]{1,0:T(8,128)S(1)}, f32[520,128]{1,0:T(8,128)S(1)}, u32[]{:S(2)}, u32[]{:S(2)}) collective-permute-start(f32[520,128]{1,0:T(8,128)S(1)} %add.92), channel_id=1, source_target_pairs={{0,24},{1,25},{2,26},{3,27},{4,100},{5,101},{6,102},{7,103},{8,16}... | collective-permute-start | bytes 798728 | tf_op jit(solution)/shard_map/ppermute | solution.py:225
  183.3 5.3 %collective-permute-start.20 = (f32[520,128]{1,0:T(8,128)S(1)}, f32[520,128]{1,0:T(8,128)S(1)}, u32[]{:S(2)}, u32[]{:S(2)}) collective-permute-start(f32[520,128]{1,0:T(8,128)S(1)} %add.93), channel_id=1, source_target_pairs={{0,4},{1,5},{2,6},{3,7},{4,0},{5,1},{6,2},{7,3},{8,12},{9,13},{10,... | collective-permute-start | bytes 798728 | tf_op jit(solution)/shard_map/ppermute | solution.py:225
  (17 other events, 203.7 us)

commit v2 on v1

v2 whole, which is shorter than its diff:
```python
import functools
import math

import jax
import jax.numpy as jnp
from jax import lax
from jax.experimental import pallas as pl
from jax.experimental.pallas import tpu as pltpu
from jax.sharding import PartitionSpec as P

decay_first = 0.9
decay_second = 0.999
epsilon = 1e-06
rate_factors = 0.2
rate_loadings = 0.2
offset_unit = 0.125
LOG2E = math.log2(math.e)
LANES = 128
SUB = 8
DEPTH = 256
f32 = jnp.float32
bf16 = jnp.bfloat16
LOW = False
CELL_BLOCK = 512
GENE_BLOCK = 256
COPY_CELLS = 256
PARTS = 2
CHUNK = 512


def split(x):
    high = x.astype(bf16)
    return high, (x - high.astype(f32)).astype(bf16)


def inverse_root(variance):
    return 1.0 / (jnp.sqrt(variance) + epsilon)


def square_tile(scale):
    square = scale * scale
    total = None
    for r in range(0, scale.shape[0], SUB):
        for c in range(0, scale.shape[1], LANES):
            part = square[r : r + SUB, c : c + LANES]
            total = part if total is None else total + part
    return total


def cell_operand(f, off):
    high, low = split(f)
    first = off.astype(bf16).astype(f32)
    rest = off - first
    second = rest.astype(bf16).astype(f32)
    third = rest - second
    row = lax.broadcasted_iota(jnp.int32, f.shape, 0)
    extra = jnp.where(row == 0, first, jnp.where(row == 1, second, jnp.where(row == 2, third, 0.0)))
    return high, low, jnp.concatenate([high, high, low, extra.astype(bf16)], 0)


def gene_operand(l):
    high, low = split(l * LOG2E)
    row = lax.broadcasted_iota(jnp.int32, l.shape, 0)
    ones = jnp.where(row < 3, 1.0, 0.0).astype(bf16)
    return jnp.concatenate([high, low, high, ones], 0)


def offsets_of(donors, table):
    column = jnp.broadcast_to(table.astype(f32), (LANES, table.shape[1])).T[:, :1]
    which = lax.broadcasted_iota(jnp.int32, (table.shape[1], donors.shape[1]), 0)
    picked = jnp.where(which == donors, column, 0.0)
    return jnp.sum(picked, axis=0, keepdims=True) * (offset_unit * LOG2E)


def set_loads(l, load_cat, load_hl):
    load_cat[...] = gene_operand(l)
    high, low = split(l)
    load_hl[...] = jnp.concatenate([high, low], 0)


def set_cells(f, off, cell_cat, cell_hl):
    high, low, cat = cell_operand(f, off)
    cell_cat[...] = cat.T
    cell_hl[...] = jnp.concatenate([high, low], 0)


def lane_rows(grad):
    return jnp.concatenate([grad[:, c : c + LANES] for c in range(0, grad.shape[1], LANES)], 0)


def wait_all(copies):
    for copy in copies:
        copy.wait()


def start_all(copies):
    for copy in copies:
        copy.start()
    return copies


def cell_pass(f_ref, off_ref, load_cat, load_hl, counts, stream, g_refs, genes_total):
    width, cells = f_ref.shape
    blocks = cells // CELL_BLOCK
    rows = width * CELL_BLOCK // LANES
    last = (((1,), (1,)), ((), ()))
    for b in range(blocks):
        at = slice(b * CELL_BLOCK, (b + 1) * CELL_BLOCK)
        _, _, cat = cell_operand(f_ref[:, at], off_ref[:, at])
        lhs = cat.T
        if stream is not None:
            stream(b)
        total, small = None, None
        for g in range(0, load_cat.shape[1], CHUNK):
            of = slice(g, g + CHUNK)
            lin = jnp.dot(lhs, load_cat[:, of], preferred_element_type=f32)
            high, low = split(jnp.exp2(lin) - counts[at, of].astype(f32))
            part = lax.dot_general(load_hl[:, of], high, last, preferred_element_type=f32)
            total = part if total is None else total + part
            if LOW:
                part = lax.dot_general(load_hl[:width, of], low, last, preferred_element_type=f32)
                small = part if small is None else small + part
        grad = total[:width] + total[width:]
        if LOW:
            grad += small
        half = blocks // 2
        g_refs[b // half][b % half * rows : (b % half + 1) * rows, :] = lane_rows(grad * (1.0 / math.sqrt(genes_total)))


def gene_pass(l_ref, cell_cat, cell_hl, counts, g_refs, cells_total):
    width, genes = l_ref.shape
    blocks = genes // GENE_BLOCK
    rows = width * GENE_BLOCK // LANES
    quarter = blocks // 4
    for b in range(blocks):
        at = slice(b * GENE_BLOCK, (b + 1) * GENE_BLOCK)
        load = gene_operand(l_ref[:, at])
        total = None
        for c in range(0, cell_cat.shape[0], CHUNK):
            of = slice(c, c + CHUNK)
            lin = jnp.dot(cell_cat[of, :], load, preferred_element_type=f32)
            resid = (jnp.exp2(lin) - counts[of, at].astype(f32)).astype(bf16)
            part = jnp.dot(cell_hl[:, of], resid, preferred_element_type=f32)
            total = part if total is None else total + part
        grad = (total[:width] + total[width:]) * (1.0 / math.sqrt(cells_total))
        q = b // quarter
        g_refs[q // 2][q % 2, b % quarter * rows : (b % quarter + 1) * rows, :] = lane_rows(grad)


def move(held, grad_row, total, entries, rate, moved):
    factor = rate / jnp.sqrt(total / entries)
    tile = None
    for c in range(0, moved.shape[2], LANES):
        at = slice(c, c + LANES)
        gradient = grad_row(c // LANES)
        var_old = held[2][:, at]
        mean = decay_first * held[1][:, at] + (1.0 - decay_first) * gradient
        var = decay_second * var_old + (1.0 - decay_second) * gradient * gradient
        moved[0, :, at] = held[0][:, at] - factor * mean * inverse_root(var_old)
        moved[1, :, at] = mean
        moved[2, :, at] = var
        part = square_tile(inverse_root(var))
        tile = part if tile is None else tile + part
    return tile


def total_kernel(var_hbm, tile_ref, var_ref, sem):
    copy = pltpu.make_async_copy(var_hbm, var_ref, sem)
    copy.start()
    copy.wait()
    tile_ref[...] = square_tile(inverse_root(var_ref[...]))


def load_kernel(after_ref, *refs):
    del after_ref
    *refs, sems = refs
    half = len(refs) // 2
    size = refs[0].shape[0] // (sems.shape[0] - half + 1)
    copies = []
    for r in range(0, refs[0].shape[0], size):
        at = pl.ds(r, size)
        copies.append(pltpu.make_async_copy(refs[0].at[at], refs[half].at[at], sems.at[len(copies)]))
    for i in range(1, half):
        copies.append(pltpu.make_async_copy(refs[i], refs[half + i], sems.at[len(copies)]))
    wait_all(start_all(copies))


class Stream:
    def __init__(self, copies, ahead=3):
        self.copies, self.ahead, self.done = copies, ahead, 0
        start_all(copies[:ahead])

    def need(self, count):
        while self.done < count:
            self.copies[self.done].wait()
            start_all(self.copies[self.done + self.ahead : self.done + self.ahead + 1])
            self.done += 1


def counts_by_cells(counts_hbm, held, sems):
    copies = []
    for b in range(held.shape[0] // COPY_CELLS):
        at = pl.ds(b * COPY_CELLS, COPY_CELLS)
        copies.append(pltpu.make_async_copy(counts_hbm.at[at], held.at[at], sems.at[b]))
    return Stream(copies)


def first_kernel(
    tile_ref, donors_hbm, table_hbm, f_hbm, l_hbm, lv_hbm, counts_hbm, ga_ref, gb_ref, off_ref, narrow_hbm,
    held, narrow, donors_ref, table_ref, f_ref, l_ref, lv_ref, load_cat, load_hl, sems, small, out_sems, *, genes_total
):
    del tile_ref
    pairs = [(l_hbm, l_ref), (f_hbm, f_ref), (donors_hbm, donors_ref), (table_hbm, table_ref), (lv_hbm, lv_ref)]
    copies = start_all([pltpu.make_async_copy(src, dst, small.at[i]) for i, (src, dst) in enumerate(pairs)])
    stream = counts_by_cells(counts_hbm, held, sems)
    wait_all(copies)
    off_ref[...] = offsets_of(donors_ref[...], table_ref[...])
    set_loads(l_ref[...], load_cat, load_hl)
    ga_ref[ga_ref.shape[0] - SUB :, :] = square_tile(inverse_root(lv_ref[...]))
    kept = []

    def ready(b):
        stream.need((b + 1) * CELL_BLOCK // COPY_CELLS)
        at = pl.ds(b * CELL_BLOCK, CELL_BLOCK)
        narrow[b] = held[at, :].astype(bf16)
        kept.append(pltpu.make_async_copy(narrow.at[b], narrow_hbm.at[at], out_sems.at[b]))
        kept[-1].start()

    cell_pass(f_ref, off_ref, load_cat, load_hl, held, ready, (ga_ref, gb_ref), genes_total)
    wait_all(kept)


def out_copies(moved, outs, sems):
    return [pltpu.make_async_copy(moved.at[i], out, sems.at[i]) for i, out in enumerate(outs)]


def gene_kernel(
    tile_ref, ga_ref, gb_ref, off_ref, counts, f_ref, fm_ref, fv_ref, l_ref,
    la_ref, lb_ref, nf_hbm, nm_hbm, nv_hbm, moved, cell_cat, cell_hl, sems, *, cells_total
):
    held = f_ref, fm_ref, fv_ref
    width, cells = moved.shape[1:]
    half = cells // LANES // 2
    tile = move(
        held, lambda c: (ga_ref if c < half else gb_ref)[c % half * width : (c % half + 1) * width, :],
        jnp.sum(tile_ref[...]), cells_total * width, rate_factors, moved,
    )
    copies = start_all(out_copies(moved, (nf_hbm, nm_hbm, nv_hbm), sems))
    rows = la_ref.shape[1]
    for h in range(2):
        la_ref[h, rows - SUB : rows, :] = tile
    set_cells(moved[0], off_ref[...], cell_cat, cell_hl)
    gene_pass(l_ref, cell_cat, cell_hl, counts, (la_ref, lb_ref), cells_total)
    wait_all(copies)


def loading_rows(la_ref, lb_ref, width, genes):
    per = genes // LANES // 4

    def grad_row(c):
        q = c // per
        return (la_ref, lb_ref)[q // 2][q % 2, c % per * width : (c % per + 1) * width, :]

    return grad_row


def cell_kernel(
    tile_ref, la_ref, lb_ref, off_ref, counts, l_ref, lm_ref, lv_ref, f_ref,
    ga_ref, gb_ref, nl_hbm, nm_hbm, nv_hbm, moved, load_cat, load_hl, sems, *, genes_total
):
    held = l_ref, lm_ref, lv_ref
    width, genes = moved.shape[1:]
    tile = move(
        held, loading_rows(la_ref, lb_ref, width, genes), jnp.sum(tile_ref[...]), genes_total * width, rate_loadings, moved
    )
    copies = start_all(out_copies(moved, (nl_hbm, nm_hbm, nv_hbm), sems))
    ga_ref[ga_ref.shape[0] - SUB :, :] = tile
    set_loads(moved[0], load_cat, load_hl)
    cell_pass(f_ref, off_ref, load_cat, load_hl, counts, None, (ga_ref, gb_ref), genes_total)
    wait_all(copies)


def last_kernel(
    tile_ref, la_ref, lb_ref, l_ref, lm_ref, lv_ref, nl_hbm, nm_hbm, nv_hbm, moved, sems, *, genes_total
):
    held = l_ref, lm_ref, lv_ref
    width, genes = moved.shape[1:]
    move(
        held, loading_rows(la_ref, lb_ref, width, genes), jnp.sum(tile_ref[...]), genes_total * width, rate_loadings, moved
    )
    wait_all(start_all(out_copies(moved, (nl_hbm, nm_hbm, nv_hbm), sems)))


def exchange(value, partner):
    pairs = []
    for cell in range(32):
        for z in range(4):
            x, y, core, depth = partner(cell // 8, cell // 2 % 4, cell % 2, z)
            pairs.append((cell * 4 + z, ((x * 4 + y) * 2 + core) * 4 + depth))
    return lax.ppermute(value, ("cell", "gene"), pairs)


def near(i):
    return i ^ 1


def far(i):
    return 3 - i


def other_core(value):
    return exchange(value, lambda x, y, core, z: (x, y, 1 - core, z))


def along_cells(step):
    turn = near if step % 2 == 0 else far

    def partner(x, y, core, z):
        if (step // 2 + core) % 2 == 0:
            return turn(x), y, core, z
        return x, turn(y), core, z

    return partner


def along_genes(step):
    def partner(x, y, core, z):
        return x, y, core, (near if (step + core) % 2 == 0 else far)(z)

    return partner


def sum_over_chips(values, seen=None):
    for step in range(4):
        came = [exchange(v, along_cells(step ^ i)) for i, v in enumerate(values)]
        values = [v + c for v, c in zip(values, came)]
        if seen is not None:
            seen += values
    return values


def sum_over_cores(halves):
    core = lax.axis_index("cell") % 2
    keep = lax.dynamic_index_in_dim(halves, core, 0, keepdims=False)
    give = lax.dynamic_index_in_dim(halves, 1 - core, 0, keepdims=False)
    return keep + other_core(give)


def both_halves(own):
    core = lax.axis_index("cell") % 2
    theirs = other_core(own)
    return jnp.stack([jnp.where(core == 0, own, theirs), jnp.where(core == 0, theirs, own)])


def sum_over_cells(first, second):
    seen = []
    first, second = sum_over_chips([sum_over_cores(first), sum_over_cores(second)], seen)
    return both_halves(first), both_halves(second), seen


def on_device(counts, donors, offset_table, factors, factor_mean, factor_var, loadings, loading_mean, loading_var):
    width, cells = factors.shape
    genes = loadings.shape[1]
    cells_total = float(cells * lax.axis_size("cell"))
    genes_total = float(genes * lax.axis_size("gene"))
    vmem = pl.BlockSpec(memory_space=pltpu.VMEM)
    hbm = pl.BlockSpec(memory_space=pltpu.HBM)
    like = lambda *shape: jax.ShapeDtypeStruct(shape, f32)
    cell_rows = width * cells // LANES // 2
    gene_rows = width * genes // LANES // 4
    flops = 2 * (2 * DEPTH) * cells * genes
    dma = lambda n: pltpu.SemaphoreType.DMA((n,))
    in_vmem = lambda *shape: pltpu.VMEM(shape, f32)
    operand = lambda *shape: pltpu.VMEM(shape, bf16)
    three_f, three_l = [like(width, cells)] * 3, [like(width, genes)] * 3
    cell_grad = [like(cell_rows + SUB, LANES), like(cell_rows, LANES)]
    gene_grad = [like(2, gene_rows + SUB, LANES), like(2, gene_rows, LANES)]

    def call(kernel, name, ins, in_hbm, outs, out_hbm, scratch, work, moves=0, limit=12, **static):
        return pl.pallas_call(
            functools.partial(kernel, **static),
            name=name,
            in_specs=[vmem] * len(ins) + [hbm] * len(in_hbm),
            out_specs=[vmem] * len(outs) + [hbm] * len(out_hbm),
            out_shape=[pltpu.VMEM(o.shape, o.dtype) for o in outs] + [pltpu.HBM(o.shape, o.dtype) for o in out_hbm],
            scratch_shapes=list(scratch),
            compiler_params=pltpu.CompilerParams(vmem_limit_bytes=(limit << 20) if work else 4 << 20),
            cost_estimate=pl.CostEstimate(
                flops=int(flops * work), bytes_accessed=4 * width * cells + moves, transcendentals=int(cells * genes * work)
            ),
        )(
            *(pltpu.with_memory_space_constraint(x, pltpu.VMEM) for x in ins),
            *(pltpu.with_memory_space_constraint(x, pltpu.HBM) for x in in_hbm),
        )

    def bring(after, *arrays):
        size = sum(a.size * a.dtype.itemsize for a in arrays)
        return call(
            load_kernel, "load", [after], list(arrays), [jax.ShapeDtypeStruct(a.shape, a.dtype) for a in arrays], [],
            [dma(len(arrays) + 3)], 0, size,
        )

    (fac_tile,) = call(
        total_kernel, "factor_scale_total", [], [factor_var], [like(SUB, LANES)], [],
        [in_vmem(width, cells), pltpu.SemaphoreType.DMA], 0,
    )
    fac_tile = fac_tile + other_core(fac_tile)
    donor_row, table_row = donors.reshape(1, cells), offset_table.reshape(1, -1)
    grad_a, grad_b, off, narrow = call(
        first_kernel, "cell_pass_first", [fac_tile], [donor_row, table_row, factors, loadings, loading_var, counts],
        cell_grad + [like(1, cells)], [jax.ShapeDtypeStruct((cells, genes), bf16)],
        [
            in_vmem(cells, genes), operand(cells // CELL_BLOCK, CELL_BLOCK, genes),
            pltpu.VMEM((1, cells), jnp.int32), pltpu.VMEM((1, table_row.shape[1]), jnp.int32),
            in_vmem(width, cells), in_vmem(width, genes), in_vmem(width, genes),
            operand(DEPTH, genes), operand(2 * width, genes), dma(cells // COPY_CELLS), dma(5),
            dma(cells // CELL_BLOCK),
        ],
        1, limit=36, genes_total=genes_total,
    )

    def loading_gradient(fac_tile, grad_a, grad_b, held):
        first, second, *new = call(
            gene_kernel, "gene_pass", [fac_tile, grad_a, grad_b, off, *held], [], gene_grad, three_f,
            [in_vmem(3, width, cells), operand(cells, DEPTH), operand(2 * width, cells), dma(3)], 1, cells_total=cells_total,
        )
        return first, second, new

    def factor_gradient(load_tile, grad_l, grad_m, held):
        first, second, *new = call(
            cell_kernel, "cell_pass", [load_tile, grad_l, grad_m, off, *held], [], cell_grad, three_l,
            [in_vmem(3, width, genes), operand(DEPTH, genes), operand(2 * width, genes), dma(3)], 1, genes_total=genes_total,
        )
        return first, second, new

    fac_tile = fac_tile + exchange(fac_tile, along_cells(0))
    grad_a, fac_tile = lax.optimization_barrier((grad_a, fac_tile))
    came_a, came_b = exchange(grad_a, along_genes(0)), exchange(grad_b, along_genes(1))
    fac_tile = fac_tile + exchange(fac_tile, along_cells(1))
    fac_tile, grad_a, grad_b = lax.optimization_barrier((fac_tile, grad_a + came_a, grad_b + came_b))
    came_a, came_b = exchange(grad_a, along_genes(1)), exchange(grad_b, along_genes(0))
    held = bring(grad_a, narrow, factors, factor_mean, factor_var, loadings)
    for step in (2, 3):
        fac_tile = fac_tile + exchange(fac_tile, along_cells(step))
    grad_a, grad_b = grad_a + came_a, grad_b + came_b
    load_tile = grad_a[cell_rows:]
    grad_l, grad_m, f = loading_gradient(fac_tile, grad_a, grad_b, held)
    grad_l, grad_m, seen = sum_over_cells(grad_l, grad_m)
    fac_tile = grad_l[0, gene_rows:]
    held = bring(seen[4], narrow, loadings, loading_mean, loading_var, f[0])
    grad_a, grad_b, l = factor_gradient(load_tile, grad_l, grad_m, held)
    came_a, came_b = exchange(grad_a, along_genes(0)), exchange(grad_b, along_genes(1))
    grad_a, grad_b = grad_a + came_a, grad_b + came_b
    came_a, came_b = exchange(grad_a, along_genes(1)), exchange(grad_b, along_genes(0))
    held = bring(grad_a, narrow, *f, l[0])
    grad_a, grad_b = grad_a + came_a, grad_b + came_b
    load_tile = grad_a[cell_rows:]
    grad_l, grad_m, f = loading_gradient(fac_tile, grad_a, grad_b, held)
    grad_l, grad_m, seen = sum_over_cells(grad_l, grad_m)
    held = bring(seen[0], *l)
    l = call(
        last_kernel, "loading_move", [load_tile, grad_l, grad_m, *held], [], [], three_l, [in_vmem(3, width, genes), dma(3)],
        0, genes_total=genes_total,
    )
    return (*f, *l)


def solution(mesh):
    by_cell, by_gene = P(None, "cell"), P(None, "gene")
    return jax.shard_map(
        on_device,
        mesh=mesh,
        in_specs=(P("cell", "gene"), P("cell"), P(), by_cell, by_cell, by_cell, by_gene, by_gene, by_gene),
        out_specs=(by_cell, by_cell, by_cell, by_gene, by_gene, by_gene),
        check_vma=False,
    )
```

time: 191 us -> 141 us (0.74)
  waiting for transfers between devices: 73.3 us -> 44.9 us
  local copies, waits for them, and re-layouts: 25.7 us -> 0.06 us
  starting transfers between devices: 42.7 us -> 47 us
  other arithmetic: 4.01 us -> 0.88 us
  Pallas kernels: 43.5 us -> 46.6 us
    ppermute x21 -> x37, waiting for transfers between devices: 73.3 us -> 44.9 us  [exchange(): return lax.ppermute(value, ('cell', 'gene'), pairs)]
    unnamed x40 -> x0, local copies, waits for them, and re-layouts: 24.9 us -> none
    ppermute x21 -> x37, starting transfers between devices: 42.7 us -> 47 us  [exchange(): return lax.ppermute(value, ('cell', 'gene'), pairs)]
    pallas_call x6 -> x10, Pallas kernels: 43.5 us -> 46.6 us  [call(): pl.pallas_call(functools.partial(kernel, **static), name=name, in_specs=[...]
    add x18 -> x32, other arithmetic: 2.91 us -> 0.65 us  [the longest x16 0.3 us: sum_over_chips(): values = [v + c for v, c in zip(values, came)]]
  transfers between devices with their start and end apart: 21 -> 37, of which waited for: 20 -> 20; matrix products, arithmetic and copies ran while one was open for 0% -> 0% of each run, Pallas kernels for 0% -> 19%
where the time goes in v2:
time: 141 us
  starting transfers between devices  47 us (33%)
  Pallas kernels  46.6 us (33%)
  waiting for transfers between devices  44.9 us (32%)
    ppermute x37, starting transfers between devices, exchange(): return lax.ppermute(value, ('cell', 'gene'), pairs)  47 us
    pallas_call x10, Pallas kernels, call(): pl.pallas_call(functools.partial(kernel, **static), name=name, in_specs=[...  46.6 us
    ppermute x37, waiting for transfers between devices, exchange(): return lax.ppermute(value, ('cell', 'gene'), pairs)  44.9 us
  transfers between devices with their start and end apart: 37, of which 20 were waited for; matrix products, arithmetic and copies ran while one was open for 0% of the time, Pallas kernels for 19%

profile of v2, /device:TPU:1, one launch (start us, length us, event | category | flops | bytes accessed | tf_op | source)
XLA Modules:
  0.0 140.7 jit_solution(2953052906067333653)
XLA Ops:
  5.6 12.7 %cell_pass_first.1 = (f32[520,128]{1,0:T(8,128)S(1)}, f32[512,128]{1,0:T(8,128)S(1)}, f32[1,2048]{1,0:T(1,128)S(1)}, bf16[2048,2048]{1,0:T(8,128)(2,1)}) custom-call(f32[8,128]{1,0:T(8,128)S(1)} %add.126.tile_ref, s32[1,2048]{1,0:T(1,128)} %bitcast.36, s32[1,128]{1,0:T(1,128)} %bitcast.37, f32[64,2048]{1,0:T(8,128)} %refs_1_.2, f32[64,2048]{1,0:T(8,128)} %refs_1_.3, ...), custom_call_target="tpu_custom_call" | custom-call | flops 4294967296 | bytes 524288 | tf_op jit(solution)/shard_map/cell_pass_first/pallas_call | solution.py:380
  18.4 3.8 %collective-permute-start.3 = (f32[520,128]{1,0:T(8,128)S(1)}, f32[520,128]{1,0:T(8,128)S(1)}, u32[]{:S(2)}, u32[]{:S(2)}) collective-permute-start(f32[520,128]{1,0:T(8,128)S(1)} %get-tuple-element.53), channel_id=1, source_target_pairs={{0,1},{1,0},{2,3},{3,2},{4,7},{5,6},{6,5},{7,4},{8,9},{9,8},{10,11... | collective-permute-start | bytes 798728 | tf_op jit(solution)/shard_map/ppermute | solution.py:300
  30.6 2.3 %collective-permute-start.5 = (f32[8,128]{1,0:T(8,128)S(1)}, f32[8,128]{1,0:T(8,128)S(1)}, u32[]{:S(2)}, u32[]{:S(2)}) collective-permute-start(f32[8,128]{1,0:T(8,128)S(1)} %add.128), channel_id=1, source_target_pairs={{0,8},{1,9},{2,10},{3,11},{4,36},{5,37},{6,38},{7,39},{8,0},{9,1},... | collective-permute-start | bytes 12296 | tf_op jit(solution)/shard_map/ppermute | solution.py:300
  36.3 4.1 %load.4 = (bf16[2048,2048]{1,0:T(8,128)(2,1)S(1)}, f32[64,2048]{1,0:T(8,128)S(1)}, f32[64,2048]{1,0:T(8,128)S(1)}, f32[64,2048]{1,0:T(8,128)S(1)}, f32[64,2048]{1,0:T(8,128)S(1)}) custom-call(f32[520,128]{1,0:T(8,128)S(1)} %add.129.after_ref, bf16[2048,2048]{1,0:T(8,128)(2,1)} %get-tuple-element.59.refs_0_, f32[64,2048]{1,0:T(8,128)} %refs_1_.2, ...), custom_call_target="tpu_custom_call" | custom-call | bytes 11010048 | tf_op jit(solution)/shard_map/load/pallas_call | solution.py:380
  40.5 5.7 %gene_pass.2 = (f32[2,264,128]{2,1,0:T(8,128)S(1)}, f32[2,256,128]{2,1,0:T(8,128)S(1)}, f32[64,2048]{1,0:T(8,128)}, f32[64,2048]{1,0:T(8,128)}, f32[64,2048]{1,0:T(8,128)}) custom-call(f32[8,128]{1,0:T(8,128)S(1)} %add.132.tile_ref, f32[520,128]{1,0:T(8,128)S(1)} %add.133.ga_ref, f32[512,128]{1,0:T(8,128)S(1)} %add.134.gb_ref, ...), custom_call_target="tpu_custom_call" | custom-call | flops 4294967296 | bytes 524288 | tf_op jit(solution)/shard_map/gene_pass/pallas_call | solution.py:380
  46.2 2.2 %collective-permute-start.15 = (f32[256,128]{1,0:T(8,128)S(1)}, f32[256,128]{1,0:T(8,128)S(1)}, u32[]{:S(2)}, u32[]{:S(2)}) collective-permute-start(f32[256,128]{1,0:T(8,128)S(1)} %dynamic-slice_bitcast_fusion.3), channel_id=1, source_target_pairs={{0,4},{1,5},{2,6},{3,7},{4,0},{5,1},{6,2},{7,3},{8,12},{9,13},{10,... | collective-permute-start | bytes 393224 | tf_op jit(solution)/shard_map/ppermute | solution.py:300
  50.4 4.4 %collective-permute-done.16 = f32[256,128]{1,0:T(8,128)S(1)} collective-permute-done((f32[256,128]{1,0:T(8,128)S(1)}, f32[256,128]{1,0:T(8,128)S(1)}, u32[]{:S(2)}, u32[]{:S(2)}) %collective-permute-start.16) | collective-permute-done | bytes 131104 | tf_op jit(solution)/shard_map/ppermute | solution.py:300
  56.5 2.2 %collective-permute-done.17 = f32[256,128]{1,0:T(8,128)S(1)} collective-permute-done((f32[256,128]{1,0:T(8,128)S(1)}, f32[256,128]{1,0:T(8,128)S(1)}, u32[]{:S(2)}, u32[]{:S(2)}) %collective-permute-start.17) | collective-permute-done | bytes 131104 | tf_op jit(solution)/shard_map/ppermute | solution.py:300
  58.8 2.6 %collective-permute-start.18 = (f32[256,128]{1,0:T(8,128)S(1)}, f32[256,128]{1,0:T(8,128)S(1)}, u32[]{:S(2)}, u32[]{:S(2)}) collective-permute-start(f32[256,128]{1,0:T(8,128)S(1)} %add.144), channel_id=1, source_target_pairs={{0,24},{1,25},{2,26},{3,27},{4,100},{5,101},{6,102},{7,103},{8,16}... | collective-permute-start | bytes 393224 | tf_op jit(solution)/shard_map/ppermute | solution.py:300
  61.5 3.3 %collective-permute-done.18 = f32[256,128]{1,0:T(8,128)S(1)} collective-permute-done((f32[256,128]{1,0:T(8,128)S(1)}, f32[256,128]{1,0:T(8,128)S(1)}, u32[]{:S(2)}, u32[]{:S(2)}) %collective-permute-start.18) | collective-permute-done | bytes 131104 | tf_op jit(solution)/shard_map/ppermute | solution.py:300
  66.7 2.3 %collective-permute-done.19 = f32[256,128]{1,0:T(8,128)S(1)} collective-permute-done((f32[256,128]{1,0:T(8,128)S(1)}, f32[256,128]{1,0:T(8,128)S(1)}, u32[]{:S(2)}, u32[]{:S(2)}) %collective-permute-start.19) | collective-permute-done | bytes 131104 | tf_op jit(solution)/shard_map/ppermute | solution.py:300
  69.0 3.5 %collective-permute-start.20 = (f32[256,128]{1,0:T(8,128)S(1)}, f32[256,128]{1,0:T(8,128)S(1)}, u32[]{:S(2)}, u32[]{:S(2)}) collective-permute-start(f32[256,128]{1,0:T(8,128)S(1)} %add.146), channel_id=1, source_target_pairs={{0,4},{1,5},{2,6},{3,7},{4,0},{5,1},{6,2},{7,3},{8,12},{9,13},{10,... | collective-permute-start | bytes 393224 | tf_op jit(solution)/shard_map/ppermute | solution.py:300
  72.6 4.0 %load.5 = (bf16[2048,2048]{1,0:T(8,128)(2,1)S(1)}, f32[64,2048]{1,0:T(8,128)S(1)}, f32[64,2048]{1,0:T(8,128)S(1)}, f32[64,2048]{1,0:T(8,128)S(1)}, f32[64,2048]{1,0:T(8,128)S(1)}) custom-call(f32[264,128]{1,0:T(8,128)S(1)} %add.140.after_ref, bf16[2048,2048]{1,0:T(8,128)(2,1)} %get-tuple-element.59.refs_0_, f32[64,2048]{1,0:T(8,128)} %refs_1_.3, ...), custom_call_target="tpu_custom_call" | custom-call | bytes 11010048 | tf_op jit(solution)/shard_map/load/pallas_call | solution.py:380
  78.4 6.0 %cell_pass.1 = (f32[520,128]{1,0:T(8,128)S(1)}, f32[512,128]{1,0:T(8,128)S(1)}, f32[64,2048]{1,0:T(8,128)}, f32[64,2048]{1,0:T(8,128)}, f32[64,2048]{1,0:T(8,128)}) custom-call(f32[8,128]{1,0:T(8,128)S(1)} %slice.13.tile_ref, f32[2,264,128]{2,1,0:T(8,128)S(1)} %pad_maximum_fusion.la_ref, f32[2,256,128]{2,1,0:T(8,128)S(1)} %pad_maximum_fusion.2.lb_ref, ...), custom_call_target="tpu_custom_call" | custom-call | flops 4294967296 | bytes 524288 | tf_op jit(solution)/shard_map/cell_pass/pallas_call | solution.py:380
  86.3 5.1 %collective-permute-done.21 = f32[520,128]{1,0:T(8,128)S(1)} collective-permute-done((f32[520,128]{1,0:T(8,128)S(1)}, f32[520,128]{1,0:T(8,128)S(1)}, u32[]{:S(2)}, u32[]{:S(2)}) %collective-permute-start.21) | collective-permute-done | bytes 266272 | tf_op jit(solution)/shard_map/ppermute | solution.py:300
  91.4 2.7 %collective-permute-start.22 = (f32[520,128]{1,0:T(8,128)S(1)}, f32[520,128]{1,0:T(8,128)S(1)}, u32[]{:S(2)}, u32[]{:S(2)}) collective-permute-start(f32[520,128]{1,0:T(8,128)S(1)} %add.147.after_ref), channel_id=1, source_target_pairs={{0,3},{1,2},{2,1},{3,0},{4,5},{5,4},{6,7},{7,6},{8,11},{9,10},{10,... | collective-permute-start | bytes 798728 | tf_op jit(solution)/shard_map/ppermute | solution.py:300
  95.0 4.0 %load.6 = (bf16[2048,2048]{1,0:T(8,128)(2,1)S(1)}, f32[64,2048]{1,0:T(8,128)S(1)}, f32[64,2048]{1,0:T(8,128)S(1)}, f32[64,2048]{1,0:T(8,128)S(1)}, f32[64,2048]{1,0:T(8,128)S(1)}) custom-call(f32[520,128]{1,0:T(8,128)S(1)} %add.147.after_ref, bf16[2048,2048]{1,0:T(8,128)(2,1)} %get-tuple-element.59.refs_0_, f32[64,2048]{1,0:T(8,128)} %get-tuple-element.67.refs_4_.refs_1_, ...), custom_call_target="tpu_custom_call" | custom-call | bytes 11010048 | tf_op jit(solution)/shard_map/load/pallas_call | solution.py:380
  99.0 4.6 %collective-permute-done.24 = f32[512,128]{1,0:T(8,128)S(1)} collective-permute-done((f32[512,128]{1,0:T(8,128)S(1)}, f32[512,128]{1,0:T(8,128)S(1)}, u32[]{:S(2)}, u32[]{:S(2)}) %collective-permute-start.24) | collective-permute-done | bytes 262176 | tf_op jit(solution)/shard_map/ppermute | solution.py:300
  103.6 5.7 %gene_pass.3 = (f32[2,264,128]{2,1,0:T(8,128)S(1)}, f32[2,256,128]{2,1,0:T(8,128)S(1)}, f32[64,2048]{1,0:T(8,128)}, f32[64,2048]{1,0:T(8,128)}, f32[64,2048]{1,0:T(8,128)}) custom-call(f32[8,128]{1,0:T(8,128)S(1)} %slice_bitcast_fusion.tile_ref, f32[520,128]{1,0:T(8,128)S(1)} %add.148.ga_ref, f32[512,128]{1,0:T(8,128)S(1)} %add.150.gb_ref, ...), custom_call_target="tpu_custom_call" | custom-call | flops 4294967296 | bytes 524288 | tf_op jit(solution)/shard_map/gene_pass/pallas_call | solution.py:380
  111.9 4.4 %collective-permute-done.32 = f32[256,128]{1,0:T(8,128)S(1)} collective-permute-done((f32[256,128]{1,0:T(8,128)S(1)}, f32[256,128]{1,0:T(8,128)S(1)}, u32[]{:S(2)}, u32[]{:S(2)}) %collective-permute-start.32) | collective-permute-done | bytes 131104 | tf_op jit(solution)/shard_map/ppermute | solution.py:300
  118.1 2.5 %collective-permute-done.33 = f32[256,128]{1,0:T(8,128)S(1)} collective-permute-done((f32[256,128]{1,0:T(8,128)S(1)}, f32[256,128]{1,0:T(8,128)S(1)}, u32[]{:S(2)}, u32[]{:S(2)}) %collective-permute-start.33) | collective-permute-done | bytes 131104 | tf_op jit(solution)/shard_map/ppermute | solution.py:300
  120.6 2.5 %collective-permute-start.34 = (f32[256,128]{1,0:T(8,128)S(1)}, f32[256,128]{1,0:T(8,128)S(1)}, u32[]{:S(2)}, u32[]{:S(2)}) collective-permute-start(f32[256,128]{1,0:T(8,128)S(1)} %add.158), channel_id=1, source_target_pairs={{0,24},{1,25},{2,26},{3,27},{4,100},{5,101},{6,102},{7,103},{8,16}... | collective-permute-start | bytes 393224 | tf_op jit(solution)/shard_map/ppermute | solution.py:300
  123.2 3.1 %collective-permute-done.34 = f32[256,128]{1,0:T(8,128)S(1)} collective-permute-done((f32[256,128]{1,0:T(8,128)S(1)}, f32[256,128]{1,0:T(8,128)S(1)}, u32[]{:S(2)}, u32[]{:S(2)}) %collective-permute-start.34) | collective-permute-done | bytes 131104 | tf_op jit(solution)/shard_map/ppermute | solution.py:300
  130.6 3.8 %collective-permute-start.36 = (f32[256,128]{1,0:T(8,128)S(1)}, f32[256,128]{1,0:T(8,128)S(1)}, u32[]{:S(2)}, u32[]{:S(2)}) collective-permute-start(f32[256,128]{1,0:T(8,128)S(1)} %add.160), channel_id=1, source_target_pairs={{0,4},{1,5},{2,6},{3,7},{4,0},{5,1},{6,2},{7,3},{8,12},{9,13},{10,... | collective-permute-start | bytes 393224 | tf_op jit(solution)/shard_map/ppermute | solution.py:300
  (108 shorter events, 41.8 us)
Async XLA Ops:
  4.3 14.1 %collective-permute-start.1 = (f32[8,128]{1,0:T(8,128)S(1)}, f32[8,128]{1,0:T(8,128)S(1)}, u32[]{:S(2)}, u32[]{:S(2)}) collective-permute-start(f32[8,128]{1,0:T(8,128)S(1)} %add.126.tile_ref), channel_id=1, source_target_pairs={{0,32},{1,33},{2,34},{3,35},{4,12},{5,13},{6,14},{7,15},{8,40},{9,... | collective-permute-start | bytes 12296 | tf_op jit(solution)/shard_map/ppermute | solution.py:300
  18.4 9.5 %collective-permute-start.3 = (f32[520,128]{1,0:T(8,128)S(1)}, f32[520,128]{1,0:T(8,128)S(1)}, u32[]{:S(2)}, u32[]{:S(2)}) collective-permute-start(f32[520,128]{1,0:T(8,128)S(1)} %get-tuple-element.53), channel_id=1, source_target_pairs={{0,1},{1,0},{2,3},{3,2},{4,7},{5,6},{6,5},{7,4},{8,9},{9,8},{10,11... | collective-permute-start | bytes 798728 | tf_op jit(solution)/shard_map/ppermute | solution.py:300
  22.2 5.6 %collective-permute-start.4 = (f32[512,128]{1,0:T(8,128)S(1)}, f32[512,128]{1,0:T(8,128)S(1)}, u32[]{:S(2)}, u32[]{:S(2)}) collective-permute-start(f32[512,128]{1,0:T(8,128)S(1)} %get-tuple-element.54), channel_id=1, source_target_pairs={{0,3},{1,2},{2,1},{3,0},{4,5},{5,4},{6,7},{7,6},{8,11},{9,10},{10,... | collective-permute-start | bytes 786440 | tf_op jit(solution)/shard_map/ppermute | solution.py:300
  27.9 12.5 %collective-permute-start.7 = (f32[520,128]{1,0:T(8,128)S(1)}, f32[520,128]{1,0:T(8,128)S(1)}, u32[]{:S(2)}, u32[]{:S(2)}) collective-permute-start(f32[520,128]{1,0:T(8,128)S(1)} %add.129.after_ref), channel_id=1, source_target_pairs={{0,3},{1,2},{2,1},{3,0},{4,5},{5,4},{6,7},{7,6},{8,11},{9,10},{10,... | collective-permute-start | bytes 798728 | tf_op jit(solution)/shard_map/ppermute | solution.py:300
  29.3 11.1 %collective-permute-start.8 = (f32[512,128]{1,0:T(8,128)S(1)}, f32[512,128]{1,0:T(8,128)S(1)}, u32[]{:S(2)}, u32[]{:S(2)}) collective-permute-start(f32[512,128]{1,0:T(8,128)S(1)} %add.130), channel_id=1, source_target_pairs={{0,1},{1,0},{2,3},{3,2},{4,7},{5,6},{6,5},{7,4},{8,9},{9,8},{10,11... | collective-permute-start | bytes 786440 | tf_op jit(solution)/shard_map/ppermute | solution.py:300
  34.2 6.2 %collective-permute-start.6 = (f32[8,128]{1,0:T(8,128)S(1)}, f32[8,128]{1,0:T(8,128)S(1)}, u32[]{:S(2)}, u32[]{:S(2)}) collective-permute-start(f32[8,128]{1,0:T(8,128)S(1)} %add.131), channel_id=1, source_target_pairs={{0,24},{1,25},{2,26},{3,27},{4,100},{5,101},{6,102},{7,103},{8,16}... | collective-permute-start | bytes 12296 | tf_op jit(solution)/shard_map/ppermute | solution.py:300
  49.4 5.4 %collective-permute-start.16 = (f32[256,128]{1,0:T(8,128)S(1)}, f32[256,128]{1,0:T(8,128)S(1)}, u32[]{:S(2)}, u32[]{:S(2)}) collective-permute-start(f32[256,128]{1,0:T(8,128)S(1)} %bitcast_add_fusion.3), channel_id=1, source_target_pairs={{0,96},{1,97},{2,98},{3,99},{4,28},{5,29},{6,30},{7,31},{8,104},{9... | collective-permute-start | bytes 393224 | tf_op jit(solution)/shard_map/ppermute | solution.py:300
  50.3 4.6 %collective-permute-start.10 = (f32[264,128]{1,0:T(8,128)S(1)}, f32[264,128]{1,0:T(8,128)S(1)}, u32[]{:S(2)}, u32[]{:S(2)}) collective-permute-start(f32[264,128]{1,0:T(8,128)S(1)} %bitcast_add_fusion.1), channel_id=1, source_target_pairs={{0,32},{1,33},{2,34},{3,35},{4,12},{5,13},{6,14},{7,15},{8,40},{9,... | collective-permute-start | bytes 405512 | tf_op jit(solution)/shard_map/ppermute | solution.py:300
  55.0 6.4 %collective-permute-start.11 = (f32[264,128]{1,0:T(8,128)S(1)}, f32[264,128]{1,0:T(8,128)S(1)}, u32[]{:S(2)}, u32[]{:S(2)}) collective-permute-start(f32[264,128]{1,0:T(8,128)S(1)} %add.138), channel_id=1, source_target_pairs={{0,96},{1,97},{2,98},{3,99},{4,28},{5,29},{6,30},{7,31},{8,104},{9... | collective-permute-start | bytes 405512 | tf_op jit(solution)/shard_map/ppermute | solution.py:300
  58.8 6.0 %collective-permute-start.18 = (f32[256,128]{1,0:T(8,128)S(1)}, f32[256,128]{1,0:T(8,128)S(1)}, u32[]{:S(2)}, u32[]{:S(2)}) collective-permute-start(f32[256,128]{1,0:T(8,128)S(1)} %add.144), channel_id=1, source_target_pairs={{0,24},{1,25},{2,26},{3,27},{4,100},{5,101},{6,102},{7,103},{8,16}... | collective-permute-start | bytes 393224 | tf_op jit(solution)/shard_map/ppermute | solution.py:300
  64.8 4.2 %collective-permute-start.19 = (f32[256,128]{1,0:T(8,128)S(1)}, f32[256,128]{1,0:T(8,128)S(1)}, u32[]{:S(2)}, u32[]{:S(2)}) collective-permute-start(f32[256,128]{1,0:T(8,128)S(1)} %add.145), channel_id=1, source_target_pairs={{0,8},{1,9},{2,10},{3,11},{4,36},{5,37},{6,38},{7,39},{8,0},{9,1},... | collective-permute-start | bytes 393224 | tf_op jit(solution)/shard_map/ppermute | solution.py:300
  65.3 11.3 %collective-permute-start.13 = (f32[264,128]{1,0:T(8,128)S(1)}, f32[264,128]{1,0:T(8,128)S(1)}, u32[]{:S(2)}, u32[]{:S(2)}) collective-permute-start(f32[264,128]{1,0:T(8,128)S(1)} %add.140.after_ref), channel_id=1, source_target_pairs={{0,24},{1,25},{2,26},{3,27},{4,100},{5,101},{6,102},{7,103},{8,16}... | collective-permute-start | bytes 405512 | tf_op jit(solution)/shard_map/ppermute | solution.py:300
  69.0 7.9 %collective-permute-start.20 = (f32[256,128]{1,0:T(8,128)S(1)}, f32[256,128]{1,0:T(8,128)S(1)}, u32[]{:S(2)}, u32[]{:S(2)}) collective-permute-start(f32[256,128]{1,0:T(8,128)S(1)} %add.146), channel_id=1, source_target_pairs={{0,4},{1,5},{2,6},{3,7},{4,0},{5,1},{6,2},{7,3},{8,12},{9,13},{10,... | collective-permute-start | bytes 393224 | tf_op jit(solution)/shard_map/ppermute | solution.py:300
  84.4 7.0 %collective-permute-start.21 = (f32[520,128]{1,0:T(8,128)S(1)}, f32[520,128]{1,0:T(8,128)S(1)}, u32[]{:S(2)}, u32[]{:S(2)}) collective-permute-start(f32[520,128]{1,0:T(8,128)S(1)} %get-tuple-element.73), channel_id=1, source_target_pairs={{0,1},{1,0},{2,3},{3,2},{4,7},{5,6},{6,5},{7,4},{8,9},{9,8},{10,11... | collective-permute-start | bytes 798728 | tf_op jit(solution)/shard_map/ppermute | solution.py:300
  85.0 9.1 %collective-permute-start.23 = (f32[512,128]{1,0:T(8,128)S(1)}, f32[512,128]{1,0:T(8,128)S(1)}, u32[]{:S(2)}, u32[]{:S(2)}) collective-permute-start(f32[512,128]{1,0:T(8,128)S(1)} %get-tuple-element.74), channel_id=1, source_target_pairs={{0,3},{1,2},{2,1},{3,0},{4,5},{5,4},{6,7},{7,6},{8,11},{9,10},{10,... | collective-permute-start | bytes 786440 | tf_op jit(solution)/shard_map/ppermute | solution.py:300
  91.4 12.2 %collective-permute-start.22 = (f32[520,128]{1,0:T(8,128)S(1)}, f32[520,128]{1,0:T(8,128)S(1)}, u32[]{:S(2)}, u32[]{:S(2)}) collective-permute-start(f32[520,128]{1,0:T(8,128)S(1)} %add.147.after_ref), channel_id=1, source_target_pairs={{0,3},{1,2},{2,1},{3,0},{4,5},{5,4},{6,7},{7,6},{8,11},{9,10},{10,... | collective-permute-start | bytes 798728 | tf_op jit(solution)/shard_map/ppermute | solution.py:300
  94.1 9.5 %collective-permute-start.24 = (f32[512,128]{1,0:T(8,128)S(1)}, f32[512,128]{1,0:T(8,128)S(1)}, u32[]{:S(2)}, u32[]{:S(2)}) collective-permute-start(f32[512,128]{1,0:T(8,128)S(1)} %add.149), channel_id=1, source_target_pairs={{0,1},{1,0},{2,3},{3,2},{4,7},{5,6},{6,5},{7,4},{8,9},{9,8},{10,11... | collective-permute-start | bytes 786440 | tf_op jit(solution)/shard_map/ppermute | solution.py:300
  111.0 5.4 %collective-permute-start.32 = (f32[256,128]{1,0:T(8,128)S(1)}, f32[256,128]{1,0:T(8,128)S(1)}, u32[]{:S(2)}, u32[]{:S(2)}) collective-permute-start(f32[256,128]{1,0:T(8,128)S(1)} %bitcast_add_fusion.2), channel_id=1, source_target_pairs={{0,96},{1,97},{2,98},{3,99},{4,28},{5,29},{6,30},{7,31},{8,104},{9... | collective-permute-start | bytes 393224 | tf_op jit(solution)/shard_map/ppermute | solution.py:300
  111.8 4.9 %collective-permute-start.26 = (f32[264,128]{1,0:T(8,128)S(1)}, f32[264,128]{1,0:T(8,128)S(1)}, u32[]{:S(2)}, u32[]{:S(2)}) collective-permute-start(f32[264,128]{1,0:T(8,128)S(1)} %bitcast_add_fusion), channel_id=1, source_target_pairs={{0,32},{1,33},{2,34},{3,35},{4,12},{5,13},{6,14},{7,15},{8,40},{9,... | collective-permute-start | bytes 405512 | tf_op jit(solution)/shard_map/ppermute | solution.py:300
  116.8 6.3 %collective-permute-start.27 = (f32[264,128]{1,0:T(8,128)S(1)}, f32[264,128]{1,0:T(8,128)S(1)}, u32[]{:S(2)}, u32[]{:S(2)}) collective-permute-start(f32[264,128]{1,0:T(8,128)S(1)} %add.152.after_ref), channel_id=1, source_target_pairs={{0,96},{1,97},{2,98},{3,99},{4,28},{5,29},{6,30},{7,31},{8,104},{9... | collective-permute-start | bytes 405512 | tf_op jit(solution)/shard_map/ppermute | solution.py:300
  120.6 5.7 %collective-permute-start.34 = (f32[256,128]{1,0:T(8,128)S(1)}, f32[256,128]{1,0:T(8,128)S(1)}, u32[]{:S(2)}, u32[]{:S(2)}) collective-permute-start(f32[256,128]{1,0:T(8,128)S(1)} %add.158), channel_id=1, source_target_pairs={{0,24},{1,25},{2,26},{3,27},{4,100},{5,101},{6,102},{7,103},{8,16}... | collective-permute-start | bytes 393224 | tf_op jit(solution)/shard_map/ppermute | solution.py:300
  126.3 4.2 %collective-permute-start.35 = (f32[256,128]{1,0:T(8,128)S(1)}, f32[256,128]{1,0:T(8,128)S(1)}, u32[]{:S(2)}, u32[]{:S(2)}) collective-permute-start(f32[256,128]{1,0:T(8,128)S(1)} %add.159), channel_id=1, source_target_pairs={{0,8},{1,9},{2,10},{3,11},{4,36},{5,37},{6,38},{7,39},{8,0},{9,1},... | collective-permute-start | bytes 393224 | tf_op jit(solution)/shard_map/ppermute | solution.py:300
  127.1 8.8 %collective-permute-start.29 = (f32[264,128]{1,0:T(8,128)S(1)}, f32[264,128]{1,0:T(8,128)S(1)}, u32[]{:S(2)}, u32[]{:S(2)}) collective-permute-start(f32[264,128]{1,0:T(8,128)S(1)} %add.154), channel_id=1, source_target_pairs={{0,24},{1,25},{2,26},{3,27},{4,100},{5,101},{6,102},{7,103},{8,16}... | collective-permute-start | bytes 405512 | tf_op jit(solution)/shard_map/ppermute | solution.py:300
  130.6 7.2 %collective-permute-start.36 = (f32[256,128]{1,0:T(8,128)S(1)}, f32[256,128]{1,0:T(8,128)S(1)}, u32[]{:S(2)}, u32[]{:S(2)}) collective-permute-start(f32[256,128]{1,0:T(8,128)S(1)} %add.160), channel_id=1, source_target_pairs={{0,4},{1,5},{2,6},{3,7},{4,0},{5,1},{6,2},{7,3},{8,12},{9,13},{10,... | collective-permute-start | bytes 393224 | tf_op jit(solution)/shard_map/ppermute | solution.py:300
  (13 other events, 38.8 us)

commit v3 on v2

--- a/solution.py
+++ b/solution.py
@@ -20,12 +20,13 @@
 DEPTH = 256
 f32 = jnp.float32
 bf16 = jnp.bfloat16
-LOW = False
 CELL_BLOCK = 512
 GENE_BLOCK = 256
 COPY_CELLS = 256
 PARTS = 2
 CHUNK = 512
+FIRST_LOW_CHUNKS = 2
+NARROW = jnp.float8_e4m3fn
 
 
 def split(x):
@@ -78,6 +79,11 @@
     load_hl[...] = jnp.concatenate([high, low], 0)
 
 
+def set_cell_cat(f, off, cell_cat):
+    _, _, cat = cell_operand(f, off)
+    cell_cat[...] = cat.T
+
+
 def set_cells(f, off, cell_cat, cell_hl):
     high, low, cat = cell_operand(f, off)
     cell_cat[...] = cat.T
@@ -99,42 +105,49 @@
     return copies
 
 
-def cell_pass(f_ref, off_ref, load_cat, load_hl, counts, stream, g_refs, genes_total):
-    width, cells = f_ref.shape
+def cell_pass(cell_cat, load_cat, load_hl, counts, g_refs, genes_total, low_chunks):
+    cells, genes = cell_cat.shape[0], load_cat.shape[1]
+    width = load_hl.shape[0] // 2
     blocks = cells // CELL_BLOCK
     rows = width * CELL_BLOCK // LANES
     last = (((1,), (1,)), ((), ()))
     for b in range(blocks):
-        at = slice(b * CELL_BLOCK, (b + 1) * CELL_BLOCK)
-        _, _, cat = cell_operand(f_ref[:, at], off_ref[:, at])
-        lhs = cat.T
-        if stream is not None:
-            stream(b)
+        lhs = cell_cat[b * CELL_BLOCK : (b + 1) * CELL_BLOCK, :]
+        held = counts(b)
+
+        def lin_of(g):
+            return jnp.dot(lhs, load_cat[:, g : g + CHUNK], preferred_element_type=f32)
+
         total, small = None, None
-        for g in range(0, load_cat.shape[1], CHUNK):
+        lin = lin_of(0)
+        for g in range(0, genes, CHUNK):
             of = slice(g, g + CHUNK)
-            lin = jnp.dot(lhs, load_cat[:, of], preferred_element_type=f32)
-            high, low = split(jnp.exp2(lin) - counts[at, of].astype(f32))
+            resid = jnp.exp2(lin) - held[:, of].astype(f32)
+            if low_chunks and g + CHUNK < genes:
+                lin = lin_of(g + CHUNK)
+            high, low = split(resid)
             part = lax.dot_general(load_hl[:, of], high, last, preferred_element_type=f32)
             total = part if total is None else total + part
-            if LOW:
+            if g // CHUNK < low_chunks:
                 part = lax.dot_general(load_hl[:width, of], low, last, preferred_element_type=f32)
                 small = part if small is None else small + part
+            if not low_chunks and g + CHUNK < genes:
+                lin = lin_of(g + CHUNK)
         grad = total[:width] + total[width:]
-        if LOW:
+        if low_chunks:
             grad += small
         half = blocks // 2
         g_refs[b // half][b % half * rows : (b % half + 1) * rows, :] = lane_rows(grad * (1.0 / math.sqrt(genes_total)))
 
 
-def gene_pass(l_ref, cell_cat, cell_hl, counts, g_refs, cells_total):
-    width, genes = l_ref.shape
+def gene_pass(load_cat, cell_cat, cell_hl, counts, g_refs, cells_total):
+    width, genes = cell_hl.shape[0] // 2, load_cat.shape[1]
     blocks = genes // GENE_BLOCK
     rows = width * GENE_BLOCK // LANES
     quarter = blocks // 4
     for b in range(blocks):
         at = slice(b * GENE_BLOCK, (b + 1) * GENE_BLOCK)
-        load = gene_operand(l_ref[:, at])
+        load = load_cat[:, at]
         total = None
         for c in range(0, cell_cat.shape[0], CHUNK):
             of = slice(c, c + CHUNK)
@@ -164,25 +177,66 @@
     return tile
 
 
-def total_kernel(var_hbm, tile_ref, var_ref, sem):
-    copy = pltpu.make_async_copy(var_hbm, var_ref, sem)
-    copy.start()
-    copy.wait()
-    tile_ref[...] = square_tile(inverse_root(var_ref[...]))
+def front_kernel(
+    fv_hbm, lv_hbm, l_hbm, donors_hbm, table_hbm, f_hbm, counts_hbm,
+    fac_ref, load_ref, off_ref, load_cat, load_hl, cell_cat, front, fv_ref, lv_ref, l_ref, donors_ref, table_ref, f_ref, sems
+):
+    pairs = [
+        (fv_hbm, fv_ref), (lv_hbm, lv_ref), (l_hbm, l_ref), (donors_hbm, donors_ref), (table_hbm, table_ref), (f_hbm, f_ref)
+    ]
+    copies = start_all([pltpu.make_async_copy(src, dst, sems.at[i]) for i, (src, dst) in enumerate(pairs)])
+    size = front.shape[0] // 4
+    blocks = []
+    for b in range(4):
+        at = pl.ds(b * size, size)
+        blocks.append(pltpu.make_async_copy(counts_hbm.at[at], front.at[at], sems.at[len(pairs) + b]))
+    start_all(blocks)
+    copies[0].wait()
+    fac_ref[...] = square_tile(inverse_root(fv_ref[...]))
+    copies[1].wait()
+    load_ref[...] = square_tile(inverse_root(lv_ref[...]))
+    copies[2].wait()
+    set_loads(l_ref[...], load_cat, load_hl)
+    wait_all(copies[3:])
+    off_ref[...] = offsets_of(donors_ref[...], table_ref[...])
+    set_cell_cat(f_ref[...], off_ref[...], cell_cat)
+    wait_all(blocks)
+
+
+def start_loads(sources, places, sems):
+    size = sources[0].shape[0] // 4
+    copies = []
+    for r in range(0, sources[0].shape[0], size):
+        at = pl.ds(r, size)
+        copies.append(pltpu.make_async_copy(sources[0].at[at], places[0].at[at], sems.at[len(copies)]))
+    for source, place in zip(sources[1:], places[1:]):
+        copies.append(pltpu.make_async_copy(source, place, sems.at[len(copies)]))
+    return start_all(copies[::-1])
 
 
 def load_kernel(after_ref, *refs):
     del after_ref
     *refs, sems = refs
     half = len(refs) // 2
-    size = refs[0].shape[0] // (sems.shape[0] - half + 1)
-    copies = []
-    for r in range(0, refs[0].shape[0], size):
-        at = pl.ds(r, size)
-        copies.append(pltpu.make_async_copy(refs[0].at[at], refs[half].at[at], sems.at[len(copies)]))
-    for i in range(1, half):
-        copies.append(pltpu.make_async_copy(refs[i], refs[half + i], sems.at[len(copies)]))
-    wait_all(start_all(copies))
+    wait_all(start_loads(refs[:half], refs[half:], sems))
+
+
+def load_for_genes_kernel(after_ref, *refs):
+    del after_ref
+    sources, places, (load_cat, l_ref, sems) = refs[:5], refs[5:9], refs[9:]
+    copies = start_loads(sources, (*places, l_ref), sems)
+    copies[0].wait()
+    load_cat[...] = gene_operand(l_ref[...])
+    wait_all(copies[1:])
+
+
+def load_for_cells_kernel(after_ref, off_ref, *refs):
+    del after_ref
+    sources, places, (cell_cat, f_ref, sems) = refs[:5], refs[5:9], refs[9:]
+    copies = start_loads(sources, (*places, f_ref), sems)
+    copies[0].wait()
+    set_cell_cat(f_ref[...], off_ref[...], cell_cat)
+    wait_all(copies[1:])
 
 
 class Stream:
@@ -197,36 +251,35 @@
             self.done += 1
 
 
-def counts_by_cells(counts_hbm, held, sems):
+def first_kernel(
+    after_ref, tile_ref, load_cat, load_hl, cell_cat, front, counts_hbm, ga_ref, gb_ref, narrow_hbm,
+    held, narrow, sems, out_sems, *, genes_total
+):
+    del after_ref
+    begin = front.shape[0]
     copies = []
-    for b in range(held.shape[0] // COPY_CELLS):
-        at = pl.ds(b * COPY_CELLS, COPY_CELLS)
-        copies.append(pltpu.make_async_copy(counts_hbm.at[at], held.at[at], sems.at[b]))
-    return Stream(copies)
-
-
-def first_kernel(
-    tile_ref, donors_hbm, table_hbm, f_hbm, l_hbm, lv_hbm, counts_hbm, ga_ref, gb_ref, off_ref, narrow_hbm,
-    held, narrow, donors_ref, table_ref, f_ref, l_ref, lv_ref, load_cat, load_hl, sems, small, out_sems, *, genes_total
-):
-    del tile_ref
-    pairs = [(l_hbm, l_ref), (f_hbm, f_ref), (donors_hbm, donors_ref), (table_hbm, table_ref), (lv_hbm, lv_ref)]
-    copies = start_all([pltpu.make_async_copy(src, dst, small.at[i]) for i, (src, dst) in enumerate(pairs)])
-    stream = counts_by_cells(counts_hbm, held, sems)
-    wait_all(copies)
-    off_ref[...] = offsets_of(donors_ref[...], table_ref[...])
-    set_loads(l_ref[...], load_cat, load_hl)
-    ga_ref[ga_ref.shape[0] - SUB :, :] = square_tile(inverse_root(lv_ref[...]))
+    for r in range(0, held.shape[0], COPY_CELLS):
+        copies.append(
+            pltpu.make_async_copy(
+                counts_hbm.at[pl.ds(begin + r, COPY_CELLS)], held.at[pl.ds(r, COPY_CELLS)], sems.at[r // COPY_CELLS]
+            )
+        )
+    stream = Stream(copies)
+    ga_ref[ga_ref.shape[0] - SUB :, :] = tile_ref[...]
     kept = []
 
-    def ready(b):
-        stream.need((b + 1) * CELL_BLOCK // COPY_CELLS)
-        at = pl.ds(b * CELL_BLOCK, CELL_BLOCK)
-        narrow[b] = held[at, :].astype(bf16)
-        kept.append(pltpu.make_async_copy(narrow.at[b], narrow_hbm.at[at], out_sems.at[b]))
-        kept[-1].start()
-
-    cell_pass(f_ref, off_ref, load_cat, load_hl, held, ready, (ga_ref, gb_ref), genes_total)
+    def block(b):
+        place = front if b == 0 else held.at[pl.ds(b * CELL_BLOCK - begin, CELL_BLOCK)]
+        if len(kept) == b:
+            stream.need(max(0, (b + 1) * CELL_BLOCK - begin) // COPY_CELLS)
+            narrow[b] = place[...].astype(NARROW)
+            kept.append(
+                pltpu.make_async_copy(narrow.at[b], narrow_hbm.at[pl.ds(b * CELL_BLOCK, CELL_BLOCK)], out_sems.at[b])
+            )
+            kept[-1].start()
+        return place
+
+    cell_pass(cell_cat, load_cat, load_hl, block, (ga_ref, gb_ref), genes_total, FIRST_LOW_CHUNKS)
     wait_all(kept)
 
 
@@ -235,7 +288,7 @@
 
 
 def gene_kernel(
-    tile_ref, ga_ref, gb_ref, off_ref, counts, f_ref, fm_ref, fv_ref, l_ref,
+    tile_ref, ga_ref, gb_ref, off_ref, counts, f_ref, fm_ref, fv_ref, load_cat,
     la_ref, lb_ref, nf_hbm, nm_hbm, nv_hbm, moved, cell_cat, cell_hl, sems, *, cells_total
 ):
     held = f_ref, fm_ref, fv_ref
@@ -250,7 +303,7 @@
     for h in range(2):
         la_ref[h, rows - SUB : rows, :] = tile
     set_cells(moved[0], off_ref[...], cell_cat, cell_hl)
-    gene_pass(l_ref, cell_cat, cell_hl, counts, (la_ref, lb_ref), cells_total)
+    gene_pass(load_cat, cell_cat, cell_hl, counts, (la_ref, lb_ref), cells_total)
     wait_all(copies)
 
 
@@ -265,7 +318,7 @@
 
 
 def cell_kernel(
-    tile_ref, la_ref, lb_ref, off_ref, counts, l_ref, lm_ref, lv_ref, f_ref,
+    tile_ref, la_ref, lb_ref, counts, l_ref, lm_ref, lv_ref, cell_cat,
     ga_ref, gb_ref, nl_hbm, nm_hbm, nv_hbm, moved, load_cat, load_hl, sems, *, genes_total
 ):
     held = l_ref, lm_ref, lv_ref
@@ -276,7 +329,8 @@
     copies = start_all(out_copies(moved, (nl_hbm, nm_hbm, nv_hbm), sems))
     ga_ref[ga_ref.shape[0] - SUB :, :] = tile
     set_loads(moved[0], load_cat, load_hl)
-    cell_pass(f_ref, off_ref, load_cat, load_hl, counts, None, (ga_ref, gb_ref), genes_total)
+    block = lambda b: counts.at[pl.ds(b * CELL_BLOCK, CELL_BLOCK)]
+    cell_pass(cell_cat, load_cat, load_hl, block, (ga_ref, gb_ref), genes_total, 0)
     wait_all(copies)
 
 
@@ -384,7 +438,7 @@
             out_specs=[vmem] * len(outs) + [hbm] * len(out_hbm),
             out_shape=[pltpu.VMEM(o.shape, o.dtype) for o in outs] + [pltpu.HBM(o.shape, o.dtype) for o in out_hbm],
             scratch_shapes=list(scratch),
-            compiler_params=pltpu.CompilerParams(vmem_limit_bytes=(limit << 20) if work else 4 << 20),
+            compiler_params=pltpu.CompilerParams(vmem_limit_bytes=(limit << 20) if work else 6 << 20),
             cost_estimate=pl.CostEstimate(
                 flops=int(flops * work), bytes_accessed=4 * width * cells + moves, transcendentals=int(cells * genes * work)
             ),
@@ -393,30 +447,51 @@
             *(pltpu.with_memory_space_constraint(x, pltpu.HBM) for x in in_hbm),
         )
 
+    def shapes(arrays):
+        return [jax.ShapeDtypeStruct(a.shape, a.dtype) for a in arrays]
+
+    def bring_for_genes(after, *arrays):
+        return call(
+            load_for_genes_kernel, "load_for_genes", [after], list(arrays),
+            shapes(arrays[:4]) + [jax.ShapeDtypeStruct((DEPTH, genes), bf16)], [],
+            [in_vmem(width, genes), dma(8)], 0, cells * genes + 16 * width * cells,
+        )
+
+    def bring_for_cells(after, off, *arrays):
+        return call(
+            load_for_cells_kernel, "load_for_cells", [after, off], list(arrays),
+            shapes(arrays[:4]) + [jax.ShapeDtypeStruct((cells, DEPTH), bf16)], [],
+            [in_vmem(width, cells), dma(8)], 0, cells * genes + 16 * width * cells,
+        )
+
     def bring(after, *arrays):
-        size = sum(a.size * a.dtype.itemsize for a in arrays)
         return call(
-            load_kernel, "load", [after], list(arrays), [jax.ShapeDtypeStruct(a.shape, a.dtype) for a in arrays], [],
-            [dma(len(arrays) + 3)], 0, size,
-        )
-
-    (fac_tile,) = call(
-        total_kernel, "factor_scale_total", [], [factor_var], [like(SUB, LANES)], [],
-        [in_vmem(width, cells), pltpu.SemaphoreType.DMA], 0,
+            load_kernel, "load", [after], list(arrays), shapes(arrays), [], [dma(len(arrays) + 3)], 0, 12 * width * cells
+        )
+
+    donor_row, table_row = donors.reshape(1, cells), offset_table.reshape(1, -1)
+    operands = [jax.ShapeDtypeStruct((DEPTH, genes), bf16), jax.ShapeDtypeStruct((2 * width, genes), bf16)]
+    fac_tile, load_tile, off, *ready = call(
+        front_kernel, "front", [],
+        [factor_var, loading_var, loadings, donor_row, table_row, factors, counts],
+        [like(SUB, LANES), like(SUB, LANES), like(1, cells), *operands, jax.ShapeDtypeStruct((cells, DEPTH), bf16), like(CELL_BLOCK, genes)], [],
+        [
+            in_vmem(width, cells), in_vmem(width, genes), in_vmem(width, genes),
+            pltpu.VMEM((1, cells), jnp.int32), pltpu.VMEM((1, table_row.shape[1]), jnp.int32),
+            in_vmem(width, cells), dma(10),
+        ],
+        0, 4 * CELL_BLOCK * genes,
     )
     fac_tile = fac_tile + other_core(fac_tile)
-    donor_row, table_row = donors.reshape(1, cells), offset_table.reshape(1, -1)
-    grad_a, grad_b, off, narrow = call(
-        first_kernel, "cell_pass_first", [fac_tile], [donor_row, table_row, factors, loadings, loading_var, counts],
-        cell_grad + [like(1, cells)], [jax.ShapeDtypeStruct((cells, genes), bf16)],
+    blocks = cells // CELL_BLOCK
+    rest = cells - CELL_BLOCK
+    grad_a, grad_b, narrow = call(
+        first_kernel, "cell_pass_first", [fac_tile, load_tile, *ready], [counts],
+        cell_grad, [jax.ShapeDtypeStruct((cells, genes), NARROW)],
         [
-            in_vmem(cells, genes), operand(cells // CELL_BLOCK, CELL_BLOCK, genes),
-            pltpu.VMEM((1, cells), jnp.int32), pltpu.VMEM((1, table_row.shape[1]), jnp.int32),
-            in_vmem(width, cells), in_vmem(width, genes), in_vmem(width, genes),
-            operand(DEPTH, genes), operand(2 * width, genes), dma(cells // COPY_CELLS), dma(5),
-            dma(cells // CELL_BLOCK),
+            in_vmem(rest, genes), pltpu.VMEM((blocks, CELL_BLOCK, genes), NARROW), dma(rest // COPY_CELLS), dma(blocks),
         ],
-        1, limit=36, genes_total=genes_total,
+        1.5, limit=32, genes_total=genes_total,
     )
 
     def loading_gradient(fac_tile, grad_a, grad_b, held):
@@ -428,18 +503,18 @@
 
     def factor_gradient(load_tile, grad_l, grad_m, held):
         first, second, *new = call(
-            cell_kernel, "cell_pass", [load_tile, grad_l, grad_m, off, *held], [], cell_grad, three_l,
+            cell_kernel, "cell_pass", [load_tile, grad_l, grad_m, *held], [], cell_grad, three_l,
             [in_vmem(3, width, genes), operand(DEPTH, genes), operand(2 * width, genes), dma(3)], 1, genes_total=genes_total,
         )
         return first, second, new
 
     fac_tile = fac_tile + exchange(fac_tile, along_cells(0))
     grad_a, fac_tile = lax.optimization_barrier((grad_a, fac_tile))
-    came_a, came_b = exchange(grad_a, along_genes(0)), exchange(grad_b, along_genes(1))
+    came_a, came_b = exchange(grad_a, along_genes(0)), exchange(grad_b, along_genes(0))
     fac_tile = fac_tile + exchange(fac_tile, along_cells(1))
     fac_tile, grad_a, grad_b = lax.optimization_barrier((fac_tile, grad_a + came_a, grad_b + came_b))
-    came_a, came_b = exchange(grad_a, along_genes(1)), exchange(grad_b, along_genes(0))
-    held = bring(grad_a, narrow, factors, factor_mean, factor_var, loadings)
+    came_a, came_b = exchange(grad_a, along_genes(1)), exchange(grad_b, along_genes(1))
+    held = bring_for_genes(grad_a, narrow, factors, factor_mean, factor_var, loadings)
     for step in (2, 3):
         fac_tile = fac_tile + exchange(fac_tile, along_cells(step))
     grad_a, grad_b = grad_a + came_a, grad_b + came_b
@@ -447,12 +522,12 @@
     grad_l, grad_m, f = loading_gradient(fac_tile, grad_a, grad_b, held)
     grad_l, grad_m, seen = sum_over_cells(grad_l, grad_m)
     fac_tile = grad_l[0, gene_rows:]
-    held = bring(seen[4], narrow, loadings, loading_mean, loading_var, f[0])
+    held = bring_for_cells(seen[4], off, narrow, loadings, loading_mean, loading_var, f[0])
     grad_a, grad_b, l = factor_gradient(load_tile, grad_l, grad_m, held)
-    came_a, came_b = exchange(grad_a, along_genes(0)), exchange(grad_b, along_genes(1))
+    came_a, came_b = exchange(grad_a, along_genes(0)), exchange(grad_b, along_genes(0))
     grad_a, grad_b = grad_a + came_a, grad_b + came_b
-    came_a, came_b = exchange(grad_a, along_genes(1)), exchange(grad_b, along_genes(0))
-    held = bring(grad_a, narrow, *f, l[0])
+    came_a, came_b = exchange(grad_a, along_genes(1)), exchange(grad_b, along_genes(1))
+    held = bring_for_genes(grad_a, narrow, *f, l[0])
     grad_a, grad_b = grad_a + came_a, grad_b + came_b
     load_tile = grad_a[cell_rows:]
     grad_l, grad_m, f = loading_gradient(fac_tile, grad_a, grad_b, held)

time: 141 us -> 134 us (0.950)
  Pallas kernels: 46.6 us -> 40.6 us
  waiting for transfers between devices: 44.9 us -> 42.2 us
  starting transfers between devices: 47 us -> 49 us
    pallas_call x10, Pallas kernels: 46.6 us -> 40.6 us  [call(): pl.pallas_call(functools.partial(kernel, **static), name=name, in_specs=[...]
    ppermute x37, waiting for transfers between devices: 44.9 us -> 42.2 us  [exchange(): return lax.ppermute(value, ('cell', 'gene'), pairs)]
    ppermute x37, starting transfers between devices: 47 us -> 49 us  [exchange(): return lax.ppermute(value, ('cell', 'gene'), pairs)]
  transfers between devices with their start and end apart: 37 -> 37, of which waited for: 20 -> 24; matrix products, arithmetic and copies ran while one was open for 0% -> 0% of each run, Pallas kernels for 19% -> 14%
where the time goes in v3:
time: 134 us
  starting transfers between devices  49 us (37%)
  waiting for transfers between devices  42.2 us (31%)
  Pallas kernels  40.6 us (30%)
    ppermute x37, starting transfers between devices, exchange(): return lax.ppermute(value, ('cell', 'gene'), pairs)  49 us
    ppermute x37, waiting for transfers between devices, exchange(): return lax.ppermute(value, ('cell', 'gene'), pairs)  42.2 us
    pallas_call x10, Pallas kernels, call(): pl.pallas_call(functools.partial(kernel, **static), name=name, in_specs=[...  40.6 us
  transfers between devices with their start and end apart: 37, of which 24 were waited for; matrix products, arithmetic and copies ran while one was open for 0% of the time, Pallas kernels for 14%

profile of v3, /device:TPU:1, one launch (start us, length us, event | category | flops | bytes accessed | tf_op | source)
XLA Modules:
  0.0 134.0 jit_solution(1232428424275360508)
XLA Ops:
  0.6 2.9 %front.1 = (f32[8,128]{1,0:T(8,128)S(1)}, f32[8,128]{1,0:T(8,128)S(1)}, f32[1,2048]{1,0:T(1,128)S(1)}, bf16[256,2048]{1,0:T(8,128)(2,1)S(1)}, bf16[128,2048]{1,0...) custom-call(f32[64,2048]{1,0:T(8,128)} %refs_3_.2, f32[64,2048]{1,0:T(8,128)} %refs_3_.3, ...), custom_call_target="tpu_custom_call" | custom-call | bytes 4718592 | tf_op jit(solution)/shard_map/front/pallas_call | solution.py:434
  7.3 9.3 %cell_pass_first.1 = (f32[520,128]{1,0:T(8,128)S(1)}, f32[512,128]{1,0:T(8,128)S(1)}, f8e4m3fn[2048,2048]{1,0:T(32,128)(4,1)}) custom-call(f32[8,128]{1,0:T(8,128)S(1)} %add.126.after_ref, f32[8,128]{1,0:T(8,128)S(1)} %get-tuple-element.58.tile_ref, bf16[256,2048]{1,0:T(8,128)(2,1)S(1)} %get-tuple-element.59.load_cat, ...), custom_call_target="tpu_custom_call" | custom-call | flops 6442450944 | bytes 524288 | tf_op jit(solution)/shard_map/cell_pass_first/pallas_call | solution.py:434
  16.6 3.8 %collective-permute-start.3 = (f32[520,128]{1,0:T(8,128)S(1)}, f32[520,128]{1,0:T(8,128)S(1)}, u32[]{:S(2)}, u32[]{:S(2)}) collective-permute-start(f32[520,128]{1,0:T(8,128)S(1)} %get-tuple-element.65), channel_id=1, source_target_pairs={{0,1},{1,0},{2,3},{3,2},{4,7},{5,6},{6,5},{7,4},{8,9},{9,8},{10,11... | collective-permute-start | bytes 798728 | tf_op jit(solution)/shard_map/ppermute | solution.py:354
  24.2 2.8 %collective-permute-done.4 = f32[512,128]{1,0:T(8,128)S(1)} collective-permute-done((f32[512,128]{1,0:T(8,128)S(1)}, f32[512,128]{1,0:T(8,128)S(1)}, u32[]{:S(2)}, u32[]{:S(2)}) %collective-permute-start.4) | collective-permute-done | bytes 262176 | tf_op jit(solution)/shard_map/ppermute | solution.py:354
  31.2 2.8 %collective-permute-start.6 = (f32[8,128]{1,0:T(8,128)S(1)}, f32[8,128]{1,0:T(8,128)S(1)}, u32[]{:S(2)}, u32[]{:S(2)}) collective-permute-start(f32[8,128]{1,0:T(8,128)S(1)} %add.131), channel_id=1, source_target_pairs={{0,24},{1,25},{2,26},{3,27},{4,100},{5,101},{6,102},{7,103},{8,16}... | collective-permute-start | bytes 12296 | tf_op jit(solution)/shard_map/ppermute | solution.py:354
  33.9 2.9 %load_for_genes.2 = (f8e4m3fn[2048,2048]{1,0:T(32,128)(4,1)S(1)}, f32[64,2048]{1,0:T(8,128)S(1)}, f32[64,2048]{1,0:T(8,128)S(1)}, f32[64,2048]{1,0:T(8,128)S(1)}, bf16[256,2048]{1,0:T(8,128)(2,1)S(1)}) custom-call(f32[520,128]{1,0:T(8,128)S(1)} %add.129.after_ref, f8e4m3fn[2048,2048]{1,0:T(32,128)(4,1)} %get-tuple-element.71.refs_0_, f32[64,2048]{1,0:T(8,128)} %refs_1_.2, ...), custom_call_target="tpu_custom_call" | custom-call | bytes 6815744 | tf_op jit(solution)/shard_map/load_for_genes/pallas_call | solution.py:434
  37.0 5.5 %gene_pass.2 = (f32[2,264,128]{2,1,0:T(8,128)S(1)}, f32[2,256,128]{2,1,0:T(8,128)S(1)}, f32[64,2048]{1,0:T(8,128)}, f32[64,2048]{1,0:T(8,128)}, f32[64,2048]{1,0:T(8,128)}) custom-call(f32[8,128]{1,0:T(8,128)S(1)} %add.132.tile_ref, f32[520,128]{1,0:T(8,128)S(1)} %add.133.ga_ref, f32[512,128]{1,0:T(8,128)S(1)} %add.134.gb_ref, ...), custom_call_target="tpu_custom_call" | custom-call | flops 4294967296 | bytes 524288 | tf_op jit(solution)/shard_map/gene_pass/pallas_call | solution.py:434
  42.5 3.5 %collective-permute-start.15 = (f32[256,128]{1,0:T(8,128)S(1)}, f32[256,128]{1,0:T(8,128)S(1)}, u32[]{:S(2)}, u32[]{:S(2)}) collective-permute-start(f32[256,128]{1,0:T(8,128)S(1)} %dynamic-slice_bitcast_fusion.3), channel_id=1, source_target_pairs={{0,4},{1,5},{2,6},{3,7},{4,0},{5,1},{6,2},{7,3},{8,12},{9,13},{10,... | collective-permute-start | bytes 393224 | tf_op jit(solution)/shard_map/ppermute | solution.py:354
  48.8 3.6 %collective-permute-done.16 = f32[256,128]{1,0:T(8,128)S(1)} collective-permute-done((f32[256,128]{1,0:T(8,128)S(1)}, f32[256,128]{1,0:T(8,128)S(1)}, u32[]{:S(2)}, u32[]{:S(2)}) %collective-permute-start.16) | collective-permute-done | bytes 131104 | tf_op jit(solution)/shard_map/ppermute | solution.py:354
  58.7 3.0 %collective-permute-done.18 = f32[256,128]{1,0:T(8,128)S(1)} collective-permute-done((f32[256,128]{1,0:T(8,128)S(1)}, f32[256,128]{1,0:T(8,128)S(1)}, u32[]{:S(2)}, u32[]{:S(2)}) %collective-permute-start.18) | collective-permute-done | bytes 131104 | tf_op jit(solution)/shard_map/ppermute | solution.py:354
  65.9 4.2 %collective-permute-start.20 = (f32[256,128]{1,0:T(8,128)S(1)}, f32[256,128]{1,0:T(8,128)S(1)}, u32[]{:S(2)}, u32[]{:S(2)}) collective-permute-start(f32[256,128]{1,0:T(8,128)S(1)} %add.146), channel_id=1, source_target_pairs={{0,4},{1,5},{2,6},{3,7},{4,0},{5,1},{6,2},{7,3},{8,12},{9,13},{10,... | collective-permute-start | bytes 393224 | tf_op jit(solution)/shard_map/ppermute | solution.py:354
  70.2 2.9 %load_for_cells.1 = (f8e4m3fn[2048,2048]{1,0:T(32,128)(4,1)S(1)}, f32[64,2048]{1,0:T(8,128)S(1)}, f32[64,2048]{1,0:T(8,128)S(1)}, f32[64,2048]{1,0:T(8,128)S(1)}, bf16[2048,256]{1,0:T(8,128)(2,1)S(1)}) custom-call(f32[264,128]{1,0:T(8,128)S(1)} %add.140.after_ref, f32[1,2048]{1,0:T(1,128)S(1)} %get-tuple-element.70.off_ref, ...), custom_call_target="tpu_custom_call" | custom-call | bytes 6815744 | tf_op jit(solution)/shard_map/load_for_cells/pallas_call | solution.py:434
  74.8 5.8 %cell_pass.1 = (f32[520,128]{1,0:T(8,128)S(1)}, f32[512,128]{1,0:T(8,128)S(1)}, f32[64,2048]{1,0:T(8,128)}, f32[64,2048]{1,0:T(8,128)}, f32[64,2048]{1,0:T(8,128)}) custom-call(f32[8,128]{1,0:T(8,128)S(1)} %slice.13.tile_ref, f32[2,264,128]{2,1,0:T(8,128)S(1)} %pad_maximum_fusion.la_ref, f32[2,256,128]{2,1,0:T(8,128)S(1)} %pad_maximum_fusion.2.lb_ref, ...), custom_call_target="tpu_custom_call" | custom-call | flops 4294967296 | bytes 524288 | tf_op jit(solution)/shard_map/cell_pass/pallas_call | solution.py:434
  80.6 2.9 %collective-permute-start.21 = (f32[520,128]{1,0:T(8,128)S(1)}, f32[520,128]{1,0:T(8,128)S(1)}, u32[]{:S(2)}, u32[]{:S(2)}) collective-permute-start(f32[520,128]{1,0:T(8,128)S(1)} %get-tuple-element.85), channel_id=1, source_target_pairs={{0,1},{1,0},{2,3},{3,2},{4,7},{5,6},{6,5},{7,4},{8,9},{9,8},{10,11... | collective-permute-start | bytes 798728 | tf_op jit(solution)/shard_map/ppermute | solution.py:354
  83.6 3.7 %collective-permute-done.21 = f32[520,128]{1,0:T(8,128)S(1)} collective-permute-done((f32[520,128]{1,0:T(8,128)S(1)}, f32[520,128]{1,0:T(8,128)S(1)}, u32[]{:S(2)}, u32[]{:S(2)}) %collective-permute-start.21) | collective-permute-done | bytes 266272 | tf_op jit(solution)/shard_map/ppermute | solution.py:354
  87.5 2.7 %collective-permute-done.23 = f32[512,128]{1,0:T(8,128)S(1)} collective-permute-done((f32[512,128]{1,0:T(8,128)S(1)}, f32[512,128]{1,0:T(8,128)S(1)}, u32[]{:S(2)}, u32[]{:S(2)}) %collective-permute-start.23) | collective-permute-done | bytes 262176 | tf_op jit(solution)/shard_map/ppermute | solution.py:354
  90.3 2.9 %load_for_genes.3 = (f8e4m3fn[2048,2048]{1,0:T(32,128)(4,1)S(1)}, f32[64,2048]{1,0:T(8,128)S(1)}, f32[64,2048]{1,0:T(8,128)S(1)}, f32[64,2048]{1,0:T(8,128)S(1)}, bf16[256,2048]{1,0:T(8,128)(2,1)S(1)}) custom-call(f32[520,128]{1,0:T(8,128)S(1)} %add.147.after_ref, f8e4m3fn[2048,2048]{1,0:T(32,128)(4,1)} %get-tuple-element.71.refs_0_, ...), custom_call_target="tpu_custom_call" | custom-call | bytes 6815744 | tf_op jit(solution)/shard_map/load_for_genes/pallas_call | solution.py:434
  93.2 2.6 %collective-permute-done.24 = f32[512,128]{1,0:T(8,128)S(1)} collective-permute-done((f32[512,128]{1,0:T(8,128)S(1)}, f32[512,128]{1,0:T(8,128)S(1)}, u32[]{:S(2)}, u32[]{:S(2)}) %collective-permute-start.24) | collective-permute-done | bytes 262176 | tf_op jit(solution)/shard_map/ppermute | solution.py:354
  95.9 5.5 %gene_pass.3 = (f32[2,264,128]{2,1,0:T(8,128)S(1)}, f32[2,256,128]{2,1,0:T(8,128)S(1)}, f32[64,2048]{1,0:T(8,128)}, f32[64,2048]{1,0:T(8,128)}, f32[64,2048]{1,0:T(8,128)}) custom-call(f32[8,128]{1,0:T(8,128)S(1)} %slice_bitcast_fusion.tile_ref, f32[520,128]{1,0:T(8,128)S(1)} %add.148.ga_ref, f32[512,128]{1,0:T(8,128)S(1)} %add.150.gb_ref, ...), custom_call_target="tpu_custom_call" | custom-call | flops 4294967296 | bytes 524288 | tf_op jit(solution)/shard_map/gene_pass/pallas_call | solution.py:434
  101.4 2.5 %collective-permute-start.31 = (f32[256,128]{1,0:T(8,128)S(1)}, f32[256,128]{1,0:T(8,128)S(1)}, u32[]{:S(2)}, u32[]{:S(2)}) collective-permute-start(f32[256,128]{1,0:T(8,128)S(1)} %dynamic-slice_bitcast_fusion.2), channel_id=1, source_target_pairs={{0,4},{1,5},{2,6},{3,7},{4,0},{5,1},{6,2},{7,3},{8,12},{9,13},{10,... | collective-permute-start | bytes 393224 | tf_op jit(solution)/shard_map/ppermute | solution.py:354
  106.6 3.6 %collective-permute-done.32 = f32[256,128]{1,0:T(8,128)S(1)} collective-permute-done((f32[256,128]{1,0:T(8,128)S(1)}, f32[256,128]{1,0:T(8,128)S(1)}, u32[]{:S(2)}, u32[]{:S(2)}) %collective-permute-start.32) | collective-permute-done | bytes 131104 | tf_op jit(solution)/shard_map/ppermute | solution.py:354
  116.3 3.5 %collective-permute-done.34 = f32[256,128]{1,0:T(8,128)S(1)} collective-permute-done((f32[256,128]{1,0:T(8,128)S(1)}, f32[256,128]{1,0:T(8,128)S(1)}, u32[]{:S(2)}, u32[]{:S(2)}) %collective-permute-start.34) | collective-permute-done | bytes 131104 | tf_op jit(solution)/shard_map/ppermute | solution.py:354
  120.2 2.2 %collective-permute-start.29 = (f32[264,128]{1,0:T(8,128)S(1)}, f32[264,128]{1,0:T(8,128)S(1)}, u32[]{:S(2)}, u32[]{:S(2)}) collective-permute-start(f32[264,128]{1,0:T(8,128)S(1)} %add.154), channel_id=1, source_target_pairs={{0,24},{1,25},{2,26},{3,27},{4,100},{5,101},{6,102},{7,103},{8,16}... | collective-permute-start | bytes 405512 | tf_op jit(solution)/shard_map/ppermute | solution.py:354
  124.0 4.0 %collective-permute-start.36 = (f32[256,128]{1,0:T(8,128)S(1)}, f32[256,128]{1,0:T(8,128)S(1)}, u32[]{:S(2)}, u32[]{:S(2)}) collective-permute-start(f32[256,128]{1,0:T(8,128)S(1)} %add.160), channel_id=1, source_target_pairs={{0,4},{1,5},{2,6},{3,7},{4,0},{5,1},{6,2},{7,3},{8,12},{9,13},{10,... | collective-permute-start | bytes 393224 | tf_op jit(solution)/shard_map/ppermute | solution.py:354
  (108 shorter events, 43.6 us)
Async XLA Ops:
  5.9 10.7 %collective-permute-start.1 = (f32[8,128]{1,0:T(8,128)S(1)}, f32[8,128]{1,0:T(8,128)S(1)}, u32[]{:S(2)}, u32[]{:S(2)}) collective-permute-start(f32[8,128]{1,0:T(8,128)S(1)} %add.126.after_ref), channel_id=1, source_target_pairs={{0,32},{1,33},{2,34},{3,35},{4,12},{5,13},{6,14},{7,15},{8,40},{9,... | collective-permute-start | bytes 12296 | tf_op jit(solution)/shard_map/ppermute | solution.py:354
  16.6 10.5 %collective-permute-start.3 = (f32[520,128]{1,0:T(8,128)S(1)}, f32[520,128]{1,0:T(8,128)S(1)}, u32[]{:S(2)}, u32[]{:S(2)}) collective-permute-start(f32[520,128]{1,0:T(8,128)S(1)} %get-tuple-element.65), channel_id=1, source_target_pairs={{0,1},{1,0},{2,3},{3,2},{4,7},{5,6},{6,5},{7,4},{8,9},{9,8},{10,11... | collective-permute-start | bytes 798728 | tf_op jit(solution)/shard_map/ppermute | solution.py:354
  20.4 6.6 %collective-permute-start.4 = (f32[512,128]{1,0:T(8,128)S(1)}, f32[512,128]{1,0:T(8,128)S(1)}, u32[]{:S(2)}, u32[]{:S(2)}) collective-permute-start(f32[512,128]{1,0:T(8,128)S(1)} %get-tuple-element.66), channel_id=1, source_target_pairs={{0,1},{1,0},{2,3},{3,2},{4,7},{5,6},{6,5},{7,4},{8,9},{9,8},{10,11... | collective-permute-start | bytes 786440 | tf_op jit(solution)/shard_map/ppermute | solution.py:354
  27.1 9.8 %collective-permute-start.7 = (f32[520,128]{1,0:T(8,128)S(1)}, f32[520,128]{1,0:T(8,128)S(1)}, u32[]{:S(2)}, u32[]{:S(2)}) collective-permute-start(f32[520,128]{1,0:T(8,128)S(1)} %add.129.after_ref), channel_id=1, source_target_pairs={{0,3},{1,2},{2,1},{3,0},{4,5},{5,4},{6,7},{7,6},{8,11},{9,10},{10,... | collective-permute-start | bytes 798728 | tf_op jit(solution)/shard_map/ppermute | solution.py:354
  27.2 9.6 %collective-permute-start.8 = (f32[512,128]{1,0:T(8,128)S(1)}, f32[512,128]{1,0:T(8,128)S(1)}, u32[]{:S(2)}, u32[]{:S(2)}) collective-permute-start(f32[512,128]{1,0:T(8,128)S(1)} %add.130), channel_id=1, source_target_pairs={{0,3},{1,2},{2,1},{3,0},{4,5},{5,4},{6,7},{7,6},{8,11},{9,10},{10,... | collective-permute-start | bytes 786440 | tf_op jit(solution)/shard_map/ppermute | solution.py:354
  31.2 5.7 %collective-permute-start.6 = (f32[8,128]{1,0:T(8,128)S(1)}, f32[8,128]{1,0:T(8,128)S(1)}, u32[]{:S(2)}, u32[]{:S(2)}) collective-permute-start(f32[8,128]{1,0:T(8,128)S(1)} %add.131), channel_id=1, source_target_pairs={{0,24},{1,25},{2,26},{3,27},{4,100},{5,101},{6,102},{7,103},{8,16}... | collective-permute-start | bytes 12296 | tf_op jit(solution)/shard_map/ppermute | solution.py:354
  42.5 4.5 %collective-permute-start.15 = (f32[256,128]{1,0:T(8,128)S(1)}, f32[256,128]{1,0:T(8,128)S(1)}, u32[]{:S(2)}, u32[]{:S(2)}) collective-permute-start(f32[256,128]{1,0:T(8,128)S(1)} %dynamic-slice_bitcast_fusion.3), channel_id=1, source_target_pairs={{0,4},{1,5},{2,6},{3,7},{4,0},{5,1},{6,2},{7,3},{8,12},{9,13},{10,... | collective-permute-start | bytes 393224 | tf_op jit(solution)/shard_map/ppermute | solution.py:354
  47.0 5.4 %collective-permute-start.16 = (f32[256,128]{1,0:T(8,128)S(1)}, f32[256,128]{1,0:T(8,128)S(1)}, u32[]{:S(2)}, u32[]{:S(2)}) collective-permute-start(f32[256,128]{1,0:T(8,128)S(1)} %bitcast_add_fusion.3), channel_id=1, source_target_pairs={{0,96},{1,97},{2,98},{3,99},{4,28},{5,29},{6,30},{7,31},{8,104},{9... | collective-permute-start | bytes 393224 | tf_op jit(solution)/shard_map/ppermute | solution.py:354
  48.7 4.2 %collective-permute-start.10 = (f32[264,128]{1,0:T(8,128)S(1)}, f32[264,128]{1,0:T(8,128)S(1)}, u32[]{:S(2)}, u32[]{:S(2)}) collective-permute-start(f32[264,128]{1,0:T(8,128)S(1)} %bitcast_add_fusion.1), channel_id=1, source_target_pairs={{0,32},{1,33},{2,34},{3,35},{4,12},{5,13},{6,14},{7,15},{8,40},{9,... | collective-permute-start | bytes 405512 | tf_op jit(solution)/shard_map/ppermute | solution.py:354
  53.0 5.3 %collective-permute-start.11 = (f32[264,128]{1,0:T(8,128)S(1)}, f32[264,128]{1,0:T(8,128)S(1)}, u32[]{:S(2)}, u32[]{:S(2)}) collective-permute-start(f32[264,128]{1,0:T(8,128)S(1)} %add.138), channel_id=1, source_target_pairs={{0,96},{1,97},{2,98},{3,99},{4,28},{5,29},{6,30},{7,31},{8,104},{9... | collective-permute-start | bytes 405512 | tf_op jit(solution)/shard_map/ppermute | solution.py:354
  56.4 5.3 %collective-permute-start.18 = (f32[256,128]{1,0:T(8,128)S(1)}, f32[256,128]{1,0:T(8,128)S(1)}, u32[]{:S(2)}, u32[]{:S(2)}) collective-permute-start(f32[256,128]{1,0:T(8,128)S(1)} %add.144), channel_id=1, source_target_pairs={{0,24},{1,25},{2,26},{3,27},{4,100},{5,101},{6,102},{7,103},{8,16}... | collective-permute-start | bytes 393224 | tf_op jit(solution)/shard_map/ppermute | solution.py:354
  62.2 10.8 %collective-permute-start.13 = (f32[264,128]{1,0:T(8,128)S(1)}, f32[264,128]{1,0:T(8,128)S(1)}, u32[]{:S(2)}, u32[]{:S(2)}) collective-permute-start(f32[264,128]{1,0:T(8,128)S(1)} %add.140.after_ref), channel_id=1, source_target_pairs={{0,24},{1,25},{2,26},{3,27},{4,100},{5,101},{6,102},{7,103},{8,16}... | collective-permute-start | bytes 405512 | tf_op jit(solution)/shard_map/ppermute | solution.py:354
  65.9 7.5 %collective-permute-start.20 = (f32[256,128]{1,0:T(8,128)S(1)}, f32[256,128]{1,0:T(8,128)S(1)}, u32[]{:S(2)}, u32[]{:S(2)}) collective-permute-start(f32[256,128]{1,0:T(8,128)S(1)} %add.146), channel_id=1, source_target_pairs={{0,4},{1,5},{2,6},{3,7},{4,0},{5,1},{6,2},{7,3},{8,12},{9,13},{10,... | collective-permute-start | bytes 393224 | tf_op jit(solution)/shard_map/ppermute | solution.py:354
  80.6 6.7 %collective-permute-start.21 = (f32[520,128]{1,0:T(8,128)S(1)}, f32[520,128]{1,0:T(8,128)S(1)}, u32[]{:S(2)}, u32[]{:S(2)}) collective-permute-start(f32[520,128]{1,0:T(8,128)S(1)} %get-tuple-element.85), channel_id=1, source_target_pairs={{0,1},{1,0},{2,3},{3,2},{4,7},{5,6},{6,5},{7,4},{8,9},{9,8},{10,11... | collective-permute-start | bytes 798728 | tf_op jit(solution)/shard_map/ppermute | solution.py:354
  83.5 6.6 %collective-permute-start.23 = (f32[512,128]{1,0:T(8,128)S(1)}, f32[512,128]{1,0:T(8,128)S(1)}, u32[]{:S(2)}, u32[]{:S(2)}) collective-permute-start(f32[512,128]{1,0:T(8,128)S(1)} %get-tuple-element.86), channel_id=1, source_target_pairs={{0,1},{1,0},{2,3},{3,2},{4,7},{5,6},{6,5},{7,4},{8,9},{9,8},{10,11... | collective-permute-start | bytes 786440 | tf_op jit(solution)/shard_map/ppermute | solution.py:354
  87.4 8.5 %collective-permute-start.22 = (f32[520,128]{1,0:T(8,128)S(1)}, f32[520,128]{1,0:T(8,128)S(1)}, u32[]{:S(2)}, u32[]{:S(2)}) collective-permute-start(f32[520,128]{1,0:T(8,128)S(1)} %add.147.after_ref), channel_id=1, source_target_pairs={{0,3},{1,2},{2,1},{3,0},{4,5},{5,4},{6,7},{7,6},{8,11},{9,10},{10,... | collective-permute-start | bytes 798728 | tf_op jit(solution)/shard_map/ppermute | solution.py:354
  90.2 5.6 %collective-permute-start.24 = (f32[512,128]{1,0:T(8,128)S(1)}, f32[512,128]{1,0:T(8,128)S(1)}, u32[]{:S(2)}, u32[]{:S(2)}) collective-permute-start(f32[512,128]{1,0:T(8,128)S(1)} %add.149), channel_id=1, source_target_pairs={{0,3},{1,2},{2,1},{3,0},{4,5},{5,4},{6,7},{7,6},{8,11},{9,10},{10,... | collective-permute-start | bytes 786440 | tf_op jit(solution)/shard_map/ppermute | solution.py:354
  104.9 5.4 %collective-permute-start.32 = (f32[256,128]{1,0:T(8,128)S(1)}, f32[256,128]{1,0:T(8,128)S(1)}, u32[]{:S(2)}, u32[]{:S(2)}) collective-permute-start(f32[256,128]{1,0:T(8,128)S(1)} %bitcast_add_fusion.2), channel_id=1, source_target_pairs={{0,96},{1,97},{2,98},{3,99},{4,28},{5,29},{6,30},{7,31},{8,104},{9... | collective-permute-start | bytes 393224 | tf_op jit(solution)/shard_map/ppermute | solution.py:354
  106.5 4.2 %collective-permute-start.26 = (f32[264,128]{1,0:T(8,128)S(1)}, f32[264,128]{1,0:T(8,128)S(1)}, u32[]{:S(2)}, u32[]{:S(2)}) collective-permute-start(f32[264,128]{1,0:T(8,128)S(1)} %bitcast_add_fusion), channel_id=1, source_target_pairs={{0,32},{1,33},{2,34},{3,35},{4,12},{5,13},{6,14},{7,15},{8,40},{9,... | collective-permute-start | bytes 405512 | tf_op jit(solution)/shard_map/ppermute | solution.py:354
  110.8 5.4 %collective-permute-start.27 = (f32[264,128]{1,0:T(8,128)S(1)}, f32[264,128]{1,0:T(8,128)S(1)}, u32[]{:S(2)}, u32[]{:S(2)}) collective-permute-start(f32[264,128]{1,0:T(8,128)S(1)} %add.152.after_ref), channel_id=1, source_target_pairs={{0,96},{1,97},{2,98},{3,99},{4,28},{5,29},{6,30},{7,31},{8,104},{9... | collective-permute-start | bytes 405512 | tf_op jit(solution)/shard_map/ppermute | solution.py:354
  114.2 5.6 %collective-permute-start.34 = (f32[256,128]{1,0:T(8,128)S(1)}, f32[256,128]{1,0:T(8,128)S(1)}, u32[]{:S(2)}, u32[]{:S(2)}) collective-permute-start(f32[256,128]{1,0:T(8,128)S(1)} %add.158), channel_id=1, source_target_pairs={{0,24},{1,25},{2,26},{3,27},{4,100},{5,101},{6,102},{7,103},{8,16}... | collective-permute-start | bytes 393224 | tf_op jit(solution)/shard_map/ppermute | solution.py:354
  119.8 4.2 %collective-permute-start.35 = (f32[256,128]{1,0:T(8,128)S(1)}, f32[256,128]{1,0:T(8,128)S(1)}, u32[]{:S(2)}, u32[]{:S(2)}) collective-permute-start(f32[256,128]{1,0:T(8,128)S(1)} %add.159), channel_id=1, source_target_pairs={{0,8},{1,9},{2,10},{3,11},{4,36},{5,37},{6,38},{7,39},{8,0},{9,1},... | collective-permute-start | bytes 393224 | tf_op jit(solution)/shard_map/ppermute | solution.py:354
  120.2 9.2 %collective-permute-start.29 = (f32[264,128]{1,0:T(8,128)S(1)}, f32[264,128]{1,0:T(8,128)S(1)}, u32[]{:S(2)}, u32[]{:S(2)}) collective-permute-start(f32[264,128]{1,0:T(8,128)S(1)} %add.154), channel_id=1, source_target_pairs={{0,24},{1,25},{2,26},{3,27},{4,100},{5,101},{6,102},{7,103},{8,16}... | collective-permute-start | bytes 405512 | tf_op jit(solution)/shard_map/ppermute | solution.py:354
  124.0 7.1 %collective-permute-start.36 = (f32[256,128]{1,0:T(8,128)S(1)}, f32[256,128]{1,0:T(8,128)S(1)}, u32[]{:S(2)}, u32[]{:S(2)}) collective-permute-start(f32[256,128]{1,0:T(8,128)S(1)} %add.160), channel_id=1, source_target_pairs={{0,4},{1,5},{2,6},{3,7},{4,0},{5,1},{6,2},{7,3},{8,12},{9,13},{10,... | collective-permute-start | bytes 393224 | tf_op jit(solution)/shard_map/ppermute | solution.py:354
  (13 other events, 41.4 us)

commit v4 on v3

--- a/solution.py
+++ b/solution.py
@@ -511,12 +511,12 @@
     fac_tile = fac_tile + exchange(fac_tile, along_cells(0))
     grad_a, fac_tile = lax.optimization_barrier((grad_a, fac_tile))
     came_a, came_b = exchange(grad_a, along_genes(0)), exchange(grad_b, along_genes(0))
-    fac_tile = fac_tile + exchange(fac_tile, along_cells(1))
+    for step in (1, 2):
+        fac_tile = fac_tile + exchange(fac_tile, along_cells(step))
     fac_tile, grad_a, grad_b = lax.optimization_barrier((fac_tile, grad_a + came_a, grad_b + came_b))
     came_a, came_b = exchange(grad_a, along_genes(1)), exchange(grad_b, along_genes(1))
     held = bring_for_genes(grad_a, narrow, factors, factor_mean, factor_var, loadings)
-    for step in (2, 3):
-        fac_tile = fac_tile + exchange(fac_tile, along_cells(step))
+    fac_tile = fac_tile + exchange(fac_tile, along_cells(3))
     grad_a, grad_b = grad_a + came_a, grad_b + came_b
     load_tile = grad_a[cell_rows:]
     grad_l, grad_m, f = loading_gradient(fac_tile, grad_a, grad_b, held)

time: 134 us -> 133 us (level)
  waiting for transfers between devices: 42.2 us -> 40.3 us
    ppermute x37, waiting for transfers between devices: 42.2 us -> 40.3 us  [exchange(): return lax.ppermute(value, ('cell', 'gene'), pairs)]
  transfers between devices with their start and end apart: 37 -> 37, of which waited for: 24 -> 26; matrix products, arithmetic and copies ran while one was open for 0% -> 0% of each run, Pallas kernels for 14% -> 15%
where the time goes in v4:
time: 133 us
  starting transfers between devices  49.9 us (38%)
  Pallas kernels  40.6 us (31%)
  waiting for transfers between devices  40.3 us (30%)
    ppermute x37, starting transfers between devices, exchange(): return lax.ppermute(value, ('cell', 'gene'), pairs)  49.9 us
    pallas_call x10, Pallas kernels, call(): pl.pallas_call(functools.partial(kernel, **static), name=name, in_specs=[...  40.6 us
    ppermute x37, waiting for transfers between devices, exchange(): return lax.ppermute(value, ('cell', 'gene'), pairs)  40.3 us
  transfers between devices with their start and end apart: 37, of which 26 were waited for; matrix products, arithmetic and copies ran while one was open for 0% of the time, Pallas kernels for 15%

profile of v4, /device:TPU:1, one launch (start us, length us, event | category | flops | bytes accessed | tf_op | source)
XLA Modules:
  0.0 132.9 jit_solution(2031766325747737425)
XLA Ops:
  0.6 2.9 %front.1 = (f32[8,128]{1,0:T(8,128)S(1)}, f32[8,128]{1,0:T(8,128)S(1)}, f32[1,2048]{1,0:T(1,128)S(1)}, bf16[256,2048]{1,0:T(8,128)(2,1)S(1)}, bf16[128,2048]{1,0...) custom-call(f32[64,2048]{1,0:T(8,128)} %refs_3_.2, f32[64,2048]{1,0:T(8,128)} %refs_3_.3, ...), custom_call_target="tpu_custom_call" | custom-call | bytes 4718592 | tf_op jit(solution)/shard_map/front/pallas_call | solution.py:434
  7.3 9.3 %cell_pass_first.1 = (f32[520,128]{1,0:T(8,128)S(1)}, f32[512,128]{1,0:T(8,128)S(1)}, f8e4m3fn[2048,2048]{1,0:T(32,128)(4,1)}) custom-call(f32[8,128]{1,0:T(8,128)S(1)} %add.126.after_ref, f32[8,128]{1,0:T(8,128)S(1)} %get-tuple-element.58.tile_ref, bf16[256,2048]{1,0:T(8,128)(2,1)S(1)} %get-tuple-element.59.load_cat, ...), custom_call_target="tpu_custom_call" | custom-call | flops 6442450944 | bytes 524288 | tf_op jit(solution)/shard_map/cell_pass_first/pallas_call | solution.py:434
  16.6 3.8 %collective-permute-start.4 = (f32[520,128]{1,0:T(8,128)S(1)}, f32[520,128]{1,0:T(8,128)S(1)}, u32[]{:S(2)}, u32[]{:S(2)}) collective-permute-start(f32[520,128]{1,0:T(8,128)S(1)} %get-tuple-element.65), channel_id=1, source_target_pairs={{0,1},{1,0},{2,3},{3,2},{4,7},{5,6},{6,5},{7,4},{8,9},{9,8},{10,11... | collective-permute-start | bytes 798728 | tf_op jit(solution)/shard_map/ppermute | solution.py:354
  28.7 2.5 %collective-permute-start.6 = (f32[8,128]{1,0:T(8,128)S(1)}, f32[8,128]{1,0:T(8,128)S(1)}, u32[]{:S(2)}, u32[]{:S(2)}) collective-permute-start(f32[8,128]{1,0:T(8,128)S(1)} %add.129), channel_id=1, source_target_pairs={{0,24},{1,25},{2,26},{3,27},{4,100},{5,101},{6,102},{7,103},{8,16}... | collective-permute-start | bytes 12296 | tf_op jit(solution)/shard_map/ppermute | solution.py:354
  31.2 2.9 %load_for_genes.2 = (f8e4m3fn[2048,2048]{1,0:T(32,128)(4,1)S(1)}, f32[64,2048]{1,0:T(8,128)S(1)}, f32[64,2048]{1,0:T(8,128)S(1)}, f32[64,2048]{1,0:T(8,128)S(1)}, bf16[256,2048]{1,0:T(8,128)(2,1)S(1)}) custom-call(f32[520,128]{1,0:T(8,128)S(1)} %add.130.after_ref, f8e4m3fn[2048,2048]{1,0:T(32,128)(4,1)} %get-tuple-element.71.refs_0_, f32[64,2048]{1,0:T(8,128)} %refs_1_.2, ...), custom_call_target="tpu_custom_call" | custom-call | bytes 6815744 | tf_op jit(solution)/shard_map/load_for_genes/pallas_call | solution.py:434
  35.7 5.5 %gene_pass.2 = (f32[2,264,128]{2,1,0:T(8,128)S(1)}, f32[2,256,128]{2,1,0:T(8,128)S(1)}, f32[64,2048]{1,0:T(8,128)}, f32[64,2048]{1,0:T(8,128)}, f32[64,2048]{1,0:T(8,128)}) custom-call(f32[8,128]{1,0:T(8,128)S(1)} %add.132.tile_ref, f32[520,128]{1,0:T(8,128)S(1)} %add.133.ga_ref, f32[512,128]{1,0:T(8,128)S(1)} %add.134.gb_ref, ...), custom_call_target="tpu_custom_call" | custom-call | flops 4294967296 | bytes 524288 | tf_op jit(solution)/shard_map/gene_pass/pallas_call | solution.py:434
  41.2 4.0 %collective-permute-start.15 = (f32[256,128]{1,0:T(8,128)S(1)}, f32[256,128]{1,0:T(8,128)S(1)}, u32[]{:S(2)}, u32[]{:S(2)}) collective-permute-start(f32[256,128]{1,0:T(8,128)S(1)} %dynamic-slice_bitcast_fusion.3), channel_id=1, source_target_pairs={{0,4},{1,5},{2,6},{3,7},{4,0},{5,1},{6,2},{7,3},{8,12},{9,13},{10,... | collective-permute-start | bytes 393224 | tf_op jit(solution)/shard_map/ppermute | solution.py:354
  46.2 2.8 %collective-permute-start.16 = (f32[256,128]{1,0:T(8,128)S(1)}, f32[256,128]{1,0:T(8,128)S(1)}, u32[]{:S(2)}, u32[]{:S(2)}) collective-permute-start(f32[256,128]{1,0:T(8,128)S(1)} %bitcast_add_fusion.3), channel_id=1, source_target_pairs={{0,96},{1,97},{2,98},{3,99},{4,28},{5,29},{6,30},{7,31},{8,104},{9... | collective-permute-start | bytes 393224 | tf_op jit(solution)/shard_map/ppermute | solution.py:354
  49.1 2.5 %collective-permute-done.16 = f32[256,128]{1,0:T(8,128)S(1)} collective-permute-done((f32[256,128]{1,0:T(8,128)S(1)}, f32[256,128]{1,0:T(8,128)S(1)}, u32[]{:S(2)}, u32[]{:S(2)}) %collective-permute-start.16) | collective-permute-done | bytes 131104 | tf_op jit(solution)/shard_map/ppermute | solution.py:354
  58.8 2.0 %collective-permute-done.18 = f32[256,128]{1,0:T(8,128)S(1)} collective-permute-done((f32[256,128]{1,0:T(8,128)S(1)}, f32[256,128]{1,0:T(8,128)S(1)}, u32[]{:S(2)}, u32[]{:S(2)}) %collective-permute-start.18) | collective-permute-done | bytes 131104 | tf_op jit(solution)/shard_map/ppermute | solution.py:354
  65.1 4.2 %collective-permute-start.20 = (f32[256,128]{1,0:T(8,128)S(1)}, f32[256,128]{1,0:T(8,128)S(1)}, u32[]{:S(2)}, u32[]{:S(2)}) collective-permute-start(f32[256,128]{1,0:T(8,128)S(1)} %add.146), channel_id=1, source_target_pairs={{0,4},{1,5},{2,6},{3,7},{4,0},{5,1},{6,2},{7,3},{8,12},{9,13},{10,... | collective-permute-start | bytes 393224 | tf_op jit(solution)/shard_map/ppermute | solution.py:354
  69.3 2.9 %load_for_cells.1 = (f8e4m3fn[2048,2048]{1,0:T(32,128)(4,1)S(1)}, f32[64,2048]{1,0:T(8,128)S(1)}, f32[64,2048]{1,0:T(8,128)S(1)}, f32[64,2048]{1,0:T(8,128)S(1)}, bf16[2048,256]{1,0:T(8,128)(2,1)S(1)}) custom-call(f32[264,128]{1,0:T(8,128)S(1)} %add.140.after_ref, f32[1,2048]{1,0:T(1,128)S(1)} %get-tuple-element.70.off_ref, ...), custom_call_target="tpu_custom_call" | custom-call | bytes 6815744 | tf_op jit(solution)/shard_map/load_for_cells/pallas_call | solution.py:434
  73.9 5.8 %cell_pass.1 = (f32[520,128]{1,0:T(8,128)S(1)}, f32[512,128]{1,0:T(8,128)S(1)}, f32[64,2048]{1,0:T(8,128)}, f32[64,2048]{1,0:T(8,128)}, f32[64,2048]{1,0:T(8,128)}) custom-call(f32[8,128]{1,0:T(8,128)S(1)} %slice.13.tile_ref, f32[2,264,128]{2,1,0:T(8,128)S(1)} %pad_maximum_fusion.la_ref, f32[2,256,128]{2,1,0:T(8,128)S(1)} %pad_maximum_fusion.2.lb_ref, ...), custom_call_target="tpu_custom_call" | custom-call | flops 4294967296 | bytes 524288 | tf_op jit(solution)/shard_map/cell_pass/pallas_call | solution.py:434
  79.7 2.7 %collective-permute-start.21 = (f32[520,128]{1,0:T(8,128)S(1)}, f32[520,128]{1,0:T(8,128)S(1)}, u32[]{:S(2)}, u32[]{:S(2)}) collective-permute-start(f32[520,128]{1,0:T(8,128)S(1)} %get-tuple-element.85), channel_id=1, source_target_pairs={{0,1},{1,0},{2,3},{3,2},{4,7},{5,6},{6,5},{7,4},{8,9},{9,8},{10,11... | collective-permute-start | bytes 798728 | tf_op jit(solution)/shard_map/ppermute | solution.py:354
  82.5 3.8 %collective-permute-done.21 = f32[520,128]{1,0:T(8,128)S(1)} collective-permute-done((f32[520,128]{1,0:T(8,128)S(1)}, f32[520,128]{1,0:T(8,128)S(1)}, u32[]{:S(2)}, u32[]{:S(2)}) %collective-permute-start.21) | collective-permute-done | bytes 266272 | tf_op jit(solution)/shard_map/ppermute | solution.py:354
  86.4 2.7 %collective-permute-done.23 = f32[512,128]{1,0:T(8,128)S(1)} collective-permute-done((f32[512,128]{1,0:T(8,128)S(1)}, f32[512,128]{1,0:T(8,128)S(1)}, u32[]{:S(2)}, u32[]{:S(2)}) %collective-permute-start.23) | collective-permute-done | bytes 262176 | tf_op jit(solution)/shard_map/ppermute | solution.py:354
  89.2 2.9 %load_for_genes.3 = (f8e4m3fn[2048,2048]{1,0:T(32,128)(4,1)S(1)}, f32[64,2048]{1,0:T(8,128)S(1)}, f32[64,2048]{1,0:T(8,128)S(1)}, f32[64,2048]{1,0:T(8,128)S(1)}, bf16[256,2048]{1,0:T(8,128)(2,1)S(1)}) custom-call(f32[520,128]{1,0:T(8,128)S(1)} %add.147.after_ref, f8e4m3fn[2048,2048]{1,0:T(32,128)(4,1)} %get-tuple-element.71.refs_0_, ...), custom_call_target="tpu_custom_call" | custom-call | bytes 6815744 | tf_op jit(solution)/shard_map/load_for_genes/pallas_call | solution.py:434
  92.1 2.6 %collective-permute-done.24 = f32[512,128]{1,0:T(8,128)S(1)} collective-permute-done((f32[512,128]{1,0:T(8,128)S(1)}, f32[512,128]{1,0:T(8,128)S(1)}, u32[]{:S(2)}, u32[]{:S(2)}) %collective-permute-start.24) | collective-permute-done | bytes 262176 | tf_op jit(solution)/shard_map/ppermute | solution.py:354
  94.9 5.5 %gene_pass.3 = (f32[2,264,128]{2,1,0:T(8,128)S(1)}, f32[2,256,128]{2,1,0:T(8,128)S(1)}, f32[64,2048]{1,0:T(8,128)}, f32[64,2048]{1,0:T(8,128)}, f32[64,2048]{1,0:T(8,128)}) custom-call(f32[8,128]{1,0:T(8,128)S(1)} %slice_bitcast_fusion.tile_ref, f32[520,128]{1,0:T(8,128)S(1)} %add.148.ga_ref, f32[512,128]{1,0:T(8,128)S(1)} %add.150.gb_ref, ...), custom_call_target="tpu_custom_call" | custom-call | flops 4294967296 | bytes 524288 | tf_op jit(solution)/shard_map/gene_pass/pallas_call | solution.py:434
  100.4 2.5 %collective-permute-start.31 = (f32[256,128]{1,0:T(8,128)S(1)}, f32[256,128]{1,0:T(8,128)S(1)}, u32[]{:S(2)}, u32[]{:S(2)}) collective-permute-start(f32[256,128]{1,0:T(8,128)S(1)} %dynamic-slice_bitcast_fusion.2), channel_id=1, source_target_pairs={{0,4},{1,5},{2,6},{3,7},{4,0},{5,1},{6,2},{7,3},{8,12},{9,13},{10,... | collective-permute-start | bytes 393224 | tf_op jit(solution)/shard_map/ppermute | solution.py:354
  103.9 2.6 %collective-permute-start.32 = (f32[256,128]{1,0:T(8,128)S(1)}, f32[256,128]{1,0:T(8,128)S(1)}, u32[]{:S(2)}, u32[]{:S(2)}) collective-permute-start(f32[256,128]{1,0:T(8,128)S(1)} %bitcast_add_fusion.2), channel_id=1, source_target_pairs={{0,96},{1,97},{2,98},{3,99},{4,28},{5,29},{6,30},{7,31},{8,104},{9... | collective-permute-start | bytes 393224 | tf_op jit(solution)/shard_map/ppermute | solution.py:354
  106.6 2.6 %collective-permute-done.32 = f32[256,128]{1,0:T(8,128)S(1)} collective-permute-done((f32[256,128]{1,0:T(8,128)S(1)}, f32[256,128]{1,0:T(8,128)S(1)}, u32[]{:S(2)}, u32[]{:S(2)}) %collective-permute-start.32) | collective-permute-done | bytes 131104 | tf_op jit(solution)/shard_map/ppermute | solution.py:354
  116.6 2.1 %collective-permute-done.34 = f32[256,128]{1,0:T(8,128)S(1)} collective-permute-done((f32[256,128]{1,0:T(8,128)S(1)}, f32[256,128]{1,0:T(8,128)S(1)}, u32[]{:S(2)}, u32[]{:S(2)}) %collective-permute-start.34) | collective-permute-done | bytes 131104 | tf_op jit(solution)/shard_map/ppermute | solution.py:354
  123.0 4.1 %collective-permute-start.36 = (f32[256,128]{1,0:T(8,128)S(1)}, f32[256,128]{1,0:T(8,128)S(1)}, u32[]{:S(2)}, u32[]{:S(2)}) collective-permute-start(f32[256,128]{1,0:T(8,128)S(1)} %add.160), channel_id=1, source_target_pairs={{0,4},{1,5},{2,6},{3,7},{4,0},{5,1},{6,2},{7,3},{8,12},{9,13},{10,... | collective-permute-start | bytes 393224 | tf_op jit(solution)/shard_map/ppermute | solution.py:354
  (108 shorter events, 46.5 us)
Async XLA Ops:
  5.9 10.7 %collective-permute-start.1 = (f32[8,128]{1,0:T(8,128)S(1)}, f32[8,128]{1,0:T(8,128)S(1)}, u32[]{:S(2)}, u32[]{:S(2)}) collective-permute-start(f32[8,128]{1,0:T(8,128)S(1)} %add.126.after_ref), channel_id=1, source_target_pairs={{0,32},{1,33},{2,34},{3,35},{4,12},{5,13},{6,14},{7,15},{8,40},{9,... | collective-permute-start | bytes 12296 | tf_op jit(solution)/shard_map/ppermute | solution.py:354
  16.6 10.5 %collective-permute-start.4 = (f32[520,128]{1,0:T(8,128)S(1)}, f32[520,128]{1,0:T(8,128)S(1)}, u32[]{:S(2)}, u32[]{:S(2)}) collective-permute-start(f32[520,128]{1,0:T(8,128)S(1)} %get-tuple-element.65), channel_id=1, source_target_pairs={{0,1},{1,0},{2,3},{3,2},{4,7},{5,6},{6,5},{7,4},{8,9},{9,8},{10,11... | collective-permute-start | bytes 798728 | tf_op jit(solution)/shard_map/ppermute | solution.py:354
  20.4 6.6 %collective-permute-start.5 = (f32[512,128]{1,0:T(8,128)S(1)}, f32[512,128]{1,0:T(8,128)S(1)}, u32[]{:S(2)}, u32[]{:S(2)}) collective-permute-start(f32[512,128]{1,0:T(8,128)S(1)} %get-tuple-element.66), channel_id=1, source_target_pairs={{0,1},{1,0},{2,3},{3,2},{4,7},{5,6},{6,5},{7,4},{8,9},{9,8},{10,11... | collective-permute-start | bytes 786440 | tf_op jit(solution)/shard_map/ppermute | solution.py:354
  27.1 8.5 %collective-permute-start.7 = (f32[520,128]{1,0:T(8,128)S(1)}, f32[520,128]{1,0:T(8,128)S(1)}, u32[]{:S(2)}, u32[]{:S(2)}) collective-permute-start(f32[520,128]{1,0:T(8,128)S(1)} %add.130.after_ref), channel_id=1, source_target_pairs={{0,3},{1,2},{2,1},{3,0},{4,5},{5,4},{6,7},{7,6},{8,11},{9,10},{10,... | collective-permute-start | bytes 798728 | tf_op jit(solution)/shard_map/ppermute | solution.py:354
  27.2 8.4 %collective-permute-start.8 = (f32[512,128]{1,0:T(8,128)S(1)}, f32[512,128]{1,0:T(8,128)S(1)}, u32[]{:S(2)}, u32[]{:S(2)}) collective-permute-start(f32[512,128]{1,0:T(8,128)S(1)} %add.131), channel_id=1, source_target_pairs={{0,3},{1,2},{2,1},{3,0},{4,5},{5,4},{6,7},{7,6},{8,11},{9,10},{10,... | collective-permute-start | bytes 786440 | tf_op jit(solution)/shard_map/ppermute | solution.py:354
  28.7 5.4 %collective-permute-start.6 = (f32[8,128]{1,0:T(8,128)S(1)}, f32[8,128]{1,0:T(8,128)S(1)}, u32[]{:S(2)}, u32[]{:S(2)}) collective-permute-start(f32[8,128]{1,0:T(8,128)S(1)} %add.129), channel_id=1, source_target_pairs={{0,24},{1,25},{2,26},{3,27},{4,100},{5,101},{6,102},{7,103},{8,16}... | collective-permute-start | bytes 12296 | tf_op jit(solution)/shard_map/ppermute | solution.py:354
  41.2 5.0 %collective-permute-start.15 = (f32[256,128]{1,0:T(8,128)S(1)}, f32[256,128]{1,0:T(8,128)S(1)}, u32[]{:S(2)}, u32[]{:S(2)}) collective-permute-start(f32[256,128]{1,0:T(8,128)S(1)} %dynamic-slice_bitcast_fusion.3), channel_id=1, source_target_pairs={{0,4},{1,5},{2,6},{3,7},{4,0},{5,1},{6,2},{7,3},{8,12},{9,13},{10,... | collective-permute-start | bytes 393224 | tf_op jit(solution)/shard_map/ppermute | solution.py:354
  46.2 5.5 %collective-permute-start.16 = (f32[256,128]{1,0:T(8,128)S(1)}, f32[256,128]{1,0:T(8,128)S(1)}, u32[]{:S(2)}, u32[]{:S(2)}) collective-permute-start(f32[256,128]{1,0:T(8,128)S(1)} %bitcast_add_fusion.3), channel_id=1, source_target_pairs={{0,96},{1,97},{2,98},{3,99},{4,28},{5,29},{6,30},{7,31},{8,104},{9... | collective-permute-start | bytes 393224 | tf_op jit(solution)/shard_map/ppermute | solution.py:354
  53.3 5.4 %collective-permute-start.11 = (f32[264,128]{1,0:T(8,128)S(1)}, f32[264,128]{1,0:T(8,128)S(1)}, u32[]{:S(2)}, u32[]{:S(2)}) collective-permute-start(f32[264,128]{1,0:T(8,128)S(1)} %add.138), channel_id=1, source_target_pairs={{0,96},{1,97},{2,98},{3,99},{4,28},{5,29},{6,30},{7,31},{8,104},{9... | collective-permute-start | bytes 405512 | tf_op jit(solution)/shard_map/ppermute | solution.py:354
  55.6 5.3 %collective-permute-start.18 = (f32[256,128]{1,0:T(8,128)S(1)}, f32[256,128]{1,0:T(8,128)S(1)}, u32[]{:S(2)}, u32[]{:S(2)}) collective-permute-start(f32[256,128]{1,0:T(8,128)S(1)} %add.144), channel_id=1, source_target_pairs={{0,24},{1,25},{2,26},{3,27},{4,100},{5,101},{6,102},{7,103},{8,16}... | collective-permute-start | bytes 393224 | tf_op jit(solution)/shard_map/ppermute | solution.py:354
  58.7 4.2 %collective-permute-start.12 = (f32[264,128]{1,0:T(8,128)S(1)}, f32[264,128]{1,0:T(8,128)S(1)}, u32[]{:S(2)}, u32[]{:S(2)}) collective-permute-start(f32[264,128]{1,0:T(8,128)S(1)} %add.139), channel_id=1, source_target_pairs={{0,8},{1,9},{2,10},{3,11},{4,36},{5,37},{6,38},{7,39},{8,0},{9,1},... | collective-permute-start | bytes 405512 | tf_op jit(solution)/shard_map/ppermute | solution.py:354
  63.0 9.2 %collective-permute-start.13 = (f32[264,128]{1,0:T(8,128)S(1)}, f32[264,128]{1,0:T(8,128)S(1)}, u32[]{:S(2)}, u32[]{:S(2)}) collective-permute-start(f32[264,128]{1,0:T(8,128)S(1)} %add.140.after_ref), channel_id=1, source_target_pairs={{0,24},{1,25},{2,26},{3,27},{4,100},{5,101},{6,102},{7,103},{8,16}... | collective-permute-start | bytes 405512 | tf_op jit(solution)/shard_map/ppermute | solution.py:354
  65.1 7.8 %collective-permute-start.20 = (f32[256,128]{1,0:T(8,128)S(1)}, f32[256,128]{1,0:T(8,128)S(1)}, u32[]{:S(2)}, u32[]{:S(2)}) collective-permute-start(f32[256,128]{1,0:T(8,128)S(1)} %add.146), channel_id=1, source_target_pairs={{0,4},{1,5},{2,6},{3,7},{4,0},{5,1},{6,2},{7,3},{8,12},{9,13},{10,... | collective-permute-start | bytes 393224 | tf_op jit(solution)/shard_map/ppermute | solution.py:354
  79.7 6.6 %collective-permute-start.21 = (f32[520,128]{1,0:T(8,128)S(1)}, f32[520,128]{1,0:T(8,128)S(1)}, u32[]{:S(2)}, u32[]{:S(2)}) collective-permute-start(f32[520,128]{1,0:T(8,128)S(1)} %get-tuple-element.85), channel_id=1, source_target_pairs={{0,1},{1,0},{2,3},{3,2},{4,7},{5,6},{6,5},{7,4},{8,9},{9,8},{10,11... | collective-permute-start | bytes 798728 | tf_op jit(solution)/shard_map/ppermute | solution.py:354
  82.4 6.7 %collective-permute-start.23 = (f32[512,128]{1,0:T(8,128)S(1)}, f32[512,128]{1,0:T(8,128)S(1)}, u32[]{:S(2)}, u32[]{:S(2)}) collective-permute-start(f32[512,128]{1,0:T(8,128)S(1)} %get-tuple-element.86), channel_id=1, source_target_pairs={{0,1},{1,0},{2,3},{3,2},{4,7},{5,6},{6,5},{7,4},{8,9},{9,8},{10,11... | collective-permute-start | bytes 786440 | tf_op jit(solution)/shard_map/ppermute | solution.py:354
  86.3 8.5 %collective-permute-start.22 = (f32[520,128]{1,0:T(8,128)S(1)}, f32[520,128]{1,0:T(8,128)S(1)}, u32[]{:S(2)}, u32[]{:S(2)}) collective-permute-start(f32[520,128]{1,0:T(8,128)S(1)} %add.147.after_ref), channel_id=1, source_target_pairs={{0,3},{1,2},{2,1},{3,0},{4,5},{5,4},{6,7},{7,6},{8,11},{9,10},{10,... | collective-permute-start | bytes 798728 | tf_op jit(solution)/shard_map/ppermute | solution.py:354
  89.1 5.6 %collective-permute-start.24 = (f32[512,128]{1,0:T(8,128)S(1)}, f32[512,128]{1,0:T(8,128)S(1)}, u32[]{:S(2)}, u32[]{:S(2)}) collective-permute-start(f32[512,128]{1,0:T(8,128)S(1)} %add.149), channel_id=1, source_target_pairs={{0,3},{1,2},{2,1},{3,0},{4,5},{5,4},{6,7},{7,6},{8,11},{9,10},{10,... | collective-permute-start | bytes 786440 | tf_op jit(solution)/shard_map/ppermute | solution.py:354
  103.9 5.4 %collective-permute-start.32 = (f32[256,128]{1,0:T(8,128)S(1)}, f32[256,128]{1,0:T(8,128)S(1)}, u32[]{:S(2)}, u32[]{:S(2)}) collective-permute-start(f32[256,128]{1,0:T(8,128)S(1)} %bitcast_add_fusion.2), channel_id=1, source_target_pairs={{0,96},{1,97},{2,98},{3,99},{4,28},{5,29},{6,30},{7,31},{8,104},{9... | collective-permute-start | bytes 393224 | tf_op jit(solution)/shard_map/ppermute | solution.py:354
  106.5 4.2 %collective-permute-start.26 = (f32[264,128]{1,0:T(8,128)S(1)}, f32[264,128]{1,0:T(8,128)S(1)}, u32[]{:S(2)}, u32[]{:S(2)}) collective-permute-start(f32[264,128]{1,0:T(8,128)S(1)} %bitcast_add_fusion), channel_id=1, source_target_pairs={{0,32},{1,33},{2,34},{3,35},{4,12},{5,13},{6,14},{7,15},{8,40},{9,... | collective-permute-start | bytes 405512 | tf_op jit(solution)/shard_map/ppermute | solution.py:354
  110.8 5.7 %collective-permute-start.27 = (f32[264,128]{1,0:T(8,128)S(1)}, f32[264,128]{1,0:T(8,128)S(1)}, u32[]{:S(2)}, u32[]{:S(2)}) collective-permute-start(f32[264,128]{1,0:T(8,128)S(1)} %add.152.after_ref), channel_id=1, source_target_pairs={{0,96},{1,97},{2,98},{3,99},{4,28},{5,29},{6,30},{7,31},{8,104},{9... | collective-permute-start | bytes 405512 | tf_op jit(solution)/shard_map/ppermute | solution.py:354
  113.2 5.5 %collective-permute-start.34 = (f32[256,128]{1,0:T(8,128)S(1)}, f32[256,128]{1,0:T(8,128)S(1)}, u32[]{:S(2)}, u32[]{:S(2)}) collective-permute-start(f32[256,128]{1,0:T(8,128)S(1)} %add.158), channel_id=1, source_target_pairs={{0,24},{1,25},{2,26},{3,27},{4,100},{5,101},{6,102},{7,103},{8,16}... | collective-permute-start | bytes 393224 | tf_op jit(solution)/shard_map/ppermute | solution.py:354
  116.5 4.2 %collective-permute-start.28 = (f32[264,128]{1,0:T(8,128)S(1)}, f32[264,128]{1,0:T(8,128)S(1)}, u32[]{:S(2)}, u32[]{:S(2)}) collective-permute-start(f32[264,128]{1,0:T(8,128)S(1)} %add.153), channel_id=1, source_target_pairs={{0,8},{1,9},{2,10},{3,11},{4,36},{5,37},{6,38},{7,39},{8,0},{9,1},... | collective-permute-start | bytes 405512 | tf_op jit(solution)/shard_map/ppermute | solution.py:354
  120.8 7.6 %collective-permute-start.29 = (f32[264,128]{1,0:T(8,128)S(1)}, f32[264,128]{1,0:T(8,128)S(1)}, u32[]{:S(2)}, u32[]{:S(2)}) collective-permute-start(f32[264,128]{1,0:T(8,128)S(1)} %add.154), channel_id=1, source_target_pairs={{0,24},{1,25},{2,26},{3,27},{4,100},{5,101},{6,102},{7,103},{8,16}... | collective-permute-start | bytes 405512 | tf_op jit(solution)/shard_map/ppermute | solution.py:354
  123.0 7.1 %collective-permute-start.36 = (f32[256,128]{1,0:T(8,128)S(1)}, f32[256,128]{1,0:T(8,128)S(1)}, u32[]{:S(2)}, u32[]{:S(2)}) collective-permute-start(f32[256,128]{1,0:T(8,128)S(1)} %add.160), channel_id=1, source_target_pairs={{0,4},{1,5},{2,6},{3,7},{4,0},{5,1},{6,2},{7,3},{8,12},{9,13},{10,... | collective-permute-start | bytes 393224 | tf_op jit(solution)/shard_map/ppermute | solution.py:354
  (13 other events, 44.1 us)

commit v5 on v4

--- a/solution.py
+++ b/solution.py
@@ -272,7 +272,8 @@
         place = front if b == 0 else held.at[pl.ds(b * CELL_BLOCK - begin, CELL_BLOCK)]
         if len(kept) == b:
             stream.need(max(0, (b + 1) * CELL_BLOCK - begin) // COPY_CELLS)
-            narrow[b] = place[...].astype(NARROW)
+            for g in range(0, place.shape[1], CHUNK):
+                narrow[b, :, g : g + CHUNK] = place[:, g : g + CHUNK].astype(NARROW)
             kept.append(
                 pltpu.make_async_copy(narrow.at[b], narrow_hbm.at[pl.ds(b * CELL_BLOCK, CELL_BLOCK)], out_sems.at[b])
             )
@@ -337,12 +338,21 @@
 def last_kernel(
     tile_ref, la_ref, lb_ref, l_ref, lm_ref, lv_ref, nl_hbm, nm_hbm, nv_hbm, moved, sems, *, genes_total
 ):
-    held = l_ref, lm_ref, lv_ref
     width, genes = moved.shape[1:]
-    move(
-        held, loading_rows(la_ref, lb_ref, width, genes), jnp.sum(tile_ref[...]), genes_total * width, rate_loadings, moved
-    )
-    wait_all(start_all(out_copies(moved, (nl_hbm, nm_hbm, nv_hbm), sems)))
+    half = genes // 2
+    total = jnp.sum(tile_ref[...])
+    rows = loading_rows(la_ref, lb_ref, width, genes)
+    copies = []
+    for part in range(2):
+        at = pl.ds(part * half, half)
+        move(
+            [ref.at[:, at] for ref in (l_ref, lm_ref, lv_ref)], lambda c: rows(c + part * half // LANES), total,
+            genes_total * width, rate_loadings, moved.at[:, :, at],
+        )
+        for i, out in enumerate((nl_hbm, nm_hbm, nv_hbm)):
+            copies.append(pltpu.make_async_copy(moved.at[i, :, at], out.at[:, at], sems.at[3 * part + i]))
+        start_all(copies[-3:])
+    wait_all(copies)
 
 
 def exchange(value, partner):
@@ -534,7 +544,7 @@
     grad_l, grad_m, seen = sum_over_cells(grad_l, grad_m)
     held = bring(seen[0], *l)
     l = call(
-        last_kernel, "loading_move", [load_tile, grad_l, grad_m, *held], [], [], three_l, [in_vmem(3, width, genes), dma(3)],
+        last_kernel, "loading_move", [load_tile, grad_l, grad_m, *held], [], [], three_l, [in_vmem(3, width, genes), dma(6)],
         0, genes_total=genes_total,
     )
     return (*f, *l)

time: 133 us -> 133 us (level)
  transfers between devices with their start and end apart: 37 -> 37, of which waited for: 26 -> 26; matrix products, arithmetic and copies ran while one was open for 0% -> 0% of each run, Pallas kernels for 15% -> 14%
where the time goes in v5:
time: 133 us
  starting transfers between devices  49.9 us (38%)
  Pallas kernels  40.4 us (30%)
  waiting for transfers between devices  40.2 us (30%)
    ppermute x37, starting transfers between devices, exchange(): return lax.ppermute(value, ('cell', 'gene'), pairs)  49.9 us
    pallas_call x10, Pallas kernels, call(): pl.pallas_call(functools.partial(kernel, **static), name=name, in_specs=[...  40.4 us
    ppermute x37, waiting for transfers between devices, exchange(): return lax.ppermute(value, ('cell', 'gene'), pairs)  40.2 us
  transfers between devices with their start and end apart: 37, of which 26 were waited for; matrix products, arithmetic and copies ran while one was open for 0% of the time, Pallas kernels for 14%

profile of v5, /device:TPU:1, one launch (start us, length us, event | category | flops | bytes accessed | tf_op | source)
XLA Modules:
  0.0 132.7 jit_solution(8603636943802780048)
XLA Ops:
  0.6 2.9 %front.1 = (f32[8,128]{1,0:T(8,128)S(1)}, f32[8,128]{1,0:T(8,128)S(1)}, f32[1,2048]{1,0:T(1,128)S(1)}, bf16[256,2048]{1,0:T(8,128)(2,1)S(1)}, bf16[128,2048]{1,0...) custom-call(f32[64,2048]{1,0:T(8,128)} %refs_3_.2, f32[64,2048]{1,0:T(8,128)} %refs_3_.3, ...), custom_call_target="tpu_custom_call" | custom-call | bytes 4718592 | tf_op jit(solution)/shard_map/front/pallas_call | solution.py:444
  7.3 9.2 %cell_pass_first.1 = (f32[520,128]{1,0:T(8,128)S(1)}, f32[512,128]{1,0:T(8,128)S(1)}, f8e4m3fn[2048,2048]{1,0:T(32,128)(4,1)}) custom-call(f32[8,128]{1,0:T(8,128)S(1)} %add.126.after_ref, f32[8,128]{1,0:T(8,128)S(1)} %get-tuple-element.58.tile_ref, bf16[256,2048]{1,0:T(8,128)(2,1)S(1)} %get-tuple-element.59.load_cat, ...), custom_call_target="tpu_custom_call" | custom-call | flops 6442450944 | bytes 524288 | tf_op jit(solution)/shard_map/cell_pass_first/pallas_call | solution.py:444
  16.5 3.8 %collective-permute-start.4 = (f32[520,128]{1,0:T(8,128)S(1)}, f32[520,128]{1,0:T(8,128)S(1)}, u32[]{:S(2)}, u32[]{:S(2)}) collective-permute-start(f32[520,128]{1,0:T(8,128)S(1)} %get-tuple-element.65), channel_id=1, source_target_pairs={{0,1},{1,0},{2,3},{3,2},{4,7},{5,6},{6,5},{7,4},{8,9},{9,8},{10,11... | collective-permute-start | bytes 798728 | tf_op jit(solution)/shard_map/ppermute | solution.py:364
  28.6 2.5 %collective-permute-start.6 = (f32[8,128]{1,0:T(8,128)S(1)}, f32[8,128]{1,0:T(8,128)S(1)}, u32[]{:S(2)}, u32[]{:S(2)}) collective-permute-start(f32[8,128]{1,0:T(8,128)S(1)} %add.129), channel_id=1, source_target_pairs={{0,24},{1,25},{2,26},{3,27},{4,100},{5,101},{6,102},{7,103},{8,16}... | collective-permute-start | bytes 12296 | tf_op jit(solution)/shard_map/ppermute | solution.py:364
  31.0 2.9 %load_for_genes.2 = (f8e4m3fn[2048,2048]{1,0:T(32,128)(4,1)S(1)}, f32[64,2048]{1,0:T(8,128)S(1)}, f32[64,2048]{1,0:T(8,128)S(1)}, f32[64,2048]{1,0:T(8,128)S(1)}, bf16[256,2048]{1,0:T(8,128)(2,1)S(1)}) custom-call(f32[520,128]{1,0:T(8,128)S(1)} %add.130.after_ref, f8e4m3fn[2048,2048]{1,0:T(32,128)(4,1)} %get-tuple-element.71.refs_0_, f32[64,2048]{1,0:T(8,128)} %refs_1_.2, ...), custom_call_target="tpu_custom_call" | custom-call | bytes 6815744 | tf_op jit(solution)/shard_map/load_for_genes/pallas_call | solution.py:444
  35.5 5.5 %gene_pass.2 = (f32[2,264,128]{2,1,0:T(8,128)S(1)}, f32[2,256,128]{2,1,0:T(8,128)S(1)}, f32[64,2048]{1,0:T(8,128)}, f32[64,2048]{1,0:T(8,128)}, f32[64,2048]{1,0:T(8,128)}) custom-call(f32[8,128]{1,0:T(8,128)S(1)} %add.132.tile_ref, f32[520,128]{1,0:T(8,128)S(1)} %add.133.ga_ref, f32[512,128]{1,0:T(8,128)S(1)} %add.134.gb_ref, ...), custom_call_target="tpu_custom_call" | custom-call | flops 4294967296 | bytes 524288 | tf_op jit(solution)/shard_map/gene_pass/pallas_call | solution.py:444
  41.1 4.0 %collective-permute-start.15 = (f32[256,128]{1,0:T(8,128)S(1)}, f32[256,128]{1,0:T(8,128)S(1)}, u32[]{:S(2)}, u32[]{:S(2)}) collective-permute-start(f32[256,128]{1,0:T(8,128)S(1)} %dynamic-slice_bitcast_fusion.3), channel_id=1, source_target_pairs={{0,4},{1,5},{2,6},{3,7},{4,0},{5,1},{6,2},{7,3},{8,12},{9,13},{10,... | collective-permute-start | bytes 393224 | tf_op jit(solution)/shard_map/ppermute | solution.py:364
  46.0 2.8 %collective-permute-start.16 = (f32[256,128]{1,0:T(8,128)S(1)}, f32[256,128]{1,0:T(8,128)S(1)}, u32[]{:S(2)}, u32[]{:S(2)}) collective-permute-start(f32[256,128]{1,0:T(8,128)S(1)} %bitcast_add_fusion.3), channel_id=1, source_target_pairs={{0,96},{1,97},{2,98},{3,99},{4,28},{5,29},{6,30},{7,31},{8,104},{9... | collective-permute-start | bytes 393224 | tf_op jit(solution)/shard_map/ppermute | solution.py:364
  48.9 2.5 %collective-permute-done.16 = f32[256,128]{1,0:T(8,128)S(1)} collective-permute-done((f32[256,128]{1,0:T(8,128)S(1)}, f32[256,128]{1,0:T(8,128)S(1)}, u32[]{:S(2)}, u32[]{:S(2)}) %collective-permute-start.16) | collective-permute-done | bytes 131104 | tf_op jit(solution)/shard_map/ppermute | solution.py:364
  58.7 2.0 %collective-permute-done.18 = f32[256,128]{1,0:T(8,128)S(1)} collective-permute-done((f32[256,128]{1,0:T(8,128)S(1)}, f32[256,128]{1,0:T(8,128)S(1)}, u32[]{:S(2)}, u32[]{:S(2)}) %collective-permute-start.18) | collective-permute-done | bytes 131104 | tf_op jit(solution)/shard_map/ppermute | solution.py:364
  64.9 4.2 %collective-permute-start.20 = (f32[256,128]{1,0:T(8,128)S(1)}, f32[256,128]{1,0:T(8,128)S(1)}, u32[]{:S(2)}, u32[]{:S(2)}) collective-permute-start(f32[256,128]{1,0:T(8,128)S(1)} %add.146), channel_id=1, source_target_pairs={{0,4},{1,5},{2,6},{3,7},{4,0},{5,1},{6,2},{7,3},{8,12},{9,13},{10,... | collective-permute-start | bytes 393224 | tf_op jit(solution)/shard_map/ppermute | solution.py:364
  69.2 2.9 %load_for_cells.1 = (f8e4m3fn[2048,2048]{1,0:T(32,128)(4,1)S(1)}, f32[64,2048]{1,0:T(8,128)S(1)}, f32[64,2048]{1,0:T(8,128)S(1)}, f32[64,2048]{1,0:T(8,128)S(1)}, bf16[2048,256]{1,0:T(8,128)(2,1)S(1)}) custom-call(f32[264,128]{1,0:T(8,128)S(1)} %add.140.after_ref, f32[1,2048]{1,0:T(1,128)S(1)} %get-tuple-element.70.off_ref, ...), custom_call_target="tpu_custom_call" | custom-call | bytes 6815744 | tf_op jit(solution)/shard_map/load_for_cells/pallas_call | solution.py:444
  73.8 5.8 %cell_pass.1 = (f32[520,128]{1,0:T(8,128)S(1)}, f32[512,128]{1,0:T(8,128)S(1)}, f32[64,2048]{1,0:T(8,128)}, f32[64,2048]{1,0:T(8,128)}, f32[64,2048]{1,0:T(8,128)}) custom-call(f32[8,128]{1,0:T(8,128)S(1)} %slice.13.tile_ref, f32[2,264,128]{2,1,0:T(8,128)S(1)} %pad_maximum_fusion.la_ref, f32[2,256,128]{2,1,0:T(8,128)S(1)} %pad_maximum_fusion.2.lb_ref, ...), custom_call_target="tpu_custom_call" | custom-call | flops 4294967296 | bytes 524288 | tf_op jit(solution)/shard_map/cell_pass/pallas_call | solution.py:444
  79.6 2.6 %collective-permute-start.21 = (f32[520,128]{1,0:T(8,128)S(1)}, f32[520,128]{1,0:T(8,128)S(1)}, u32[]{:S(2)}, u32[]{:S(2)}) collective-permute-start(f32[520,128]{1,0:T(8,128)S(1)} %get-tuple-element.85), channel_id=1, source_target_pairs={{0,1},{1,0},{2,3},{3,2},{4,7},{5,6},{6,5},{7,4},{8,9},{9,8},{10,11... | collective-permute-start | bytes 798728 | tf_op jit(solution)/shard_map/ppermute | solution.py:364
  82.3 3.8 %collective-permute-done.21 = f32[520,128]{1,0:T(8,128)S(1)} collective-permute-done((f32[520,128]{1,0:T(8,128)S(1)}, f32[520,128]{1,0:T(8,128)S(1)}, u32[]{:S(2)}, u32[]{:S(2)}) %collective-permute-start.21) | collective-permute-done | bytes 266272 | tf_op jit(solution)/shard_map/ppermute | solution.py:364
  86.3 2.7 %collective-permute-done.23 = f32[512,128]{1,0:T(8,128)S(1)} collective-permute-done((f32[512,128]{1,0:T(8,128)S(1)}, f32[512,128]{1,0:T(8,128)S(1)}, u32[]{:S(2)}, u32[]{:S(2)}) %collective-permute-start.23) | collective-permute-done | bytes 262176 | tf_op jit(solution)/shard_map/ppermute | solution.py:364
  89.1 2.9 %load_for_genes.3 = (f8e4m3fn[2048,2048]{1,0:T(32,128)(4,1)S(1)}, f32[64,2048]{1,0:T(8,128)S(1)}, f32[64,2048]{1,0:T(8,128)S(1)}, f32[64,2048]{1,0:T(8,128)S(1)}, bf16[256,2048]{1,0:T(8,128)(2,1)S(1)}) custom-call(f32[520,128]{1,0:T(8,128)S(1)} %add.147.after_ref, f8e4m3fn[2048,2048]{1,0:T(32,128)(4,1)} %get-tuple-element.71.refs_0_, ...), custom_call_target="tpu_custom_call" | custom-call | bytes 6815744 | tf_op jit(solution)/shard_map/load_for_genes/pallas_call | solution.py:444
  92.0 2.6 %collective-permute-done.24 = f32[512,128]{1,0:T(8,128)S(1)} collective-permute-done((f32[512,128]{1,0:T(8,128)S(1)}, f32[512,128]{1,0:T(8,128)S(1)}, u32[]{:S(2)}, u32[]{:S(2)}) %collective-permute-start.24) | collective-permute-done | bytes 262176 | tf_op jit(solution)/shard_map/ppermute | solution.py:364
  94.7 5.5 %gene_pass.3 = (f32[2,264,128]{2,1,0:T(8,128)S(1)}, f32[2,256,128]{2,1,0:T(8,128)S(1)}, f32[64,2048]{1,0:T(8,128)}, f32[64,2048]{1,0:T(8,128)}, f32[64,2048]{1,0:T(8,128)}) custom-call(f32[8,128]{1,0:T(8,128)S(1)} %slice_bitcast_fusion.tile_ref, f32[520,128]{1,0:T(8,128)S(1)} %add.148.ga_ref, f32[512,128]{1,0:T(8,128)S(1)} %add.150.gb_ref, ...), custom_call_target="tpu_custom_call" | custom-call | flops 4294967296 | bytes 524288 | tf_op jit(solution)/shard_map/gene_pass/pallas_call | solution.py:444
  100.2 2.5 %collective-permute-start.31 = (f32[256,128]{1,0:T(8,128)S(1)}, f32[256,128]{1,0:T(8,128)S(1)}, u32[]{:S(2)}, u32[]{:S(2)}) collective-permute-start(f32[256,128]{1,0:T(8,128)S(1)} %dynamic-slice_bitcast_fusion.2), channel_id=1, source_target_pairs={{0,4},{1,5},{2,6},{3,7},{4,0},{5,1},{6,2},{7,3},{8,12},{9,13},{10,... | collective-permute-start | bytes 393224 | tf_op jit(solution)/shard_map/ppermute | solution.py:364
  103.7 2.7 %collective-permute-start.32 = (f32[256,128]{1,0:T(8,128)S(1)}, f32[256,128]{1,0:T(8,128)S(1)}, u32[]{:S(2)}, u32[]{:S(2)}) collective-permute-start(f32[256,128]{1,0:T(8,128)S(1)} %bitcast_add_fusion.2), channel_id=1, source_target_pairs={{0,96},{1,97},{2,98},{3,99},{4,28},{5,29},{6,30},{7,31},{8,104},{9... | collective-permute-start | bytes 393224 | tf_op jit(solution)/shard_map/ppermute | solution.py:364
  106.5 2.6 %collective-permute-done.32 = f32[256,128]{1,0:T(8,128)S(1)} collective-permute-done((f32[256,128]{1,0:T(8,128)S(1)}, f32[256,128]{1,0:T(8,128)S(1)}, u32[]{:S(2)}, u32[]{:S(2)}) %collective-permute-start.32) | collective-permute-done | bytes 131104 | tf_op jit(solution)/shard_map/ppermute | solution.py:364
  116.5 2.1 %collective-permute-done.34 = f32[256,128]{1,0:T(8,128)S(1)} collective-permute-done((f32[256,128]{1,0:T(8,128)S(1)}, f32[256,128]{1,0:T(8,128)S(1)}, u32[]{:S(2)}, u32[]{:S(2)}) %collective-permute-start.34) | collective-permute-done | bytes 131104 | tf_op jit(solution)/shard_map/ppermute | solution.py:364
  122.8 4.1 %collective-permute-start.36 = (f32[256,128]{1,0:T(8,128)S(1)}, f32[256,128]{1,0:T(8,128)S(1)}, u32[]{:S(2)}, u32[]{:S(2)}) collective-permute-start(f32[256,128]{1,0:T(8,128)S(1)} %add.160), channel_id=1, source_target_pairs={{0,4},{1,5},{2,6},{3,7},{4,0},{5,1},{6,2},{7,3},{8,12},{9,13},{10,... | collective-permute-start | bytes 393224 | tf_op jit(solution)/shard_map/ppermute | solution.py:364
  (108 shorter events, 46.4 us)
Async XLA Ops:
  5.9 10.6 %collective-permute-start.1 = (f32[8,128]{1,0:T(8,128)S(1)}, f32[8,128]{1,0:T(8,128)S(1)}, u32[]{:S(2)}, u32[]{:S(2)}) collective-permute-start(f32[8,128]{1,0:T(8,128)S(1)} %add.126.after_ref), channel_id=1, source_target_pairs={{0,32},{1,33},{2,34},{3,35},{4,12},{5,13},{6,14},{7,15},{8,40},{9,... | collective-permute-start | bytes 12296 | tf_op jit(solution)/shard_map/ppermute | solution.py:364
  16.5 10.5 %collective-permute-start.4 = (f32[520,128]{1,0:T(8,128)S(1)}, f32[520,128]{1,0:T(8,128)S(1)}, u32[]{:S(2)}, u32[]{:S(2)}) collective-permute-start(f32[520,128]{1,0:T(8,128)S(1)} %get-tuple-element.65), channel_id=1, source_target_pairs={{0,1},{1,0},{2,3},{3,2},{4,7},{5,6},{6,5},{7,4},{8,9},{9,8},{10,11... | collective-permute-start | bytes 798728 | tf_op jit(solution)/shard_map/ppermute | solution.py:364
  20.3 6.6 %collective-permute-start.5 = (f32[512,128]{1,0:T(8,128)S(1)}, f32[512,128]{1,0:T(8,128)S(1)}, u32[]{:S(2)}, u32[]{:S(2)}) collective-permute-start(f32[512,128]{1,0:T(8,128)S(1)} %get-tuple-element.66), channel_id=1, source_target_pairs={{0,1},{1,0},{2,3},{3,2},{4,7},{5,6},{6,5},{7,4},{8,9},{9,8},{10,11... | collective-permute-start | bytes 786440 | tf_op jit(solution)/shard_map/ppermute | solution.py:364
  27.0 8.5 %collective-permute-start.7 = (f32[520,128]{1,0:T(8,128)S(1)}, f32[520,128]{1,0:T(8,128)S(1)}, u32[]{:S(2)}, u32[]{:S(2)}) collective-permute-start(f32[520,128]{1,0:T(8,128)S(1)} %add.130.after_ref), channel_id=1, source_target_pairs={{0,3},{1,2},{2,1},{3,0},{4,5},{5,4},{6,7},{7,6},{8,11},{9,10},{10,... | collective-permute-start | bytes 798728 | tf_op jit(solution)/shard_map/ppermute | solution.py:364
  27.1 8.4 %collective-permute-start.8 = (f32[512,128]{1,0:T(8,128)S(1)}, f32[512,128]{1,0:T(8,128)S(1)}, u32[]{:S(2)}, u32[]{:S(2)}) collective-permute-start(f32[512,128]{1,0:T(8,128)S(1)} %add.131), channel_id=1, source_target_pairs={{0,3},{1,2},{2,1},{3,0},{4,5},{5,4},{6,7},{7,6},{8,11},{9,10},{10,... | collective-permute-start | bytes 786440 | tf_op jit(solution)/shard_map/ppermute | solution.py:364
  28.6 5.4 %collective-permute-start.6 = (f32[8,128]{1,0:T(8,128)S(1)}, f32[8,128]{1,0:T(8,128)S(1)}, u32[]{:S(2)}, u32[]{:S(2)}) collective-permute-start(f32[8,128]{1,0:T(8,128)S(1)} %add.129), channel_id=1, source_target_pairs={{0,24},{1,25},{2,26},{3,27},{4,100},{5,101},{6,102},{7,103},{8,16}... | collective-permute-start | bytes 12296 | tf_op jit(solution)/shard_map/ppermute | solution.py:364
  41.1 4.9 %collective-permute-start.15 = (f32[256,128]{1,0:T(8,128)S(1)}, f32[256,128]{1,0:T(8,128)S(1)}, u32[]{:S(2)}, u32[]{:S(2)}) collective-permute-start(f32[256,128]{1,0:T(8,128)S(1)} %dynamic-slice_bitcast_fusion.3), channel_id=1, source_target_pairs={{0,4},{1,5},{2,6},{3,7},{4,0},{5,1},{6,2},{7,3},{8,12},{9,13},{10,... | collective-permute-start | bytes 393224 | tf_op jit(solution)/shard_map/ppermute | solution.py:364
  46.0 5.5 %collective-permute-start.16 = (f32[256,128]{1,0:T(8,128)S(1)}, f32[256,128]{1,0:T(8,128)S(1)}, u32[]{:S(2)}, u32[]{:S(2)}) collective-permute-start(f32[256,128]{1,0:T(8,128)S(1)} %bitcast_add_fusion.3), channel_id=1, source_target_pairs={{0,96},{1,97},{2,98},{3,99},{4,28},{5,29},{6,30},{7,31},{8,104},{9... | collective-permute-start | bytes 393224 | tf_op jit(solution)/shard_map/ppermute | solution.py:364
  48.9 4.2 %collective-permute-start.10 = (f32[264,128]{1,0:T(8,128)S(1)}, f32[264,128]{1,0:T(8,128)S(1)}, u32[]{:S(2)}, u32[]{:S(2)}) collective-permute-start(f32[264,128]{1,0:T(8,128)S(1)} %bitcast_add_fusion.1), channel_id=1, source_target_pairs={{0,32},{1,33},{2,34},{3,35},{4,12},{5,13},{6,14},{7,15},{8,40},{9,... | collective-permute-start | bytes 405512 | tf_op jit(solution)/shard_map/ppermute | solution.py:364
  53.1 5.4 %collective-permute-start.11 = (f32[264,128]{1,0:T(8,128)S(1)}, f32[264,128]{1,0:T(8,128)S(1)}, u32[]{:S(2)}, u32[]{:S(2)}) collective-permute-start(f32[264,128]{1,0:T(8,128)S(1)} %add.138), channel_id=1, source_target_pairs={{0,96},{1,97},{2,98},{3,99},{4,28},{5,29},{6,30},{7,31},{8,104},{9... | collective-permute-start | bytes 405512 | tf_op jit(solution)/shard_map/ppermute | solution.py:364
  55.4 5.3 %collective-permute-start.18 = (f32[256,128]{1,0:T(8,128)S(1)}, f32[256,128]{1,0:T(8,128)S(1)}, u32[]{:S(2)}, u32[]{:S(2)}) collective-permute-start(f32[256,128]{1,0:T(8,128)S(1)} %add.144), channel_id=1, source_target_pairs={{0,24},{1,25},{2,26},{3,27},{4,100},{5,101},{6,102},{7,103},{8,16}... | collective-permute-start | bytes 393224 | tf_op jit(solution)/shard_map/ppermute | solution.py:364
  58.6 4.2 %collective-permute-start.12 = (f32[264,128]{1,0:T(8,128)S(1)}, f32[264,128]{1,0:T(8,128)S(1)}, u32[]{:S(2)}, u32[]{:S(2)}) collective-permute-start(f32[264,128]{1,0:T(8,128)S(1)} %add.139), channel_id=1, source_target_pairs={{0,8},{1,9},{2,10},{3,11},{4,36},{5,37},{6,38},{7,39},{8,0},{9,1},... | collective-permute-start | bytes 405512 | tf_op jit(solution)/shard_map/ppermute | solution.py:364
  62.8 9.2 %collective-permute-start.13 = (f32[264,128]{1,0:T(8,128)S(1)}, f32[264,128]{1,0:T(8,128)S(1)}, u32[]{:S(2)}, u32[]{:S(2)}) collective-permute-start(f32[264,128]{1,0:T(8,128)S(1)} %add.140.after_ref), channel_id=1, source_target_pairs={{0,24},{1,25},{2,26},{3,27},{4,100},{5,101},{6,102},{7,103},{8,16}... | collective-permute-start | bytes 405512 | tf_op jit(solution)/shard_map/ppermute | solution.py:364
  64.9 7.7 %collective-permute-start.20 = (f32[256,128]{1,0:T(8,128)S(1)}, f32[256,128]{1,0:T(8,128)S(1)}, u32[]{:S(2)}, u32[]{:S(2)}) collective-permute-start(f32[256,128]{1,0:T(8,128)S(1)} %add.146), channel_id=1, source_target_pairs={{0,4},{1,5},{2,6},{3,7},{4,0},{5,1},{6,2},{7,3},{8,12},{9,13},{10,... | collective-permute-start | bytes 393224 | tf_op jit(solution)/shard_map/ppermute | solution.py:364
  79.6 6.6 %collective-permute-start.21 = (f32[520,128]{1,0:T(8,128)S(1)}, f32[520,128]{1,0:T(8,128)S(1)}, u32[]{:S(2)}, u32[]{:S(2)}) collective-permute-start(f32[520,128]{1,0:T(8,128)S(1)} %get-tuple-element.85), channel_id=1, source_target_pairs={{0,1},{1,0},{2,3},{3,2},{4,7},{5,6},{6,5},{7,4},{8,9},{9,8},{10,11... | collective-permute-start | bytes 798728 | tf_op jit(solution)/shard_map/ppermute | solution.py:364
  82.2 6.7 %collective-permute-start.23 = (f32[512,128]{1,0:T(8,128)S(1)}, f32[512,128]{1,0:T(8,128)S(1)}, u32[]{:S(2)}, u32[]{:S(2)}) collective-permute-start(f32[512,128]{1,0:T(8,128)S(1)} %get-tuple-element.86), channel_id=1, source_target_pairs={{0,1},{1,0},{2,3},{3,2},{4,7},{5,6},{6,5},{7,4},{8,9},{9,8},{10,11... | collective-permute-start | bytes 786440 | tf_op jit(solution)/shard_map/ppermute | solution.py:364
  86.2 8.5 %collective-permute-start.22 = (f32[520,128]{1,0:T(8,128)S(1)}, f32[520,128]{1,0:T(8,128)S(1)}, u32[]{:S(2)}, u32[]{:S(2)}) collective-permute-start(f32[520,128]{1,0:T(8,128)S(1)} %add.147.after_ref), channel_id=1, source_target_pairs={{0,3},{1,2},{2,1},{3,0},{4,5},{5,4},{6,7},{7,6},{8,11},{9,10},{10,... | collective-permute-start | bytes 798728 | tf_op jit(solution)/shard_map/ppermute | solution.py:364
  89.0 5.6 %collective-permute-start.24 = (f32[512,128]{1,0:T(8,128)S(1)}, f32[512,128]{1,0:T(8,128)S(1)}, u32[]{:S(2)}, u32[]{:S(2)}) collective-permute-start(f32[512,128]{1,0:T(8,128)S(1)} %add.149), channel_id=1, source_target_pairs={{0,3},{1,2},{2,1},{3,0},{4,5},{5,4},{6,7},{7,6},{8,11},{9,10},{10,... | collective-permute-start | bytes 786440 | tf_op jit(solution)/shard_map/ppermute | solution.py:364
  103.7 5.4 %collective-permute-start.32 = (f32[256,128]{1,0:T(8,128)S(1)}, f32[256,128]{1,0:T(8,128)S(1)}, u32[]{:S(2)}, u32[]{:S(2)}) collective-permute-start(f32[256,128]{1,0:T(8,128)S(1)} %bitcast_add_fusion.2), channel_id=1, source_target_pairs={{0,96},{1,97},{2,98},{3,99},{4,28},{5,29},{6,30},{7,31},{8,104},{9... | collective-permute-start | bytes 393224 | tf_op jit(solution)/shard_map/ppermute | solution.py:364
  106.4 4.2 %collective-permute-start.26 = (f32[264,128]{1,0:T(8,128)S(1)}, f32[264,128]{1,0:T(8,128)S(1)}, u32[]{:S(2)}, u32[]{:S(2)}) collective-permute-start(f32[264,128]{1,0:T(8,128)S(1)} %bitcast_add_fusion), channel_id=1, source_target_pairs={{0,32},{1,33},{2,34},{3,35},{4,12},{5,13},{6,14},{7,15},{8,40},{9,... | collective-permute-start | bytes 405512 | tf_op jit(solution)/shard_map/ppermute | solution.py:364
  110.7 5.7 %collective-permute-start.27 = (f32[264,128]{1,0:T(8,128)S(1)}, f32[264,128]{1,0:T(8,128)S(1)}, u32[]{:S(2)}, u32[]{:S(2)}) collective-permute-start(f32[264,128]{1,0:T(8,128)S(1)} %add.152.after_ref), channel_id=1, source_target_pairs={{0,96},{1,97},{2,98},{3,99},{4,28},{5,29},{6,30},{7,31},{8,104},{9... | collective-permute-start | bytes 405512 | tf_op jit(solution)/shard_map/ppermute | solution.py:364
  113.1 5.5 %collective-permute-start.34 = (f32[256,128]{1,0:T(8,128)S(1)}, f32[256,128]{1,0:T(8,128)S(1)}, u32[]{:S(2)}, u32[]{:S(2)}) collective-permute-start(f32[256,128]{1,0:T(8,128)S(1)} %add.158), channel_id=1, source_target_pairs={{0,24},{1,25},{2,26},{3,27},{4,100},{5,101},{6,102},{7,103},{8,16}... | collective-permute-start | bytes 393224 | tf_op jit(solution)/shard_map/ppermute | solution.py:364
  120.6 7.6 %collective-permute-start.29 = (f32[264,128]{1,0:T(8,128)S(1)}, f32[264,128]{1,0:T(8,128)S(1)}, u32[]{:S(2)}, u32[]{:S(2)}) collective-permute-start(f32[264,128]{1,0:T(8,128)S(1)} %add.154), channel_id=1, source_target_pairs={{0,24},{1,25},{2,26},{3,27},{4,100},{5,101},{6,102},{7,103},{8,16}... | collective-permute-start | bytes 405512 | tf_op jit(solution)/shard_map/ppermute | solution.py:364
  122.8 7.1 %collective-permute-start.36 = (f32[256,128]{1,0:T(8,128)S(1)}, f32[256,128]{1,0:T(8,128)S(1)}, u32[]{:S(2)}, u32[]{:S(2)}) collective-permute-start(f32[256,128]{1,0:T(8,128)S(1)} %add.160), channel_id=1, source_target_pairs={{0,4},{1,5},{2,6},{3,7},{4,0},{5,1},{6,2},{7,3},{8,12},{9,13},{10,... | collective-permute-start | bytes 393224 | tf_op jit(solution)/shard_map/ppermute | solution.py:364
  (13 other events, 44.1 us)

commit v6 on v5

--- a/solution.py
+++ b/solution.py
@@ -21,7 +21,7 @@
 f32 = jnp.float32
 bf16 = jnp.bfloat16
 CELL_BLOCK = 512
-GENE_BLOCK = 256
+GENE_BLOCK = 512
 COPY_CELLS = 256
 PARTS = 2
 CHUNK = 512
@@ -149,10 +149,12 @@
         at = slice(b * GENE_BLOCK, (b + 1) * GENE_BLOCK)
         load = load_cat[:, at]
         total = None
+        lin = jnp.dot(cell_cat[:CHUNK, :], load, preferred_element_type=f32)
         for c in range(0, cell_cat.shape[0], CHUNK):
             of = slice(c, c + CHUNK)
-            lin = jnp.dot(cell_cat[of, :], load, preferred_element_type=f32)
             resid = (jnp.exp2(lin) - counts[of, at].astype(f32)).astype(bf16)
+            if c + CHUNK < cell_cat.shape[0]:
+                lin = jnp.dot(cell_cat[c + CHUNK : c + 2 * CHUNK, :], load, preferred_element_type=f32)
             part = jnp.dot(cell_hl[:, of], resid, preferred_element_type=f32)
             total = part if total is None else total + part
         grad = (total[:width] + total[width:]) * (1.0 / math.sqrt(cells_total))

time: 133 us -> 133 us (level)
  no operation moved by 1% of the time
where the time goes in v6:
time: 133 us
  starting transfers between devices  49.9 us (38%)
  Pallas kernels  40.8 us (31%)
  waiting for transfers between devices  40.2 us (30%)
    ppermute x37, starting transfers between devices, exchange(): return lax.ppermute(value, ('cell', 'gene'), pairs)  49.9 us
    pallas_call x10, Pallas kernels, call(): pl.pallas_call(functools.partial(kernel, **static), name=name, in_specs=[...  40.8 us
    ppermute x37, waiting for transfers between devices, exchange(): return lax.ppermute(value, ('cell', 'gene'), pairs)  40.2 us
  transfers between devices with their start and end apart: 37, of which 26 were waited for; matrix products, arithmetic and copies ran while one was open for 0% of the time, Pallas kernels for 14%

profile of v6, /device:TPU:1, one launch (start us, length us, event | category | flops | bytes accessed | tf_op | source)
XLA Modules:
  0.0 133.1 jit_solution(15356166072101699319)
XLA Ops:
  0.6 2.9 %front.1 = (f32[8,128]{1,0:T(8,128)S(1)}, f32[8,128]{1,0:T(8,128)S(1)}, f32[1,2048]{1,0:T(1,128)S(1)}, bf16[256,2048]{1,0:T(8,128)(2,1)S(1)}, bf16[128,2048]{1,0...) custom-call(f32[64,2048]{1,0:T(8,128)} %refs_3_.2, f32[64,2048]{1,0:T(8,128)} %refs_3_.3, ...), custom_call_target="tpu_custom_call" | custom-call | bytes 4718592 | tf_op jit(solution)/shard_map/front/pallas_call | solution.py:446
  7.3 9.2 %cell_pass_first.1 = (f32[520,128]{1,0:T(8,128)S(1)}, f32[512,128]{1,0:T(8,128)S(1)}, f8e4m3fn[2048,2048]{1,0:T(32,128)(4,1)}) custom-call(f32[8,128]{1,0:T(8,128)S(1)} %add.126.after_ref, f32[8,128]{1,0:T(8,128)S(1)} %get-tuple-element.58.tile_ref, bf16[256,2048]{1,0:T(8,128)(2,1)S(1)} %get-tuple-element.59.load_cat, ...), custom_call_target="tpu_custom_call" | custom-call | flops 6442450944 | bytes 524288 | tf_op jit(solution)/shard_map/cell_pass_first/pallas_call | solution.py:446
  16.5 3.8 %collective-permute-start.4 = (f32[520,128]{1,0:T(8,128)S(1)}, f32[520,128]{1,0:T(8,128)S(1)}, u32[]{:S(2)}, u32[]{:S(2)}) collective-permute-start(f32[520,128]{1,0:T(8,128)S(1)} %get-tuple-element.65), channel_id=1, source_target_pairs={{0,1},{1,0},{2,3},{3,2},{4,7},{5,6},{6,5},{7,4},{8,9},{9,8},{10,11... | collective-permute-start | bytes 798728 | tf_op jit(solution)/shard_map/ppermute | solution.py:366
  28.6 2.5 %collective-permute-start.6 = (f32[8,128]{1,0:T(8,128)S(1)}, f32[8,128]{1,0:T(8,128)S(1)}, u32[]{:S(2)}, u32[]{:S(2)}) collective-permute-start(f32[8,128]{1,0:T(8,128)S(1)} %add.129), channel_id=1, source_target_pairs={{0,24},{1,25},{2,26},{3,27},{4,100},{5,101},{6,102},{7,103},{8,16}... | collective-permute-start | bytes 12296 | tf_op jit(solution)/shard_map/ppermute | solution.py:366
  31.0 2.9 %load_for_genes.2 = (f8e4m3fn[2048,2048]{1,0:T(32,128)(4,1)S(1)}, f32[64,2048]{1,0:T(8,128)S(1)}, f32[64,2048]{1,0:T(8,128)S(1)}, f32[64,2048]{1,0:T(8,128)S(1)}, bf16[256,2048]{1,0:T(8,128)(2,1)S(1)}) custom-call(f32[520,128]{1,0:T(8,128)S(1)} %add.130.after_ref, f8e4m3fn[2048,2048]{1,0:T(32,128)(4,1)} %get-tuple-element.71.refs_0_, f32[64,2048]{1,0:T(8,128)} %refs_1_.2, ...), custom_call_target="tpu_custom_call" | custom-call | bytes 6815744 | tf_op jit(solution)/shard_map/load_for_genes/pallas_call | solution.py:446
  35.5 5.7 %gene_pass.2 = (f32[2,264,128]{2,1,0:T(8,128)S(1)}, f32[2,256,128]{2,1,0:T(8,128)S(1)}, f32[64,2048]{1,0:T(8,128)}, f32[64,2048]{1,0:T(8,128)}, f32[64,2048]{1,0:T(8,128)}) custom-call(f32[8,128]{1,0:T(8,128)S(1)} %add.132.tile_ref, f32[520,128]{1,0:T(8,128)S(1)} %add.133.ga_ref, f32[512,128]{1,0:T(8,128)S(1)} %add.134.gb_ref, ...), custom_call_target="tpu_custom_call" | custom-call | flops 4294967296 | bytes 524288 | tf_op jit(solution)/shard_map/gene_pass/pallas_call | solution.py:446
  41.3 4.0 %collective-permute-start.15 = (f32[256,128]{1,0:T(8,128)S(1)}, f32[256,128]{1,0:T(8,128)S(1)}, u32[]{:S(2)}, u32[]{:S(2)}) collective-permute-start(f32[256,128]{1,0:T(8,128)S(1)} %dynamic-slice_bitcast_fusion.3), channel_id=1, source_target_pairs={{0,4},{1,5},{2,6},{3,7},{4,0},{5,1},{6,2},{7,3},{8,12},{9,13},{10,... | collective-permute-start | bytes 393224 | tf_op jit(solution)/shard_map/ppermute | solution.py:366
  46.2 2.8 %collective-permute-start.16 = (f32[256,128]{1,0:T(8,128)S(1)}, f32[256,128]{1,0:T(8,128)S(1)}, u32[]{:S(2)}, u32[]{:S(2)}) collective-permute-start(f32[256,128]{1,0:T(8,128)S(1)} %bitcast_add_fusion.3), channel_id=1, source_target_pairs={{0,96},{1,97},{2,98},{3,99},{4,28},{5,29},{6,30},{7,31},{8,104},{9... | collective-permute-start | bytes 393224 | tf_op jit(solution)/shard_map/ppermute | solution.py:366
  49.2 2.5 %collective-permute-done.16 = f32[256,128]{1,0:T(8,128)S(1)} collective-permute-done((f32[256,128]{1,0:T(8,128)S(1)}, f32[256,128]{1,0:T(8,128)S(1)}, u32[]{:S(2)}, u32[]{:S(2)}) %collective-permute-start.16) | collective-permute-done | bytes 131104 | tf_op jit(solution)/shard_map/ppermute | solution.py:366
  58.9 2.0 %collective-permute-done.18 = f32[256,128]{1,0:T(8,128)S(1)} collective-permute-done((f32[256,128]{1,0:T(8,128)S(1)}, f32[256,128]{1,0:T(8,128)S(1)}, u32[]{:S(2)}, u32[]{:S(2)}) %collective-permute-start.18) | collective-permute-done | bytes 131104 | tf_op jit(solution)/shard_map/ppermute | solution.py:366
  65.2 4.2 %collective-permute-start.20 = (f32[256,128]{1,0:T(8,128)S(1)}, f32[256,128]{1,0:T(8,128)S(1)}, u32[]{:S(2)}, u32[]{:S(2)}) collective-permute-start(f32[256,128]{1,0:T(8,128)S(1)} %add.146), channel_id=1, source_target_pairs={{0,4},{1,5},{2,6},{3,7},{4,0},{5,1},{6,2},{7,3},{8,12},{9,13},{10,... | collective-permute-start | bytes 393224 | tf_op jit(solution)/shard_map/ppermute | solution.py:366
  69.4 2.9 %load_for_cells.1 = (f8e4m3fn[2048,2048]{1,0:T(32,128)(4,1)S(1)}, f32[64,2048]{1,0:T(8,128)S(1)}, f32[64,2048]{1,0:T(8,128)S(1)}, f32[64,2048]{1,0:T(8,128)S(1)}, bf16[2048,256]{1,0:T(8,128)(2,1)S(1)}) custom-call(f32[264,128]{1,0:T(8,128)S(1)} %add.140.after_ref, f32[1,2048]{1,0:T(1,128)S(1)} %get-tuple-element.70.off_ref, ...), custom_call_target="tpu_custom_call" | custom-call | bytes 6815744 | tf_op jit(solution)/shard_map/load_for_cells/pallas_call | solution.py:446
  74.0 5.8 %cell_pass.1 = (f32[520,128]{1,0:T(8,128)S(1)}, f32[512,128]{1,0:T(8,128)S(1)}, f32[64,2048]{1,0:T(8,128)}, f32[64,2048]{1,0:T(8,128)}, f32[64,2048]{1,0:T(8,128)}) custom-call(f32[8,128]{1,0:T(8,128)S(1)} %slice.13.tile_ref, f32[2,264,128]{2,1,0:T(8,128)S(1)} %pad_maximum_fusion.la_ref, f32[2,256,128]{2,1,0:T(8,128)S(1)} %pad_maximum_fusion.2.lb_ref, ...), custom_call_target="tpu_custom_call" | custom-call | flops 4294967296 | bytes 524288 | tf_op jit(solution)/shard_map/cell_pass/pallas_call | solution.py:446
  79.8 2.6 %collective-permute-start.21 = (f32[520,128]{1,0:T(8,128)S(1)}, f32[520,128]{1,0:T(8,128)S(1)}, u32[]{:S(2)}, u32[]{:S(2)}) collective-permute-start(f32[520,128]{1,0:T(8,128)S(1)} %get-tuple-element.85), channel_id=1, source_target_pairs={{0,1},{1,0},{2,3},{3,2},{4,7},{5,6},{6,5},{7,4},{8,9},{9,8},{10,11... | collective-permute-start | bytes 798728 | tf_op jit(solution)/shard_map/ppermute | solution.py:366
  82.6 3.8 %collective-permute-done.21 = f32[520,128]{1,0:T(8,128)S(1)} collective-permute-done((f32[520,128]{1,0:T(8,128)S(1)}, f32[520,128]{1,0:T(8,128)S(1)}, u32[]{:S(2)}, u32[]{:S(2)}) %collective-permute-start.21) | collective-permute-done | bytes 266272 | tf_op jit(solution)/shard_map/ppermute | solution.py:366
  86.5 2.7 %collective-permute-done.23 = f32[512,128]{1,0:T(8,128)S(1)} collective-permute-done((f32[512,128]{1,0:T(8,128)S(1)}, f32[512,128]{1,0:T(8,128)S(1)}, u32[]{:S(2)}, u32[]{:S(2)}) %collective-permute-start.23) | collective-permute-done | bytes 262176 | tf_op jit(solution)/shard_map/ppermute | solution.py:366
  89.3 2.9 %load_for_genes.3 = (f8e4m3fn[2048,2048]{1,0:T(32,128)(4,1)S(1)}, f32[64,2048]{1,0:T(8,128)S(1)}, f32[64,2048]{1,0:T(8,128)S(1)}, f32[64,2048]{1,0:T(8,128)S(1)}, bf16[256,2048]{1,0:T(8,128)(2,1)S(1)}) custom-call(f32[520,128]{1,0:T(8,128)S(1)} %add.147.after_ref, f8e4m3fn[2048,2048]{1,0:T(32,128)(4,1)} %get-tuple-element.71.refs_0_, ...), custom_call_target="tpu_custom_call" | custom-call | bytes 6815744 | tf_op jit(solution)/shard_map/load_for_genes/pallas_call | solution.py:446
  92.2 2.6 %collective-permute-done.24 = f32[512,128]{1,0:T(8,128)S(1)} collective-permute-done((f32[512,128]{1,0:T(8,128)S(1)}, f32[512,128]{1,0:T(8,128)S(1)}, u32[]{:S(2)}, u32[]{:S(2)}) %collective-permute-start.24) | collective-permute-done | bytes 262176 | tf_op jit(solution)/shard_map/ppermute | solution.py:366
  94.9 5.7 %gene_pass.3 = (f32[2,264,128]{2,1,0:T(8,128)S(1)}, f32[2,256,128]{2,1,0:T(8,128)S(1)}, f32[64,2048]{1,0:T(8,128)}, f32[64,2048]{1,0:T(8,128)}, f32[64,2048]{1,0:T(8,128)}) custom-call(f32[8,128]{1,0:T(8,128)S(1)} %slice_bitcast_fusion.tile_ref, f32[520,128]{1,0:T(8,128)S(1)} %add.148.ga_ref, f32[512,128]{1,0:T(8,128)S(1)} %add.150.gb_ref, ...), custom_call_target="tpu_custom_call" | custom-call | flops 4294967296 | bytes 524288 | tf_op jit(solution)/shard_map/gene_pass/pallas_call | solution.py:446
  100.7 2.5 %collective-permute-start.31 = (f32[256,128]{1,0:T(8,128)S(1)}, f32[256,128]{1,0:T(8,128)S(1)}, u32[]{:S(2)}, u32[]{:S(2)}) collective-permute-start(f32[256,128]{1,0:T(8,128)S(1)} %dynamic-slice_bitcast_fusion.2), channel_id=1, source_target_pairs={{0,4},{1,5},{2,6},{3,7},{4,0},{5,1},{6,2},{7,3},{8,12},{9,13},{10,... | collective-permute-start | bytes 393224 | tf_op jit(solution)/shard_map/ppermute | solution.py:366
  104.2 2.7 %collective-permute-start.32 = (f32[256,128]{1,0:T(8,128)S(1)}, f32[256,128]{1,0:T(8,128)S(1)}, u32[]{:S(2)}, u32[]{:S(2)}) collective-permute-start(f32[256,128]{1,0:T(8,128)S(1)} %bitcast_add_fusion.2), channel_id=1, source_target_pairs={{0,96},{1,97},{2,98},{3,99},{4,28},{5,29},{6,30},{7,31},{8,104},{9... | collective-permute-start | bytes 393224 | tf_op jit(solution)/shard_map/ppermute | solution.py:366
  106.9 2.6 %collective-permute-done.32 = f32[256,128]{1,0:T(8,128)S(1)} collective-permute-done((f32[256,128]{1,0:T(8,128)S(1)}, f32[256,128]{1,0:T(8,128)S(1)}, u32[]{:S(2)}, u32[]{:S(2)}) %collective-permute-start.32) | collective-permute-done | bytes 131104 | tf_op jit(solution)/shard_map/ppermute | solution.py:366
  116.9 2.1 %collective-permute-done.34 = f32[256,128]{1,0:T(8,128)S(1)} collective-permute-done((f32[256,128]{1,0:T(8,128)S(1)}, f32[256,128]{1,0:T(8,128)S(1)}, u32[]{:S(2)}, u32[]{:S(2)}) %collective-permute-start.34) | collective-permute-done | bytes 131104 | tf_op jit(solution)/shard_map/ppermute | solution.py:366
  123.3 4.0 %collective-permute-start.36 = (f32[256,128]{1,0:T(8,128)S(1)}, f32[256,128]{1,0:T(8,128)S(1)}, u32[]{:S(2)}, u32[]{:S(2)}) collective-permute-start(f32[256,128]{1,0:T(8,128)S(1)} %add.160), channel_id=1, source_target_pairs={{0,4},{1,5},{2,6},{3,7},{4,0},{5,1},{6,2},{7,3},{8,12},{9,13},{10,... | collective-permute-start | bytes 393224 | tf_op jit(solution)/shard_map/ppermute | solution.py:366
  (108 shorter events, 46.4 us)
Async XLA Ops:
  5.9 10.6 %collective-permute-start.1 = (f32[8,128]{1,0:T(8,128)S(1)}, f32[8,128]{1,0:T(8,128)S(1)}, u32[]{:S(2)}, u32[]{:S(2)}) collective-permute-start(f32[8,128]{1,0:T(8,128)S(1)} %add.126.after_ref), channel_id=1, source_target_pairs={{0,32},{1,33},{2,34},{3,35},{4,12},{5,13},{6,14},{7,15},{8,40},{9,... | collective-permute-start | bytes 12296 | tf_op jit(solution)/shard_map/ppermute | solution.py:366
  16.5 10.5 %collective-permute-start.4 = (f32[520,128]{1,0:T(8,128)S(1)}, f32[520,128]{1,0:T(8,128)S(1)}, u32[]{:S(2)}, u32[]{:S(2)}) collective-permute-start(f32[520,128]{1,0:T(8,128)S(1)} %get-tuple-element.65), channel_id=1, source_target_pairs={{0,1},{1,0},{2,3},{3,2},{4,7},{5,6},{6,5},{7,4},{8,9},{9,8},{10,11... | collective-permute-start | bytes 798728 | tf_op jit(solution)/shard_map/ppermute | solution.py:366
  20.3 6.6 %collective-permute-start.5 = (f32[512,128]{1,0:T(8,128)S(1)}, f32[512,128]{1,0:T(8,128)S(1)}, u32[]{:S(2)}, u32[]{:S(2)}) collective-permute-start(f32[512,128]{1,0:T(8,128)S(1)} %get-tuple-element.66), channel_id=1, source_target_pairs={{0,1},{1,0},{2,3},{3,2},{4,7},{5,6},{6,5},{7,4},{8,9},{9,8},{10,11... | collective-permute-start | bytes 786440 | tf_op jit(solution)/shard_map/ppermute | solution.py:366
  27.0 8.5 %collective-permute-start.7 = (f32[520,128]{1,0:T(8,128)S(1)}, f32[520,128]{1,0:T(8,128)S(1)}, u32[]{:S(2)}, u32[]{:S(2)}) collective-permute-start(f32[520,128]{1,0:T(8,128)S(1)} %add.130.after_ref), channel_id=1, source_target_pairs={{0,3},{1,2},{2,1},{3,0},{4,5},{5,4},{6,7},{7,6},{8,11},{9,10},{10,... | collective-permute-start | bytes 798728 | tf_op jit(solution)/shard_map/ppermute | solution.py:366
  27.1 8.4 %collective-permute-start.8 = (f32[512,128]{1,0:T(8,128)S(1)}, f32[512,128]{1,0:T(8,128)S(1)}, u32[]{:S(2)}, u32[]{:S(2)}) collective-permute-start(f32[512,128]{1,0:T(8,128)S(1)} %add.131), channel_id=1, source_target_pairs={{0,3},{1,2},{2,1},{3,0},{4,5},{5,4},{6,7},{7,6},{8,11},{9,10},{10,... | collective-permute-start | bytes 786440 | tf_op jit(solution)/shard_map/ppermute | solution.py:366
  28.6 5.4 %collective-permute-start.6 = (f32[8,128]{1,0:T(8,128)S(1)}, f32[8,128]{1,0:T(8,128)S(1)}, u32[]{:S(2)}, u32[]{:S(2)}) collective-permute-start(f32[8,128]{1,0:T(8,128)S(1)} %add.129), channel_id=1, source_target_pairs={{0,24},{1,25},{2,26},{3,27},{4,100},{5,101},{6,102},{7,103},{8,16}... | collective-permute-start | bytes 12296 | tf_op jit(solution)/shard_map/ppermute | solution.py:366
  41.3 4.9 %collective-permute-start.15 = (f32[256,128]{1,0:T(8,128)S(1)}, f32[256,128]{1,0:T(8,128)S(1)}, u32[]{:S(2)}, u32[]{:S(2)}) collective-permute-start(f32[256,128]{1,0:T(8,128)S(1)} %dynamic-slice_bitcast_fusion.3), channel_id=1, source_target_pairs={{0,4},{1,5},{2,6},{3,7},{4,0},{5,1},{6,2},{7,3},{8,12},{9,13},{10,... | collective-permute-start | bytes 393224 | tf_op jit(solution)/shard_map/ppermute | solution.py:366
  46.2 5.5 %collective-permute-start.16 = (f32[256,128]{1,0:T(8,128)S(1)}, f32[256,128]{1,0:T(8,128)S(1)}, u32[]{:S(2)}, u32[]{:S(2)}) collective-permute-start(f32[256,128]{1,0:T(8,128)S(1)} %bitcast_add_fusion.3), channel_id=1, source_target_pairs={{0,96},{1,97},{2,98},{3,99},{4,28},{5,29},{6,30},{7,31},{8,104},{9... | collective-permute-start | bytes 393224 | tf_op jit(solution)/shard_map/ppermute | solution.py:366
  49.1 4.2 %collective-permute-start.10 = (f32[264,128]{1,0:T(8,128)S(1)}, f32[264,128]{1,0:T(8,128)S(1)}, u32[]{:S(2)}, u32[]{:S(2)}) collective-permute-start(f32[264,128]{1,0:T(8,128)S(1)} %bitcast_add_fusion.1), channel_id=1, source_target_pairs={{0,32},{1,33},{2,34},{3,35},{4,12},{5,13},{6,14},{7,15},{8,40},{9,... | collective-permute-start | bytes 405512 | tf_op jit(solution)/shard_map/ppermute | solution.py:366
  53.3 5.4 %collective-permute-start.11 = (f32[264,128]{1,0:T(8,128)S(1)}, f32[264,128]{1,0:T(8,128)S(1)}, u32[]{:S(2)}, u32[]{:S(2)}) collective-permute-start(f32[264,128]{1,0:T(8,128)S(1)} %add.138), channel_id=1, source_target_pairs={{0,96},{1,97},{2,98},{3,99},{4,28},{5,29},{6,30},{7,31},{8,104},{9... | collective-permute-start | bytes 405512 | tf_op jit(solution)/shard_map/ppermute | solution.py:366
  55.6 5.3 %collective-permute-start.18 = (f32[256,128]{1,0:T(8,128)S(1)}, f32[256,128]{1,0:T(8,128)S(1)}, u32[]{:S(2)}, u32[]{:S(2)}) collective-permute-start(f32[256,128]{1,0:T(8,128)S(1)} %add.144), channel_id=1, source_target_pairs={{0,24},{1,25},{2,26},{3,27},{4,100},{5,101},{6,102},{7,103},{8,16}... | collective-permute-start | bytes 393224 | tf_op jit(solution)/shard_map/ppermute | solution.py:366
  58.8 4.2 %collective-permute-start.12 = (f32[264,128]{1,0:T(8,128)S(1)}, f32[264,128]{1,0:T(8,128)S(1)}, u32[]{:S(2)}, u32[]{:S(2)}) collective-permute-start(f32[264,128]{1,0:T(8,128)S(1)} %add.139), channel_id=1, source_target_pairs={{0,8},{1,9},{2,10},{3,11},{4,36},{5,37},{6,38},{7,39},{8,0},{9,1},... | collective-permute-start | bytes 405512 | tf_op jit(solution)/shard_map/ppermute | solution.py:366
  63.0 9.2 %collective-permute-start.13 = (f32[264,128]{1,0:T(8,128)S(1)}, f32[264,128]{1,0:T(8,128)S(1)}, u32[]{:S(2)}, u32[]{:S(2)}) collective-permute-start(f32[264,128]{1,0:T(8,128)S(1)} %add.140.after_ref), channel_id=1, source_target_pairs={{0,24},{1,25},{2,26},{3,27},{4,100},{5,101},{6,102},{7,103},{8,16}... | collective-permute-start | bytes 405512 | tf_op jit(solution)/shard_map/ppermute | solution.py:366
  65.2 7.7 %collective-permute-start.20 = (f32[256,128]{1,0:T(8,128)S(1)}, f32[256,128]{1,0:T(8,128)S(1)}, u32[]{:S(2)}, u32[]{:S(2)}) collective-permute-start(f32[256,128]{1,0:T(8,128)S(1)} %add.146), channel_id=1, source_target_pairs={{0,4},{1,5},{2,6},{3,7},{4,0},{5,1},{6,2},{7,3},{8,12},{9,13},{10,... | collective-permute-start | bytes 393224 | tf_op jit(solution)/shard_map/ppermute | solution.py:366
  79.8 6.6 %collective-permute-start.21 = (f32[520,128]{1,0:T(8,128)S(1)}, f32[520,128]{1,0:T(8,128)S(1)}, u32[]{:S(2)}, u32[]{:S(2)}) collective-permute-start(f32[520,128]{1,0:T(8,128)S(1)} %get-tuple-element.85), channel_id=1, source_target_pairs={{0,1},{1,0},{2,3},{3,2},{4,7},{5,6},{6,5},{7,4},{8,9},{9,8},{10,11... | collective-permute-start | bytes 798728 | tf_op jit(solution)/shard_map/ppermute | solution.py:366
  82.4 6.7 %collective-permute-start.23 = (f32[512,128]{1,0:T(8,128)S(1)}, f32[512,128]{1,0:T(8,128)S(1)}, u32[]{:S(2)}, u32[]{:S(2)}) collective-permute-start(f32[512,128]{1,0:T(8,128)S(1)} %get-tuple-element.86), channel_id=1, source_target_pairs={{0,1},{1,0},{2,3},{3,2},{4,7},{5,6},{6,5},{7,4},{8,9},{9,8},{10,11... | collective-permute-start | bytes 786440 | tf_op jit(solution)/shard_map/ppermute | solution.py:366
  86.4 8.5 %collective-permute-start.22 = (f32[520,128]{1,0:T(8,128)S(1)}, f32[520,128]{1,0:T(8,128)S(1)}, u32[]{:S(2)}, u32[]{:S(2)}) collective-permute-start(f32[520,128]{1,0:T(8,128)S(1)} %add.147.after_ref), channel_id=1, source_target_pairs={{0,3},{1,2},{2,1},{3,0},{4,5},{5,4},{6,7},{7,6},{8,11},{9,10},{10,... | collective-permute-start | bytes 798728 | tf_op jit(solution)/shard_map/ppermute | solution.py:366
  89.2 5.6 %collective-permute-start.24 = (f32[512,128]{1,0:T(8,128)S(1)}, f32[512,128]{1,0:T(8,128)S(1)}, u32[]{:S(2)}, u32[]{:S(2)}) collective-permute-start(f32[512,128]{1,0:T(8,128)S(1)} %add.149), channel_id=1, source_target_pairs={{0,3},{1,2},{2,1},{3,0},{4,5},{5,4},{6,7},{7,6},{8,11},{9,10},{10,... | collective-permute-start | bytes 786440 | tf_op jit(solution)/shard_map/ppermute | solution.py:366
  104.2 5.4 %collective-permute-start.32 = (f32[256,128]{1,0:T(8,128)S(1)}, f32[256,128]{1,0:T(8,128)S(1)}, u32[]{:S(2)}, u32[]{:S(2)}) collective-permute-start(f32[256,128]{1,0:T(8,128)S(1)} %bitcast_add_fusion.2), channel_id=1, source_target_pairs={{0,96},{1,97},{2,98},{3,99},{4,28},{5,29},{6,30},{7,31},{8,104},{9... | collective-permute-start | bytes 393224 | tf_op jit(solution)/shard_map/ppermute | solution.py:366
  111.1 5.7 %collective-permute-start.27 = (f32[264,128]{1,0:T(8,128)S(1)}, f32[264,128]{1,0:T(8,128)S(1)}, u32[]{:S(2)}, u32[]{:S(2)}) collective-permute-start(f32[264,128]{1,0:T(8,128)S(1)} %add.152.after_ref), channel_id=1, source_target_pairs={{0,96},{1,97},{2,98},{3,99},{4,28},{5,29},{6,30},{7,31},{8,104},{9... | collective-permute-start | bytes 405512 | tf_op jit(solution)/shard_map/ppermute | solution.py:366
  113.5 5.5 %collective-permute-start.34 = (f32[256,128]{1,0:T(8,128)S(1)}, f32[256,128]{1,0:T(8,128)S(1)}, u32[]{:S(2)}, u32[]{:S(2)}) collective-permute-start(f32[256,128]{1,0:T(8,128)S(1)} %add.158), channel_id=1, source_target_pairs={{0,24},{1,25},{2,26},{3,27},{4,100},{5,101},{6,102},{7,103},{8,16}... | collective-permute-start | bytes 393224 | tf_op jit(solution)/shard_map/ppermute | solution.py:366
  116.8 4.2 %collective-permute-start.28 = (f32[264,128]{1,0:T(8,128)S(1)}, f32[264,128]{1,0:T(8,128)S(1)}, u32[]{:S(2)}, u32[]{:S(2)}) collective-permute-start(f32[264,128]{1,0:T(8,128)S(1)} %add.153), channel_id=1, source_target_pairs={{0,8},{1,9},{2,10},{3,11},{4,36},{5,37},{6,38},{7,39},{8,0},{9,1},... | collective-permute-start | bytes 405512 | tf_op jit(solution)/shard_map/ppermute | solution.py:366
  121.1 7.6 %collective-permute-start.29 = (f32[264,128]{1,0:T(8,128)S(1)}, f32[264,128]{1,0:T(8,128)S(1)}, u32[]{:S(2)}, u32[]{:S(2)}) collective-permute-start(f32[264,128]{1,0:T(8,128)S(1)} %add.154), channel_id=1, source_target_pairs={{0,24},{1,25},{2,26},{3,27},{4,100},{5,101},{6,102},{7,103},{8,16}... | collective-permute-start | bytes 405512 | tf_op jit(solution)/shard_map/ppermute | solution.py:366
  123.3 7.1 %collective-permute-start.36 = (f32[256,128]{1,0:T(8,128)S(1)}, f32[256,128]{1,0:T(8,128)S(1)}, u32[]{:S(2)}, u32[]{:S(2)}) collective-permute-start(f32[256,128]{1,0:T(8,128)S(1)} %add.160), channel_id=1, source_target_pairs={{0,4},{1,5},{2,6},{3,7},{4,0},{5,1},{6,2},{7,3},{8,12},{9,13},{10,... | collective-permute-start | bytes 393224 | tf_op jit(solution)/shard_map/ppermute | solution.py:366
  (13 other events, 44.1 us)
